TPU v7x, 32 devices: a whole 2x2x4 slice. The times are simulated.
32 devices in a mesh: visit: 4 (over y, x), patch: 8 (over z, core).
Axes of the slice: x: 2, y: 2, z: 4, core: 2. Of those that a mesh axis runs over, the one named last changes fastest.
Arguments:
- image: float32 [4, 8, 32, 128, 128], P('visit', 'patch'), may hold values from -6 to 6
- variance: float32 [4, 8, 32, 128, 128], P('visit', 'patch'), may hold values from 4 to 64
- dest_patch: int32 [4, 8, 32], P('visit', 'patch'), may hold values from 0 to 7, as said below
- quadrant: int32 [4, 8, 32], P('visit', 'patch'), may hold values from 0 to 3
- coef_index: int32 [4, 8, 32], P('visit', 'patch'), may hold values from 0 to 799
- block_count: int32 [4, 8], P('visit', 'patch'), may hold values from 24 to 32, as said below
- coef_table: float32 [800, 16, 6], replicated, may hold values from -0.625 to 0.625
- row_taps: float32 [16, 41], replicated, may hold values from -1 to 1
- col_taps: float32 [16, 41], replicated, may hold values from -1 to 1
Outputs:
- weighted_sum: float32 [8, 256, 256], P('patch', 'visit')
- weight_sum: float32 [8, 256, 256], P('patch', 'visit')
Inputs may be any that keep to these rules, and one draw needn't show every extreme that they name: `dest_patch`: among the blocks of one device at most 8 name the same patch slice; one patch slice, drawn from the seed, is named by exactly 8 live blocks of every device. `block_count`: some device has all 32 blocks live.
All inputs are finite; a program needn't handle non-finite values.
Results may differ from a plain program's by a relative error of at most 0.0003.
Values sent between devices are 32-bit elements; how exact they have to be, the bound alone decides.
No kernel may reach another device: no remote copies, remote signals or barrier semaphores. Data moves between devices by JAX's collectives and lax.ppermute only.
A program may use at most 192 MiB of HBM per device.

v0:
```python
import jax
import jax.numpy as jnp
from jax import lax
from jax.sharding import PartitionSpec as P

highest = lax.Precision.HIGHEST


def band_matrices(filter_taps, block_side, reversed_band):
    radius = (filter_taps.shape[1] - 1) // 2
    row_index = jnp.arange(block_side)[:, None]
    col_index = jnp.arange(block_side)[None, :]
    offset = row_index - col_index if reversed_band else col_index - row_index
    banded = jnp.zeros((filter_taps.shape[0], block_side, block_side), jnp.float32)
    for tap_index in range(filter_taps.shape[1]):
        picked = (offset == tap_index - radius).astype(jnp.float32)
        banded = banded + filter_taps[:, tap_index, None, None] * picked[None, :, :]
    return banded


def match_blocks(pixels, coefficients, down_quarter, across_quarter, row_band, col_band):
    block_side = pixels.shape[-1]
    pixel_index = jnp.arange(block_side).astype(jnp.float32)
    across_pos = (
        across_quarter[:, None] * block_side + pixel_index[None, :] + 0.5
    ) / block_side - 1.0
    down_pos = (down_quarter[:, None] * block_side + pixel_index[None, :] + 0.5) / block_side - 1.0
    across_pos = across_pos[:, None, :]
    down_pos = down_pos[:, :, None]
    matched = jnp.zeros(pixels.shape, jnp.float32)
    for basis_index in range(row_band.shape[0]):
        spread = jnp.einsum(
            "nij,jk->nik",
            pixels,
            row_band[basis_index],
            precision=highest,
            preferred_element_type=jnp.float32,
        )
        convolved = jnp.einsum(
            "ij,njk->nik",
            col_band[basis_index],
            spread,
            precision=highest,
            preferred_element_type=jnp.float32,
        )
        poly_terms = coefficients[:, basis_index, :]
        weight = (
            poly_terms[:, 0, None, None]
            + poly_terms[:, 1, None, None] * across_pos
            + poly_terms[:, 2, None, None] * down_pos
            + poly_terms[:, 3, None, None] * across_pos * across_pos
            + poly_terms[:, 4, None, None] * across_pos * down_pos
            + poly_terms[:, 5, None, None] * down_pos * down_pos
        )
        matched = matched + weight * convolved
    return matched


def on_device(
    image, variance, dest_patch, quadrant, coef_index, block_count, coef_table, row_taps, col_taps
):
    pixels = image[0, 0]
    variances = variance[0, 0]
    targets = dest_patch[0, 0]
    quadrants = quadrant[0, 0]
    table_rows = coef_index[0, 0]
    live_count = block_count[0, 0]
    blocks = pixels.shape[0]
    block_side = pixels.shape[-1]
    owners = lax.axis_size("patch")
    capacity = max(2, (2 * blocks + owners - 1) // owners)
    slot_total = owners * capacity
    position = jnp.arange(blocks)
    is_live = position < live_count
    earlier_same = (
        (targets[:, None] == targets[None, :])
        & is_live[None, :]
        & (position[None, :] < position[:, None])
    )
    slot_rank = jnp.sum(earlier_same.astype(jnp.int32), axis=1)
    slot_of = jnp.where(is_live, targets * capacity + slot_rank, -1)
    slot_match = slot_of[None, :] == jnp.arange(slot_total)[:, None]
    occupied = jnp.any(slot_match, axis=1)
    source = jnp.sum(slot_match.astype(jnp.int32) * position[None, :], axis=1)
    presence = occupied.astype(jnp.float32)
    quarter_hot = (quadrants[:, None] == jnp.arange(4)[None, :]).astype(jnp.float32)
    slot_quarter = (jnp.take(quarter_hot, source, axis=0) * presence[:, None]).reshape(
        owners, capacity, 4
    )
    row_band = band_matrices(row_taps, block_side, False)
    col_band = band_matrices(col_taps, block_side, True)
    grid_shape = (owners, capacity, block_side, block_side)
    slot_pixels = (jnp.take(pixels, source, axis=0) * presence[:, None, None]).reshape(grid_shape)
    slot_variance = jnp.where(
        occupied[:, None, None], jnp.take(variances, source, axis=0), 1.0
    ).reshape(grid_shape)
    slot_coefficients = (
        jnp.take(coef_table, jnp.take(table_rows, source), axis=0) * presence[:, None, None]
    ).reshape((owners, capacity) + coef_table.shape[1:])
    got_pixels = lax.all_to_all(slot_pixels, "patch", split_axis=0, concat_axis=0, tiled=True)
    got_variance = lax.all_to_all(slot_variance, "patch", split_axis=0, concat_axis=0, tiled=True)
    got_coefficients = lax.all_to_all(
        slot_coefficients, "patch", split_axis=0, concat_axis=0, tiled=True
    )
    got_quarter = lax.all_to_all(slot_quarter, "patch", split_axis=0, concat_axis=0, tiled=True)
    senders = got_pixels.shape[0]
    items = got_pixels.shape[1]
    flat_quarter = got_quarter.reshape(senders * items, 4)
    matched = match_blocks(
        got_pixels.reshape(senders * items, block_side, block_side),
        got_coefficients.reshape((senders * items,) + got_coefficients.shape[2:]),
        flat_quarter[:, 2] + flat_quarter[:, 3],
        flat_quarter[:, 1] + flat_quarter[:, 3],
        row_band,
        col_band,
    )
    inverse = jnp.sum(flat_quarter, axis=1)[:, None, None] / got_variance.reshape(
        senders * items, block_side, block_side
    )
    weighted_slots, inverse_slots, got_quarter = (
        (inverse * matched).reshape(got_pixels.shape),
        inverse.reshape(got_pixels.shape),
        got_quarter,
    )
    quarter_grid = got_quarter.reshape(-1, 2, 2)
    weighted_patch = jnp.einsum(
        "nab,nij->aibj",
        quarter_grid,
        weighted_slots.reshape(-1, block_side, block_side),
        precision=highest,
        preferred_element_type=jnp.float32,
    ).reshape(2 * block_side, 2 * block_side)
    weight_patch = jnp.einsum(
        "nab,nij->aibj",
        quarter_grid,
        inverse_slots.reshape(-1, block_side, block_side),
        precision=highest,
        preferred_element_type=jnp.float32,
    ).reshape(2 * block_side, 2 * block_side)
    weighted_sum, weight_sum = (
        lax.psum_scatter(weighted_patch, "visit", scatter_dimension=0, tiled=True),
        lax.psum_scatter(weight_patch, "visit", scatter_dimension=0, tiled=True),
    )
    return (weighted_sum[None], weight_sum[None])


def solution(mesh):
    placed = (
        P("visit", "patch", None, None, None),
        P("visit", "patch", None, None, None),
        P("visit", "patch", None),
        P("visit", "patch", None),
        P("visit", "patch", None),
        P("visit", "patch"),
        P(),
        P(),
        P(),
    )
    return jax.shard_map(
        on_device,
        mesh=mesh,
        in_specs=placed,
        out_specs=(P("patch", "visit", None), P("patch", "visit", None)),
        check_vma=False,
    )
```

profile of v0, /device:TPU:0, one launch (start us, length us, event | category | flops | bytes accessed | tf_op | source)
XLA Modules:
  0.0 507.2 jit_solution(8851371769839467525)
XLA Ops:
  8.0 0.9 convert_reduce_fusion
  10.0 1.4 gather_fusion.1
  13.5 6.3 %all-to-all-start = ((f32[8,8,4]{1,2,0:T(4,128)}), f32[8,8,4]{1,2,0:T(4,128)S(1)}, u32[]{:S(2)}, u32[]{:S(2)}) async-start(f32[8,8,4]{1,2,0:T(4,128)} %select_multiply_fusion.1), calls=%async_computation | async-start | bytes 32768 | tf_op jit(solution)/shard_map/all_to_all | solution.py:105
  22.6 2.5 slice_reduce_fusion.97
  25.0 2.5 slice_reduce_fusion.96
  34.3 1.1 slice_reduce_fusion.56
  35.3 1.1 slice_reduce_fusion.55
  36.4 1.2 fusion.253
  37.6 2.8 gather_fusion.3
  40.4 4.4 gather_fusion.4
  44.8 2.4 copy.199
  47.2 2.5 gather_fusion.2
  49.9 5.9 %select_select_fusion = (f32[64,128,128]{2,1,0:T(8,128)}, f32[64,128,128]{2,1,0:T(8,128)}) fusion(f32[64,128,128]{2,1,0:T(8,128)} %gather_fusion.3, pred[64]{0:T(512)(128)(4,1)S(1)} %copy-done.80, pred[64]{0:T(512)(128)(4,1)S(1)} %fusion.250, f32[64]{0:T(128)S(1)} %convert_element_type.695, f32[64,128,128]{2,1,0:T(8,128)} %gather_fusion.4), kind=kLoop, calls=%fused_computation.42 | loop fusion | flops 4194304 | bytes 16777600 | tf_op jit(solution)/shard_map/jit(_where)/select_n | solution.py:94
  57.3 5.1 %all-to-all-start.2 = ((f32[8,1,768]{2,1,0:T(1,128)}), f32[8,1,768]{2,1,0:T(1,128)S(1)}, u32[]{:S(2)}, u32[]{:S(2)}) async-start(f32[8,1,768]{2,1,0:T(1,128)} %reshape.5189), calls=%async_computation.2 | async-start | bytes 49152 | tf_op jit(solution)/shard_map/all_to_all | solution.py:102
  63.2 4.9 all-to-all-done.2
  68.7 4.8 all-to-all-start.3
  74.2 5.5 %copy.198 = f32[8,8,128,128]{2,3,1,0:T(8,128)} copy(f32[8,8,128,128]{3,2,1,0:T(8,128)} %bitcast.553) | data formatting | bytes 8388608 | tf_op jit(solution)/shard_map/reshape | solution.py:96
  80.5 4.3 multiply_add_fusion.1
  85.1 3.8 multiply_add_fusion
  90.3 1.4 reduce.197
  91.9 1.7 slice_reduce_fusion.15
  95.0 1.0 multiply_multiply_fusion.31
  96.8 1.7 fusion.233
  98.5 69.1 %all-to-all-done.3 = f32[8,8,128,128]{3,2,1,0:T(8,128)} async-done(((f32[8,8,128,128]{3,2,1,0:T(8,128)}), f32[8,8,128,128]{3,2,1,0:T(8,128)}, u32[]{:S(2)}, u32[]{:S(2)}) %all-to-all-start.3) | async-done | bytes 4194336 | tf_op jit(solution)/shard_map/all_to_all | solution.py:100
  167.6 4.6 all-to-all-start.1
  172.7 8.0 %fusion.25 = f32[64,128,128]{1,2,0:T(8,128)} fusion(f32[64,128,128]{2,1,0:T(8,128)} %bitcast.24, f32[16,128,128]{2,1,0:T(8,128)S(1)} %multiply_add_fusion.1), kind=kOutput, calls=%fused_computation.75 | convolution fusion | flops 1610612736 | bytes 8454144 | tf_op jit(solution)/shard_map/nij,jk->nik/dot_general | solution.py:32
  180.8 8.0 %fusion.27 = f32[64,128,128]{1,2,0:T(8,128)} fusion(f32[64,128,128]{2,1,0:T(8,128)} %bitcast.24, f32[16,128,128]{2,1,0:T(8,128)S(1)} %multiply_add_fusion.1), kind=kOutput, calls=%fused_computation.79 | convolution fusion | flops 1610612736 | bytes 8454144 | tf_op jit(solution)/shard_map/nij,jk->nik/dot_general | solution.py:32
  188.8 8.1 %fusion.29 = f32[64,128,128]{1,2,0:T(8,128)} fusion(f32[64,128,128]{2,1,0:T(8,128)} %bitcast.24, f32[16,128,128]{2,1,0:T(8,128)S(1)} %multiply_add_fusion.1), kind=kOutput, calls=%fused_computation.83 | convolution fusion | flops 1610612736 | bytes 8454144 | tf_op jit(solution)/shard_map/nij,jk->nik/dot_general | solution.py:32
  196.8 8.2 %fusion.31 = f32[64,128,128]{1,2,0:T(8,128)} fusion(f32[64,128,128]{2,1,0:T(8,128)} %bitcast.24, f32[16,128,128]{2,1,0:T(8,128)S(1)} %multiply_add_fusion.1), kind=kOutput, calls=%fused_computation.87 | convolution fusion | flops 1610612736 | bytes 8454144 | tf_op jit(solution)/shard_map/nij,jk->nik/dot_general | solution.py:32
  205.1 8.0 %fusion.33 = f32[64,128,128]{1,2,0:T(8,128)} fusion(f32[64,128,128]{2,1,0:T(8,128)} %bitcast.24, f32[16,128,128]{2,1,0:T(8,128)S(1)} %multiply_add_fusion.1), kind=kOutput, calls=%fused_computation.91 | convolution fusion | flops 1610612736 | bytes 8454144 | tf_op jit(solution)/shard_map/nij,jk->nik/dot_general | solution.py:32
  213.1 8.1 %fusion.35 = f32[64,128,128]{1,2,0:T(8,128)} fusion(f32[64,128,128]{2,1,0:T(8,128)} %bitcast.24, f32[16,128,128]{2,1,0:T(8,128)S(1)} %multiply_add_fusion.1), kind=kOutput, calls=%fused_computation.95 | convolution fusion | flops 1610612736 | bytes 8454144 | tf_op jit(solution)/shard_map/nij,jk->nik/dot_general | solution.py:32
  221.3 5.8 %fusion.37 = f32[64,128,128]{1,2,0:T(8,128)S(1)} fusion(f32[64,128,128]{2,1,0:T(8,128)} %bitcast.24, f32[16,128,128]{2,1,0:T(8,128)S(1)} %multiply_add_fusion.1), kind=kOutput, calls=%fused_computation.99 | convolution fusion | flops 1610612736 | bytes 8454144 | tf_op jit(solution)/shard_map/nij,jk->nik/dot_general | solution.py:32
  227.1 5.6 %fusion.39 = f32[64,128,128]{1,2,0:T(8,128)S(1)} fusion(f32[64,128,128]{2,1,0:T(8,128)} %bitcast.24, f32[16,128,128]{2,1,0:T(8,128)S(1)} %multiply_add_fusion.1), kind=kOutput, calls=%fused_computation.103 | convolution fusion | flops 1610612736 | bytes 8454144 | tf_op jit(solution)/shard_map/nij,jk->nik/dot_general | solution.py:32
  232.7 5.6 %fusion.41 = f32[64,128,128]{1,2,0:T(8,128)S(1)} fusion(f32[64,128,128]{2,1,0:T(8,128)} %bitcast.24, f32[16,128,128]{2,1,0:T(8,128)S(1)} %multiply_add_fusion.1), kind=kOutput, calls=%fused_computation.107 | convolution fusion | flops 1610612736 | bytes 8454144 | tf_op jit(solution)/shard_map/nij,jk->nik/dot_general | solution.py:32
  238.3 5.6 %fusion.43 = f32[64,128,128]{1,2,0:T(8,128)S(1)} fusion(f32[64,128,128]{2,1,0:T(8,128)} %bitcast.24, f32[16,128,128]{2,1,0:T(8,128)S(1)} %multiply_add_fusion.1), kind=kOutput, calls=%fused_computation.111 | convolution fusion | flops 1610612736 | bytes 8454144 | tf_op jit(solution)/shard_map/nij,jk->nik/dot_general | solution.py:32
  244.0 5.6 %fusion.45 = f32[64,128,128]{1,2,0:T(8,128)S(1)} fusion(f32[64,128,128]{2,1,0:T(8,128)} %bitcast.24, f32[16,128,128]{2,1,0:T(8,128)S(1)} %multiply_add_fusion.1), kind=kOutput, calls=%fused_computation.115 | convolution fusion | flops 1610612736 | bytes 8454144 | tf_op jit(solution)/shard_map/nij,jk->nik/dot_general | solution.py:32
  249.6 6.0 %fusion.47 = f32[64,128,128]{1,2,0:T(8,128)S(1)} fusion(f32[64,128,128]{2,1,0:T(8,128)} %bitcast.24, f32[16,128,128]{2,1,0:T(8,128)S(1)} %multiply_add_fusion.1), kind=kOutput, calls=%fused_computation.119 | convolution fusion | flops 1610612736 | bytes 8454144 | tf_op jit(solution)/shard_map/nij,jk->nik/dot_general | solution.py:32
  255.6 5.6 %fusion.49 = f32[64,128,128]{1,2,0:T(8,128)S(1)} fusion(f32[64,128,128]{2,1,0:T(8,128)} %bitcast.24, f32[16,128,128]{2,1,0:T(8,128)S(1)} %multiply_add_fusion.1), kind=kOutput, calls=%fused_computation.123 | convolution fusion | flops 1610612736 | bytes 8454144 | tf_op jit(solution)/shard_map/nij,jk->nik/dot_general | solution.py:32
  261.2 5.6 %fusion.51 = f32[64,128,128]{1,2,0:T(8,128)S(1)} fusion(f32[64,128,128]{2,1,0:T(8,128)} %bitcast.24, f32[16,128,128]{2,1,0:T(8,128)S(1)} %multiply_add_fusion.1), kind=kOutput, calls=%fused_computation.127 | convolution fusion | flops 1610612736 | bytes 8454144 | tf_op jit(solution)/shard_map/nij,jk->nik/dot_general | solution.py:32
  266.9 5.8 %fusion.53 = f32[64,128,128]{1,2,0:T(8,128)S(1)} fusion(f32[64,128,128]{2,1,0:T(8,128)} %bitcast.24, f32[16,128,128]{2,1,0:T(8,128)S(1)} %multiply_add_fusion.1), kind=kOutput, calls=%fused_computation.131 | convolution fusion | flops 1610612736 | bytes 8454144 | tf_op jit(solution)/shard_map/nij,jk->nik/dot_general | solution.py:32
  272.7 8.1 %fusion.23 = f32[64,128,128]{1,2,0:T(8,128)} fusion(f32[64,128,128]{2,1,0:T(8,128)} %bitcast.24, f32[16,128,128]{2,1,0:T(8,128)S(1)} %multiply_add_fusion.1), kind=kOutput, calls=%fused_computation.71 | convolution fusion | flops 1610612736 | bytes 8454144 | tf_op jit(solution)/shard_map/nij,jk->nik/dot_general | solution.py:32
  280.7 6.6 %fusion.24 = f32[64,128,128]{2,1,0:T(8,128)} fusion(f32[64,128,128]{1,2,0:T(8,128)} %fusion.25, f32[16,128,128]{2,1,0:T(8,128)S(1)} %multiply_add_fusion), kind=kOutput, calls=%fused_computation.73 | convolution fusion | flops 1610612736 | bytes 8454144 | tf_op jit(solution)/shard_map/ij,njk->nik/dot_general | solution.py:39
  287.3 6.5 %fusion.26 = f32[64,128,128]{2,1,0:T(8,128)} fusion(f32[64,128,128]{1,2,0:T(8,128)} %fusion.27, f32[16,128,128]{2,1,0:T(8,128)S(1)} %multiply_add_fusion), kind=kOutput, calls=%fused_computation.77 | convolution fusion | flops 1610612736 | bytes 8454144 | tf_op jit(solution)/shard_map/ij,njk->nik/dot_general | solution.py:39
  293.9 6.6 %fusion.28 = f32[64,128,128]{2,1,0:T(8,128)} fusion(f32[64,128,128]{1,2,0:T(8,128)} %fusion.29, f32[16,128,128]{2,1,0:T(8,128)S(1)} %multiply_add_fusion), kind=kOutput, calls=%fused_computation.81 | convolution fusion | flops 1610612736 | bytes 8454144 | tf_op jit(solution)/shard_map/ij,njk->nik/dot_general | solution.py:39
  300.4 6.5 %fusion.30 = f32[64,128,128]{2,1,0:T(8,128)} fusion(f32[64,128,128]{1,2,0:T(8,128)} %fusion.31, f32[16,128,128]{2,1,0:T(8,128)S(1)} %multiply_add_fusion), kind=kOutput, calls=%fused_computation.85 | convolution fusion | flops 1610612736 | bytes 8454144 | tf_op jit(solution)/shard_map/ij,njk->nik/dot_general | solution.py:39
  307.0 6.8 %fusion.32 = f32[64,128,128]{2,1,0:T(8,128)} fusion(f32[64,128,128]{1,2,0:T(8,128)} %fusion.33, f32[16,128,128]{2,1,0:T(8,128)S(1)} %multiply_add_fusion), kind=kOutput, calls=%fused_computation.89 | convolution fusion | flops 1610612736 | bytes 8454144 | tf_op jit(solution)/shard_map/ij,njk->nik/dot_general | solution.py:39
  313.7 6.5 %fusion.34 = f32[64,128,128]{2,1,0:T(8,128)} fusion(f32[64,128,128]{1,2,0:T(8,128)} %fusion.35, f32[16,128,128]{2,1,0:T(8,128)S(1)} %multiply_add_fusion), kind=kOutput, calls=%fused_computation.93 | convolution fusion | flops 1610612736 | bytes 8454144 | tf_op jit(solution)/shard_map/ij,njk->nik/dot_general | solution.py:39
  320.3 5.0 fusion.36
  325.3 5.0 fusion.38
  330.2 4.9 fusion.40
  335.2 4.9 fusion.42
  340.1 5.4 %fusion.44 = f32[64,128,128]{2,1,0:T(8,128)} fusion(f32[64,128,128]{1,2,0:T(8,128)S(1)} %fusion.45, f32[16,128,128]{2,1,0:T(8,128)S(1)} %multiply_add_fusion), kind=kOutput, calls=%fused_computation.113 | convolution fusion | flops 1610612736 | bytes 8454144 | tf_op jit(solution)/shard_map/ij,njk->nik/dot_general | solution.py:39
  345.5 5.0 fusion.46
  350.5 4.9 fusion.48
  355.4 4.9 fusion.50
  360.6 5.0 fusion.52
  365.9 70.1 %fusion.4 = f32[64,128,128,1]{1,2,0,3:T(8,128)} fusion(f32[64,128,128]{2,1,0:T(8,128)} %fusion.24, f32[64,128,128]{2,1,0:T(8,128)} %fusion.26, f32[64,128,128]{2,1,0:T(8,128)} %fusion.28, f32[64,128,128]{2,1,0:T(8,128)} %fusion.30, f32[64,128,128]{2,1,0:T(8,128)} %fusion.32, f32[64,128,128]{2,1,0:T(8,128)} %fusion.34, f32[64,128,128]{2,1,0:T(8,128)} %fusion.36, ...), kind=kOutput, calls=%fused_computation.10 | convolution fusion | flops 1729101824 | bytes 78217728 | tf_op jit(solution)/shard_map/ij,njk->nik/dot_general | solution.py:39
  436.0 5.6 %copy.241 = f32[64,128,128,1]{2,0,3,1:T(8,128)} copy(f32[64,128,128,1]{1,2,0,3:T(8,128)} %fusion.4) | data formatting | bytes 8388608 | tf_op jit(solution)/shard_map/mul | solution.py:121
  441.6 4.4 convolution_bitcast_fusion
  447.0 4.7 broadcast_divide_fusion
  451.7 5.6 %copy.223 = f32[8,8,128,128]{3,1,0,2:T(8,128)} copy(f32[8,8,128,128]{2,3,1,0:T(8,128)} %broadcast_divide_fusion) | data formatting | bytes 8388608 | tf_op jit(solution)/shard_map/div | solution.py:117
  457.2 4.5 fusion.19
  462.5 10.0 %reduce-scatter.3.cloned.1.call-done = f32[64,256]{1,0:T(8,128)} async-done(((f32[256,256]{1,0:T(8,128)}), f32[64,256]{1,0:T(8,128)}) %reduce-scatter.3.cloned.1.call-update) | async-done | bytes 65552 | tf_op jit(solution)/shard_map/reduce_scatter | solution.py:141
  472.5 27.7 %reduce-scatter.5.cloned.1.call-done = f32[64,256]{1,0:T(8,128)} async-done(((f32[256,256]{1,0:T(8,128)}), f32[64,256]{1,0:T(8,128)}) %reduce-scatter.5.cloned.1.call-update) | async-done | bytes 65552 | tf_op jit(solution)/shard_map/reduce_scatter | solution.py:142
  (263 shorter events, 22.6 us)
Async XLA Ops:
  7.2 30.4 %copy-start = (f32[1,1,32,128,128]{4,3,2,1,0:T(8,128)S(1)}, f32[1,1,32,128,128]{4,3,2,1,0:T(8,128)}, u32[]{:S(2)}) copy-start(f32[1,1,32,128,128]{4,3,2,1,0:T(8,128)} %param.12) | copy-start | bytes 6291460
  7.2 27.1 %copy-start.3 = (f32[16,41]{1,0:T(8,128)S(1)}, f32[16,41]{1,0:T(8,128)}, u32[]{:S(2)}) copy-start(f32[16,41]{1,0:T(8,128)} %param.19) | copy-start | bytes 7876
  9.7 12.2 %copy-start.81 = (s32[64]{0:T(128)}, s32[64]{0:T(128)S(1)}, u32[]{:S(2)}) copy-start(s32[64]{0:T(128)S(1)} %select_reduce_fusion) | copy-start | bytes 772
  13.5 43.8 %all-to-all-start = ((f32[8,8,4]{1,2,0:T(4,128)}), f32[8,8,4]{1,2,0:T(4,128)S(1)}, u32[]{:S(2)}, u32[]{:S(2)}) async-start(f32[8,8,4]{1,2,0:T(4,128)} %select_multiply_fusion.1), calls=%async_computation | async-start | bytes 32768 | tf_op jit(solution)/shard_map/all_to_all | solution.py:105
  40.4 6.8 %copy-start.82 = (s32[64]{0:T(128)S(1)}, s32[64]{0:T(128)}, u32[]{:S(2)}) copy-start(s32[64]{0:T(128)} %fusion.253) | copy-start | bytes 772
  49.9 5.9 %copy-start.2 = (f32[16,41]{1,0:T(8,128)S(1)}, f32[16,41]{1,0:T(8,128)}, u32[]{:S(2)}) copy-start(f32[16,41]{1,0:T(8,128)} %param.18) | copy-start | bytes 7876
  57.3 10.8 %all-to-all-start.2 = ((f32[8,1,768]{2,1,0:T(1,128)}), f32[8,1,768]{2,1,0:T(1,128)S(1)}, u32[]{:S(2)}, u32[]{:S(2)}) async-start(f32[8,1,768]{2,1,0:T(1,128)} %reshape.5189), calls=%async_computation.2 | async-start | bytes 49152 | tf_op jit(solution)/shard_map/all_to_all | solution.py:102
  68.7 98.8 %all-to-all-start.3 = ((f32[8,8,128,128]{3,2,1,0:T(8,128)}), f32[8,8,128,128]{3,2,1,0:T(8,128)}, u32[]{:S(2)}, u32[]{:S(2)}) async-start(f32[8,8,128,128]{3,2,1,0:T(8,128)} %bitcast.552), calls=%async_computation.3 | async-start | bytes 8388608 | tf_op jit(solution)/shard_map/all_to_all | solution.py:100
  74.0 6.3 %copy-start.5 = (f32[128,128]{1,0:T(8,128)S(1)}, f32[128,128]{1,0:T(8,128)}, u32[]{:S(2)}) copy-start(f32[128,128]{1,0:T(8,128)} %get-tuple-element.309) | copy-start | bytes 196612
  74.0 6.3 %copy-start.6 = (f32[128,128]{1,0:T(8,128)S(1)}, f32[128,128]{1,0:T(8,128)}, u32[]{:S(2)}) copy-start(f32[128,128]{1,0:T(8,128)} %get-tuple-element.306) | copy-start | bytes 196612
  74.0 6.3 %copy-start.7 = (f32[128,128]{1,0:T(8,128)S(1)}, f32[128,128]{1,0:T(8,128)}, u32[]{:S(2)}) copy-start(f32[128,128]{1,0:T(8,128)} %get-tuple-element.307) | copy-start | bytes 196612
  74.0 6.3 %copy-start.8 = (f32[128,128]{1,0:T(8,128)S(1)}, f32[128,128]{1,0:T(8,128)}, u32[]{:S(2)}) copy-start(f32[128,128]{1,0:T(8,128)} %get-tuple-element.304) | copy-start | bytes 196612
  74.0 6.3 %copy-start.9 = (f32[128,128]{1,0:T(8,128)S(1)}, f32[128,128]{1,0:T(8,128)}, u32[]{:S(2)}) copy-start(f32[128,128]{1,0:T(8,128)} %get-tuple-element.305) | copy-start | bytes 196612
  74.1 6.3 %copy-start.10 = (f32[128,128]{1,0:T(8,128)S(1)}, f32[128,128]{1,0:T(8,128)}, u32[]{:S(2)}) copy-start(f32[128,128]{1,0:T(8,128)} %get-tuple-element.302) | copy-start | bytes 196612
  74.1 6.3 %copy-start.11 = (f32[128,128]{1,0:T(8,128)S(1)}, f32[128,128]{1,0:T(8,128)}, u32[]{:S(2)}) copy-start(f32[128,128]{1,0:T(8,128)} %get-tuple-element.303) | copy-start | bytes 196612
  74.1 6.3 %copy-start.12 = (f32[128,128]{1,0:T(8,128)S(1)}, f32[128,128]{1,0:T(8,128)}, u32[]{:S(2)}) copy-start(f32[128,128]{1,0:T(8,128)} %get-tuple-element.300) | copy-start | bytes 196612
  74.1 6.3 %copy-start.13 = (f32[128,128]{1,0:T(8,128)S(1)}, f32[128,128]{1,0:T(8,128)}, u32[]{:S(2)}) copy-start(f32[128,128]{1,0:T(8,128)} %get-tuple-element.301) | copy-start | bytes 196612
  74.1 6.3 %copy-start.14 = (f32[128,128]{1,0:T(8,128)S(1)}, f32[128,128]{1,0:T(8,128)}, u32[]{:S(2)}) copy-start(f32[128,128]{1,0:T(8,128)} %get-tuple-element.298) | copy-start | bytes 196612
  74.1 6.3 %copy-start.15 = (f32[128,128]{1,0:T(8,128)S(1)}, f32[128,128]{1,0:T(8,128)}, u32[]{:S(2)}) copy-start(f32[128,128]{1,0:T(8,128)} %get-tuple-element.299) | copy-start | bytes 196612
  74.1 6.3 %copy-start.16 = (f32[128,128]{1,0:T(8,128)S(1)}, f32[128,128]{1,0:T(8,128)}, u32[]{:S(2)}) copy-start(f32[128,128]{1,0:T(8,128)} %get-tuple-element.296) | copy-start | bytes 196612
  74.1 6.3 %copy-start.17 = (f32[128,128]{1,0:T(8,128)S(1)}, f32[128,128]{1,0:T(8,128)}, u32[]{:S(2)}) copy-start(f32[128,128]{1,0:T(8,128)} %get-tuple-element.297) | copy-start | bytes 196612
  74.1 6.3 %copy-start.18 = (f32[128,128]{1,0:T(8,128)S(1)}, f32[128,128]{1,0:T(8,128)}, u32[]{:S(2)}) copy-start(f32[128,128]{1,0:T(8,128)} %get-tuple-element.294) | copy-start | bytes 196612
  74.1 6.3 %copy-start.19 = (f32[128,128]{1,0:T(8,128)S(1)}, f32[128,128]{1,0:T(8,128)}, u32[]{:S(2)}) copy-start(f32[128,128]{1,0:T(8,128)} %get-tuple-element.295) | copy-start | bytes 196612
  74.2 6.3 %copy-start.20 = (f32[128,128]{1,0:T(8,128)S(1)}, f32[128,128]{1,0:T(8,128)}, u32[]{:S(2)}) copy-start(f32[128,128]{1,0:T(8,128)} %get-tuple-element.292) | copy-start | bytes 196612
  74.2 6.3 %copy-start.79 = (f32[16]{0:T(128)S(1)}, f32[16]{0:T(128)}, u32[]{:S(2)}) copy-start(f32[16]{0:T(128)} %get-tuple-element.68) | copy-start | bytes 196
  79.7 5.2 %copy-start.60 = (f32[16]{0:T(128)S(1)}, f32[16]{0:T(128)}, u32[]{:S(2)}) copy-start(f32[16]{0:T(128)} %get-tuple-element.23) | copy-start | bytes 196
  84.8 8.9 %copy-start.55 = (f32[128]{0:T(128)S(1)}, f32[128]{0:T(128)}, u32[]{:S(2)}) copy-start(f32[128]{0:T(128)} %iota_convert_fusion) | copy-start | bytes 1540
  167.6 198.0 %all-to-all-start.1 = ((f32[8,8,128,128]{2,3,1,0:T(8,128)}), f32[8,8,128,128]{2,3,1,0:T(8,128)}, u32[]{:S(2)}, u32[]{:S(2)}) async-start(f32[8,8,128,128]{2,3,1,0:T(8,128)} %copy.198), calls=%async_computation.1 | async-start | bytes 8388608 | tf_op jit(solution)/shard_map/all_to_all | solution.py:101
  172.2 300.4 %reduce-scatter.3.cloned.1.call-start = ((), (), s32[]{:S(2)}) async-start(), calls=%async_computation.6 | async-start | bytes 327680 | tf_op jit(solution)/shard_map/reduce_scatter | solution.py:141
  360.3 5.3 %copy-start.22 = (f32[64,128]{1,0:T(8,128)S(1)}, f32[64,128]{1,0:T(8,128)}, u32[]{:S(2)}) copy-start(f32[64,128]{1,0:T(8,128)} %get-tuple-element.208) | copy-start | bytes 98308
  360.3 5.3 %copy-start.23 = (f32[64,128]{1,0:T(8,128)S(1)}, f32[64,128]{1,0:T(8,128)}, u32[]{:S(2)}) copy-start(f32[64,128]{1,0:T(8,128)} %get-tuple-element.209) | copy-start | bytes 98308
  360.3 5.3 %copy-start.24 = (f32[64,128]{1,0:T(8,128)S(1)}, f32[64,128]{1,0:T(8,128)}, u32[]{:S(2)}) copy-start(f32[64,128]{1,0:T(8,128)} %get-tuple-element.210) | copy-start | bytes 98308
  360.3 5.3 %copy-start.25 = (f32[64,128]{1,0:T(8,128)S(1)}, f32[64,128]{1,0:T(8,128)}, u32[]{:S(2)}) copy-start(f32[64,128]{1,0:T(8,128)} %get-tuple-element.211) | copy-start | bytes 98308
  360.4 5.3 %copy-start.26 = (f32[64,128]{1,0:T(8,128)S(1)}, f32[64,128]{1,0:T(8,128)}, u32[]{:S(2)}) copy-start(f32[64,128]{1,0:T(8,128)} %get-tuple-element.212) | copy-start | bytes 98308
  360.4 5.3 %copy-start.27 = (f32[64,128]{1,0:T(8,128)S(1)}, f32[64,128]{1,0:T(8,128)}, u32[]{:S(2)}) copy-start(f32[64,128]{1,0:T(8,128)} %get-tuple-element.213) | copy-start | bytes 98308
  360.4 5.3 %copy-start.28 = (f32[64,128]{1,0:T(8,128)S(1)}, f32[64,128]{1,0:T(8,128)}, u32[]{:S(2)}) copy-start(f32[64,128]{1,0:T(8,128)} %get-tuple-element.232) | copy-start | bytes 98308
  360.4 5.3 %copy-start.29 = (f32[64,128]{1,0:T(8,128)S(1)}, f32[64,128]{1,0:T(8,128)}, u32[]{:S(2)}) copy-start(f32[64,128]{1,0:T(8,128)} %get-tuple-element.233) | copy-start | bytes 98308
  360.4 5.3 %copy-start.30 = (f32[64,128]{1,0:T(8,128)S(1)}, f32[64,128]{1,0:T(8,128)}, u32[]{:S(2)}) copy-start(f32[64,128]{1,0:T(8,128)} %get-tuple-element.234) | copy-start | bytes 98308
  360.4 5.3 %copy-start.31 = (f32[64,128]{1,0:T(8,128)S(1)}, f32[64,128]{1,0:T(8,128)}, u32[]{:S(2)}) copy-start(f32[64,128]{1,0:T(8,128)} %get-tuple-element.235) | copy-start | bytes 98308
  360.4 5.3 %copy-start.32 = (f32[64,128]{1,0:T(8,128)S(1)}, f32[64,128]{1,0:T(8,128)}, u32[]{:S(2)}) copy-start(f32[64,128]{1,0:T(8,128)} %get-tuple-element.236) | copy-start | bytes 98308
  360.4 5.3 %copy-start.33 = (f32[64,128]{1,0:T(8,128)S(1)}, f32[64,128]{1,0:T(8,128)}, u32[]{:S(2)}) copy-start(f32[64,128]{1,0:T(8,128)} %get-tuple-element.237) | copy-start | bytes 98308
  360.4 5.3 %copy-start.34 = (f32[64,128]{1,0:T(8,128)S(1)}, f32[64,128]{1,0:T(8,128)}, u32[]{:S(2)}) copy-start(f32[64,128]{1,0:T(8,128)} %get-tuple-element.238) | copy-start | bytes 98308
  360.4 5.3 %copy-start.35 = (f32[64,128]{1,0:T(8,128)S(1)}, f32[64,128]{1,0:T(8,128)}, u32[]{:S(2)}) copy-start(f32[64,128]{1,0:T(8,128)} %get-tuple-element.239) | copy-start | bytes 98308
  360.5 5.3 %copy-start.36 = (f32[64,128]{1,0:T(8,128)S(1)}, f32[64,128]{1,0:T(8,128)}, u32[]{:S(2)}) copy-start(f32[64,128]{1,0:T(8,128)} %get-tuple-element.240) | copy-start | bytes 98308
  360.5 5.3 %copy-start.37 = (f32[64,128]{1,0:T(8,128)S(1)}, f32[64,128]{1,0:T(8,128)}, u32[]{:S(2)}) copy-start(f32[64,128]{1,0:T(8,128)} %get-tuple-element.241) | copy-start | bytes 98308
  360.5 5.3 %copy-start.38 = (f32[64,128]{1,0:T(8,128)S(1)}, f32[64,128]{1,0:T(8,128)}, u32[]{:S(2)}) copy-start(f32[64,128]{1,0:T(8,128)} %get-tuple-element.242) | copy-start | bytes 98308
  360.5 5.3 %copy-start.39 = (f32[64,128]{1,0:T(8,128)S(1)}, f32[64,128]{1,0:T(8,128)}, u32[]{:S(2)}) copy-start(f32[64,128]{1,0:T(8,128)} %get-tuple-element.243) | copy-start | bytes 98308
  360.5 5.3 %copy-start.40 = (f32[64,128]{1,0:T(8,128)S(1)}, f32[64,128]{1,0:T(8,128)}, u32[]{:S(2)}) copy-start(f32[64,128]{1,0:T(8,128)} %get-tuple-element.244) | copy-start | bytes 98308
  360.5 5.3 %copy-start.41 = (f32[64,128]{1,0:T(8,128)S(1)}, f32[64,128]{1,0:T(8,128)}, u32[]{:S(2)}) copy-start(f32[64,128]{1,0:T(8,128)} %get-tuple-element.214) | copy-start | bytes 98308
  360.5 5.3 %copy-start.42 = (f32[64,128]{1,0:T(8,128)S(1)}, f32[64,128]{1,0:T(8,128)}, u32[]{:S(2)}) copy-start(f32[64,128]{1,0:T(8,128)} %get-tuple-element.215) | copy-start | bytes 98308
  360.5 5.3 %copy-start.43 = (f32[64,128]{1,0:T(8,128)S(1)}, f32[64,128]{1,0:T(8,128)}, u32[]{:S(2)}) copy-start(f32[64,128]{1,0:T(8,128)} %get-tuple-element.216) | copy-start | bytes 98308
  360.5 5.3 %copy-start.44 = (f32[64,128]{1,0:T(8,128)S(1)}, f32[64,128]{1,0:T(8,128)}, u32[]{:S(2)}) copy-start(f32[64,128]{1,0:T(8,128)} %get-tuple-element.217) | copy-start | bytes 98308
  360.5 5.3 %copy-start.45 = (f32[64,128]{1,0:T(8,128)S(1)}, f32[64,128]{1,0:T(8,128)}, u32[]{:S(2)}) copy-start(f32[64,128]{1,0:T(8,128)} %get-tuple-element.218) | copy-start | bytes 98308
  360.6 5.3 %copy-start.46 = (f32[64,128]{1,0:T(8,128)S(1)}, f32[64,128]{1,0:T(8,128)}, u32[]{:S(2)}) copy-start(f32[64,128]{1,0:T(8,128)} %get-tuple-element.219) | copy-start | bytes 98308
  360.6 5.3 %copy-start.47 = (f32[64,128]{1,0:T(8,128)S(1)}, f32[64,128]{1,0:T(8,128)}, u32[]{:S(2)}) copy-start(f32[64,128]{1,0:T(8,128)} %get-tuple-element.220) | copy-start | bytes 98308
  360.6 5.3 %copy-start.48 = (f32[64,128]{1,0:T(8,128)S(1)}, f32[64,128]{1,0:T(8,128)}, u32[]{:S(2)}) copy-start(f32[64,128]{1,0:T(8,128)} %get-tuple-element.221) | copy-start | bytes 98308
  360.6 5.3 %copy-start.49 = (f32[64,128]{1,0:T(8,128)S(1)}, f32[64,128]{1,0:T(8,128)}, u32[]{:S(2)}) copy-start(f32[64,128]{1,0:T(8,128)} %get-tuple-element.222) | copy-start | bytes 98308
  360.6 5.3 %copy-start.50 = (f32[64,128]{1,0:T(8,128)S(1)}, f32[64,128]{1,0:T(8,128)}, u32[]{:S(2)}) copy-start(f32[64,128]{1,0:T(8,128)} %get-tuple-element.223) | copy-start | bytes 98308
  360.6 5.3 %copy-start.51 = (f32[64,128]{1,0:T(8,128)S(1)}, f32[64,128]{1,0:T(8,128)}, u32[]{:S(2)}) copy-start(f32[64,128]{1,0:T(8,128)} %get-tuple-element.224) | copy-start | bytes 98308
  360.6 5.3 %copy-start.52 = (f32[64,128]{1,0:T(8,128)S(1)}, f32[64,128]{1,0:T(8,128)}, u32[]{:S(2)}) copy-start(f32[64,128]{1,0:T(8,128)} %get-tuple-element.225) | copy-start | bytes 98308
  360.6 5.3 %copy-start.53 = (f32[64,128]{1,0:T(8,128)S(1)}, f32[64,128]{1,0:T(8,128)}, u32[]{:S(2)}) copy-start(f32[64,128]{1,0:T(8,128)} %get-tuple-element.226) | copy-start | bytes 98308
  436.0 5.6 %copy-start.54 = (f32[64,2,2,1]{0,2,1,3:T(2,128)S(1)}, f32[64,2,2,1]{0,2,1,3:T(2,128)}, u32[]{:S(2)}) copy-start(f32[64,2,2,1]{0,2,1,3:T(2,128)} %reshape.5088) | copy-start | bytes 3076
  446.9 53.3 %reduce-scatter.5.cloned.1.call-start = ((), (), s32[]{:S(2)}) async-start(), calls=%async_computation.7 | async-start | bytes 327680 | tf_op jit(solution)/shard_map/reduce_scatter | solution.py:142
  451.7 48.5 %copy-start.1 = (f32[1,1,32,128,128]{4,3,2,1,0:T(8,128)S(1)}, f32[1,1,32,128,128]{4,3,2,1,0:T(8,128)}, u32[]{:S(2)}) copy-start(f32[1,1,32,128,128]{4,3,2,1,0:T(8,128)} %param.12) | copy-start | bytes 6291460
  (25 other events, 123.4 us)
Sparse Core Ops, SparseCore 0:
  447.0 25.4 reduce-scatter.2
  476.1 24.0 reduce-scatter.4
where the time goes:
time: 513 us; the launch traced here: 507 us
  matrix products  272 us (53%)
  waiting for transfers between devices  112 us (22%)
  local copies, waits for them, and re-layouts  46.3 us (9%)
  other arithmetic  39.5 us (8%)
  starting transfers between devices  21.5 us (4%)
  between operations  16.7 us (3%)
    dot_general x16, matrix products, match_blocks(): jnp.einsum('ij,njk->nik', col_band[basis_index], spread, precision=highes...  155 us
    dot_general x16, matrix products, match_blocks(): jnp.einsum('nij,jk->nik', pixels, row_band[basis_index], precision=highes...  108 us
    all_to_all x1, waiting for transfers between devices, on_device(): lax.all_to_all(slot_pixels, 'patch', split_axis=0, concat_axis=0, tiled=T...  69.1 us
    reduce_scatter x1, waiting for transfers between devices, on_device(): lax.psum_scatter(weight_patch, 'visit', scatter_dimension=0, tiled=True)  27.7 us
  transfers between devices with their start and end apart: 6, of which 4 were waited for; matrix products, arithmetic and copies ran while one was open for 53% of the time, Pallas kernels for 0%

commit v1 on v0

v1 whole, which is shorter than its diff:
```python
import functools

import jax
import jax.numpy as jnp
from jax import lax
from jax.experimental import pallas as pl
from jax.experimental.pallas import tpu as pltpu
from jax.sharding import PartitionSpec as P

f32 = jnp.float32
bf16 = jnp.bfloat16

SHARE = 1.0 / 32.0
KEEP = 1.0 - SHARE
VMEM_BYTES = 40 * 2**20


def split_left(value):
    first = value.astype(bf16)
    return first, (value - KEEP * first.astype(f32)).astype(bf16)


def split_right(value):
    first = (KEEP * value).astype(bf16)
    return first, ((value - first.astype(f32)) * (1.0 / SHARE)).astype(bf16)


def place_of(where, target, quarter):
    core = lax.rem(target, 2) ^ where[0]
    depth = lax.rem(target // 2 - where[1] + where[2], where[2])
    return core, depth, (quarter // 2) ^ where[3], lax.rem(quarter, 2)


def prepare_kernel(
    where, targets, quarters, count, variance, row_taps, col_taps,
    keep_out, send_out, col_band, row_band, canvas, padded,
):
    blocks, side, _ = variance.shape
    half = side // 2
    nbasis, taps = row_taps.shape
    radius = (taps - 1) // 2
    canvas[...] = jnp.zeros_like(canvas)

    def add_block(n, carry):
        live = jnp.where(n < count[0], 1.0, 0.0).astype(f32)
        inverse = live / variance[n]
        core, depth, down, across = place_of(where, targets[n], quarters[n])
        column = pl.ds(pl.multiple_of(across * side, side), side)
        for part in range(2):
            canvas[core, part ^ where[4], down, depth, :, column] += inverse[
                part * half : (part + 1) * half
            ]
        return carry

    lax.fori_loop(0, blocks, add_block, 0)
    keep_out[...] = canvas[0]
    send_out[...] = canvas[1]

    row = lax.broadcasted_iota(jnp.int32, (side, side), 0)
    column = lax.broadcasted_iota(jnp.int32, (side, side), 1)
    near = jnp.abs(row - column) <= radius
    padded[...] = jnp.zeros_like(padded)
    padded[:, :taps] = row_taps[...]
    row_placed = pltpu.roll(padded[...], side - radius, 1)
    padded[:, :taps] = col_taps[...]
    turn = (lax.rem(column - radius + row + side, side) == 0).astype(f32)
    col_placed = jnp.dot(
        padded[...], turn, precision=lax.Precision.HIGHEST, preferred_element_type=f32
    )
    for k in range(nbasis):
        base = jnp.broadcast_to(row_placed[k : k + 1], (side, side))
        band = jnp.where(near, pltpu.roll(base, 0, 1, stride=1, stride_axis=0), 0.0)
        first, second = split_right(band)
        row_band[k, :side, :] = first
        row_band[k, side:, :] = second
        base = jnp.broadcast_to(col_placed[k : k + 1], (side, side))
        band = jnp.where(near, pltpu.roll(base, 0, 1, stride=1, stride_axis=0), 0.0)
        first, second = split_left(band)
        col_band[k, :, :side] = first
        col_band[k, :, side:] = second


def prepare(where, targets, quarters, count, variance, row_taps, col_taps, depths):
    blocks, side, _ = variance.shape
    nbasis = row_taps.shape[0]
    half = side // 2
    part = jax.ShapeDtypeStruct((2, 2, depths, half, 2 * side), f32)
    scalar = pl.BlockSpec(memory_space=pltpu.SMEM)
    vector = pl.BlockSpec(memory_space=pltpu.VMEM)
    return pl.pallas_call(
        prepare_kernel,
        out_shape=(
            part,
            part,
            jax.ShapeDtypeStruct((nbasis, side, 2 * side), bf16),
            jax.ShapeDtypeStruct((nbasis, 2 * side, side), bf16),
        ),
        in_specs=[scalar] * 4 + [vector] * 3,
        out_specs=[vector] * 4,
        scratch_shapes=[
            pltpu.VMEM((2, 2, 2, depths, half, 2 * side), f32),
            pltpu.VMEM((nbasis, side), f32),
        ],
        compiler_params=pltpu.CompilerParams(vmem_limit_bytes=VMEM_BYTES),
        cost_estimate=pl.CostEstimate(flops=10**7, bytes_accessed=10**7, transcendentals=0),
    )(where, targets, quarters, count, variance, row_taps, col_taps)


def match_kernel(
    first_row, where, targets, quarters, table_rows, count, pixels, variance, table,
    col_band, row_band, keep_out, send_out, canvas, total, coefficients,
):
    blocks, side, _ = pixels.shape
    nbasis = col_band.shape[0]
    rows = canvas.shape[3]
    group = total.shape[0]
    top = pl.multiple_of(first_row[0], rows)
    canvas[...] = jnp.zeros_like(canvas)
    entries = table.shape[2]
    coefficients[:, :, :entries] = table[...]
    lane = lax.broadcasted_iota(jnp.int32, (1, side), 1).astype(f32)
    sub = lax.broadcasted_iota(jnp.int32, (8, side), 0).astype(f32)
    step = 8.0 / side
    left = col_band[:, pl.ds(top, rows), :].reshape(nbasis * rows, 2 * side)

    def add_group(j, carry):
        terms = []
        for member in range(group):
            n = group * j + member
            quarter = quarters[n]
            across = (lane + 0.5) / side - 1.0 + lax.rem(quarter, 2).astype(f32)
            down = (sub + 0.5 + top.astype(f32)) / side - 1.0 + (quarter // 2).astype(f32)
            entry = table_rows[n]
            chunk = coefficients[:, :, pl.ds(pl.multiple_of((entry // 128) * 128, 128), 128)]
            chunk = chunk.reshape(-1, 128)
            chunk = pltpu.roll(chunk, lax.rem(128 - lax.rem(entry, 128), 128), 1)
            poly = jnp.broadcast_to(chunk[:, :1], (chunk.shape[0], side))
            poly = [poly[i * nbasis : (i + 1) * nbasis] for i in range(chunk.shape[0] // nbasis)]
            constant = poly[0] + across * (poly[1] + across * poly[3])
            linear = poly[2] + across * poly[4]
            terms.append((constant, linear, poly[5], down))
        halves = []
        for pair in range(group // 2):
            n = group * j + 2 * pair
            both = jnp.concatenate([pixels[n], pixels[n + 1]], axis=1)
            right = jnp.concatenate(split_right(both), axis=0)
            convolved = jnp.dot(left, right, preferred_element_type=f32)
            halves.append(split_left(convolved))
        for k in range(nbasis):
            at = slice(k * rows, (k + 1) * rows)
            stacked = []
            for member in range(group):
                first, second = halves[member // 2]
                lanes = slice((member % 2) * side, (member % 2 + 1) * side)
                stacked.append(jnp.concatenate([first[at, lanes], second[at, lanes]], axis=1))
            spread = jnp.dot(
                jnp.concatenate(stacked, axis=0), row_band[k], preferred_element_type=f32
            )
            for member in range(group):
                constant, linear, square, down = terms[member]
                b, d = linear[k : k + 1], square[k : k + 1]
                weight = constant[k : k + 1] + down * (b + down * d)
                change = step * b + d * (2.0 * step * down + step * step)
                second_change = (2.0 * step * step) * d
                for i in range(rows // 8):
                    value = weight * spread[member * rows + 8 * i : member * rows + 8 * i + 8]
                    if k == 0:
                        total[member, 8 * i : 8 * i + 8] = value
                    else:
                        total[member, 8 * i : 8 * i + 8] += value
                    if i < rows // 8 - 1:
                        weight = weight + change
                        change = change + second_change
        for member in range(group):
            n = group * j + member
            live = jnp.where(n < count[0], 1.0, 0.0).astype(f32)
            core, depth, down, across = place_of(where, targets[n], quarters[n])
            column = pl.ds(pl.multiple_of(across * side, side), side)
            canvas[core, down, depth, :, column] += (
                live / variance[n, pl.ds(top, rows), :]
            ) * total[member]
        return carry

    lax.fori_loop(0, blocks // group, add_group, 0)
    keep_out[...] = canvas[0]
    send_out[...] = canvas[1]


def match(
    first_row, rows, where, targets, quarters, table_rows, count, pixels, variance, table,
    col_band, row_band, depths,
):
    blocks, side, _ = pixels.shape
    group = min(blocks, 256 // rows)
    part = jax.ShapeDtypeStruct((2, depths, rows, 2 * side), f32)
    scalar = pl.BlockSpec(memory_space=pltpu.SMEM)
    vector = pl.BlockSpec(memory_space=pltpu.VMEM)
    entries = -(-table.shape[2] // 128) * 128
    return pl.pallas_call(
        match_kernel,
        out_shape=(part, part),
        in_specs=[scalar] * 6 + [vector] * 5,
        out_specs=[vector] * 2,
        scratch_shapes=[
            pltpu.VMEM((2, 2, depths, rows, 2 * side), f32),
            pltpu.VMEM((group, rows, side), f32),
            pltpu.VMEM(table.shape[:2] + (entries,), f32),
        ],
        compiler_params=pltpu.CompilerParams(vmem_limit_bytes=VMEM_BYTES),
        cost_estimate=pl.CostEstimate(
            flops=2 * blocks * rows * side * 20 * 512, bytes_accessed=10**7, transcendentals=0
        ),
    )(
        first_row, where, targets, quarters, table_rows, count, pixels, variance, table,
        col_band, row_band,
    )


def on_device(
    image, variance, dest_patch, quadrant, coef_index, block_count, coef_table, row_taps, col_taps
):
    pixels = image[0, 0]
    variances = variance[0, 0]
    targets = dest_patch[0, 0]
    quarters = quadrant[0, 0]
    table_rows = coef_index[0, 0]
    count = block_count[0]
    owners = lax.axis_size("patch")
    visits = lax.axis_size("visit")
    depths = owners // 2
    half = pixels.shape[1] // 2
    patch_at = lax.axis_index("patch")
    visit_at = lax.axis_index("visit")
    my_x = lax.rem(visit_at, 2)
    where = jnp.stack(
        [lax.rem(patch_at, 2), patch_at // 2, jnp.int32(depths), visit_at // 2, my_x]
    ).astype(jnp.int32)
    table = jnp.transpose(coef_table, (2, 1, 0))

    def over_core(value):
        return lax.ppermute(value, "patch", [(i, i ^ 1) for i in range(owners)])

    def over_visit(value, flip):
        return lax.ppermute(value, "visit", [(i, i ^ flip) for i in range(visits)])

    def over_depth(value, shift):
        return lax.ppermute(
            value, "patch", [(i, (i + 2 * shift) % owners) for i in range(owners)]
        )

    def finish(value):
        pieces = [over_depth(value[s], s) for s in range(1, depths)]
        return functools.reduce(jnp.add, pieces, value[0])

    keep, send, col_band, row_band = prepare(
        where, targets, quarters, count, variances, row_taps, col_taps, depths
    )
    got = over_core(send)
    mine = {}
    for x in range(2):
        for y in range(2):
            mine[x, y] = keep[x, y] + got[x, y]
    weight_part = (
        mine[0, 0]
        + over_visit(mine[1, 0], 1)
        + over_visit(mine[0, 1], 2)
        + over_visit(mine[1, 1], 3)
    )
    weight_sum = finish(weight_part)

    def run(x):
        first_row = ((my_x ^ x) * half).astype(jnp.int32)[None]
        return match(
            first_row, half, where, targets, quarters, table_rows, count, pixels, variances,
            table, col_band, row_band, depths,
        )

    keep_far, send_far = run(1)
    got_far = over_core(send_far)
    far = [keep_far[y] + got_far[y] for y in range(2)]
    from_x = over_visit(far[0], 1)
    from_xy = over_visit(far[1], 3)
    keep_near, send_near = run(0)
    got_near = over_core(send_near)
    near = [keep_near[y] + got_near[y] for y in range(2)]
    from_y = over_visit(near[1], 2)
    weighted_sum = finish(near[0] + from_x + from_y + from_xy)
    return weighted_sum[None], weight_sum[None]


def solution(mesh):
    placed = (
        P("visit", "patch", None, None, None),
        P("visit", "patch", None, None, None),
        P("visit", "patch", None),
        P("visit", "patch", None),
        P("visit", "patch", None),
        P("visit", "patch"),
        P(),
        P(),
        P(),
    )
    return jax.shard_map(
        on_device,
        mesh=mesh,
        in_specs=placed,
        out_specs=(P("patch", "visit", None), P("patch", "visit", None)),
        check_vma=False,
    )
```

time: 513 us -> 84.6 us (0.16)
  matrix products: 272 us -> 0 us
  waiting for transfers between devices: 112 us -> 13.4 us
  other arithmetic: 39.5 us -> 5.67 us
  local copies, waits for them, and re-layouts: 46.3 us -> 16.3 us
  Pallas kernels: 0 us -> 24.3 us
  between operations: 16.7 us -> 1.42 us
    dot_general x34 -> x0, matrix products: 272 us -> none  [the longest x16 155 us: match_blocks(): jnp.einsum('ij,njk->nik', col_band[basis_index], spread, precision=highes...]
    all_to_all x4 -> x0, waiting for transfers between devices: 74 us -> none  [the longest x1 69.1 us: on_device(): lax.all_to_all(slot_pixels, 'patch', split_axis=0, concat_axis=0, tiled=T...]
    reduce_scatter x2 -> x0, waiting for transfers between devices: 37.6 us -> none  [the longest x1 27.7 us: on_device(): lax.psum_scatter(weight_patch, 'visit', scatter_dimension=0, tiled=True)]
    pallas_call x0 -> x3, Pallas kernels: none -> 24.3 us  [the longest x2 20.9 us: match(): pl.pallas_call(match_kernel, out_shape=(part, part), in_specs=[scalar] *...]
    ppermute x0 -> x15, starting transfers between devices: none -> 22.8 us  [the longest x6 11.9 us: over_depth(): lax.ppermute(value, 'patch', [(i, (i + 2 * shift) % owners) for i in rang...]
    all_to_all x4 -> x0, starting transfers between devices: 20.9 us -> none  [the longest x1 6.33 us: on_device(): lax.all_to_all(slot_quarter, 'patch', split_axis=0, concat_axis=0, tiled=...]
    ppermute x0 -> x15, waiting for transfers between devices: none -> 13.4 us  [the longest x6 9.92 us: over_visit(): return lax.ppermute(value, 'visit', [(i, i ^ flip) for i in range(visits)])]
    gather x7 -> x0, local copies, waits for them, and re-layouts: 12 us -> none  [the longest x1 4.43 us: on_device(): jnp.take(pixels, source, axis=0) * presence[:, None, None]]
  transfers between devices with their start and end apart: 6 -> 15, of which waited for: 4 -> 6; matrix products, arithmetic and copies ran while one was open for 53% -> 6% of each run, Pallas kernels for 0% -> 25%
where the time goes in v1:
time: 84.6 us; the launch traced here: 83.9 us
  Pallas kernels  24.3 us (29%)
  starting transfers between devices  22.8 us (27%)
  local copies, waits for them, and re-layouts  16.3 us (19%)
  waiting for transfers between devices  13.4 us (16%)
  other arithmetic  5.67 us (7%)
  between operations  1.42 us (2%)
    pallas_call x2, Pallas kernels, match(): pl.pallas_call(match_kernel, out_shape=(part, part), in_specs=[scalar] *...  20.9 us
    unnamed x42, local copies, waits for them, and re-layouts  16.2 us
    ppermute x6, starting transfers between devices, over_depth(): lax.ppermute(value, 'patch', [(i, (i + 2 * shift) % owners) for i in rang...  11.9 us
    ppermute x6, waiting for transfers between devices, over_visit(): return lax.ppermute(value, 'visit', [(i, i ^ flip) for i in range(visits)])  9.92 us
    ppermute x6, starting transfers between devices, over_visit(): return lax.ppermute(value, 'visit', [(i, i ^ flip) for i in range(visits)])  9.9 us
    ppermute x6, waiting for transfers between devices, over_depth(): lax.ppermute(value, 'patch', [(i, (i + 2 * shift) % owners) for i in rang...  3.47 us
    pallas_call x1, Pallas kernels, prepare(): pl.pallas_call(prepare_kernel, out_shape=(part, part, jax.ShapeDtypeStruc...  3.45 us
  transfers between devices with their start and end apart: 15, of which 6 were waited for; matrix products, arithmetic and copies ran while one was open for 6% of the time, Pallas kernels for 25%

profile of v1, /device:TPU:0, one launch (start us, length us, event | category | flops | bytes accessed | tf_op | source)
XLA Modules:
  0.0 83.9 jit_solution(4949509643447328619)
XLA Ops:
  0.6 0.0 copy-start.7
  0.6 0.0 copy-start.9
  0.7 0.0 copy-start.20
  1.3 0.1 stack.19.where
  1.4 1.6 %copy-done = f32[1,1,32,128,128]{4,3,2,1,0:T(8,128)S(1)} copy-done((f32[1,1,32,128,128]{4,3,2,1,0:T(8,128)S(1)}, f32[1,1,32,128,128]{4,3,2,1,0:T(8,128)}, u32[]{:S(2)}) %copy-start) | copy-done | bytes 2097176
  3.0 0.7 copy-done.4
  3.7 0.7 copy-done.5
  4.4 0.7 copy-done.6
  5.1 0.7 copy-done.8
  5.7 3.4 %shard_map.104 = (f32[2,2,4,64,256]{4,3,2,1,0:T(8,128)S(1)}, f32[2,2,4,64,256]{4,3,2,1,0:T(8,128)}, bf16[16,128,256]{2,1,0:T(8,128)(2,1)S(1)}, bf16[16,256,128]{2,1,0:T(8,128)(2,1)S(1)}) custom-call(s32[5]{0:T(128)S(1)} %stack.19.where, s32[32]{0:T(128)S(1)} %bitcast.83, s32[32]{0:T(128)S(1)} %bitcast.86, s32[1]{0:T(128)} %bitcast.77.count, ...), custom_call_target="tpu_custom_call" | custom-call | flops 10000000 | bytes 10000000 | tf_op jit(solution)/shard_map/pallas_call | solution.py:90
  9.2 1.0 %copy-done.12 = bf16[16,128,256]{2,1,0:T(8,128)(2,1)} copy-done((bf16[16,128,256]{2,1,0:T(8,128)(2,1)}, bf16[16,128,256]{2,1,0:T(8,128)(2,1)S(1)}, u32[]{:S(2)}) %copy-start.12) | copy-done | bytes 1048600
  10.2 1.0 %copy-done.15 = bf16[16,256,128]{2,1,0:T(8,128)(2,1)} copy-done((bf16[16,256,128]{2,1,0:T(8,128)(2,1)}, bf16[16,256,128]{2,1,0:T(8,128)(2,1)S(1)}, u32[]{:S(2)}) %copy-start.15) | copy-done | bytes 1048600
  11.2 0.5 collective-permute-start.8
  11.6 0.0 copy-done.7
  11.6 0.0 copy-done.9
  11.6 0.0 copy-done.20
  11.6 0.0 copy-done.1
  11.6 0.0 copy-start.10
  11.7 1.6 %copy-done.10 = f32[1,1,32,128,128]{4,3,2,1,0:T(8,128)S(1)} copy-done((f32[1,1,32,128,128]{4,3,2,1,0:T(8,128)S(1)}, f32[1,1,32,128,128]{4,3,2,1,0:T(8,128)}, u32[]{:S(2)}) %copy-start.10) | copy-done | bytes 2097176
  13.2 1.2 %copy-done.13 = bf16[16,128,256]{2,1,0:T(8,128)(2,1)S(1)} copy-done((bf16[16,128,256]{2,1,0:T(8,128)(2,1)S(1)}, bf16[16,128,256]{2,1,0:T(8,128)(2,1)}, u32[]{:S(2)}) %copy-start.13) | copy-done | bytes 1048600
  14.5 1.2 %copy-done.16 = bf16[16,256,128]{2,1,0:T(8,128)(2,1)S(1)} copy-done((bf16[16,256,128]{2,1,0:T(8,128)(2,1)S(1)}, bf16[16,256,128]{2,1,0:T(8,128)(2,1)}, u32[]{:S(2)}) %copy-start.16) | copy-done | bytes 1048600
  15.7 1.0 %copy-done.18 = f32[800,16,6]{0,1,2:T(8,128)S(1)} copy-done((f32[800,16,6]{0,1,2:T(8,128)S(1)}, f32[800,16,6]{0,1,2:T(8,128)}, u32[]{:S(2)}) %copy-start.18) | copy-done | bytes 307224
  16.7 10.8 %shard_map.105 = (f32[2,4,64,256]{3,2,1,0:T(8,128)S(1)}, f32[2,4,64,256]{3,2,1,0:T(8,128)}) custom-call(s32[1]{0:T(128)} %bitcast.first_row, s32[5]{0:T(128)S(1)} %stack.19.where, s32[32]{0:T(128)S(1)} %bitcast.84, s32[32]{0:T(128)S(1)} %bitcast.87, s32[32]{0:T(128)S(1)} %bitcast.93, s32[1]{0:T(128)} %bitcast.78.count, f32[32,128,128]{2,1,0:T(8,128)S(1)} %bitcast.89, ...), custom_call_target="tpu_custom_call" | custom-call | flops 5368709120 | bytes 10000000 | tf_op jit(solution)/shard_map/pallas_call | solution.py:199
  27.5 0.8 copy-done.2
  28.3 0.1 collective-permute-start
  28.3 1.6 %copy-done.11 = f32[1,1,32,128,128]{4,3,2,1,0:T(8,128)S(1)} copy-done((f32[1,1,32,128,128]{4,3,2,1,0:T(8,128)S(1)}, f32[1,1,32,128,128]{4,3,2,1,0:T(8,128)}, u32[]{:S(2)}) %copy-start.11) | copy-done | bytes 2097176
  29.9 1.2 %copy-done.14 = bf16[16,128,256]{2,1,0:T(8,128)(2,1)S(1)} copy-done((bf16[16,128,256]{2,1,0:T(8,128)(2,1)S(1)}, bf16[16,128,256]{2,1,0:T(8,128)(2,1)}, u32[]{:S(2)}) %copy-start.14) | copy-done | bytes 1048600
  31.2 1.2 %copy-done.17 = bf16[16,256,128]{2,1,0:T(8,128)(2,1)S(1)} copy-done((bf16[16,256,128]{2,1,0:T(8,128)(2,1)S(1)}, bf16[16,256,128]{2,1,0:T(8,128)(2,1)}, u32[]{:S(2)}) %copy-start.17) | copy-done | bytes 1048600
  32.4 10.1 %shard_map.106 = (f32[2,4,64,256]{3,2,1,0:T(8,128)S(1)}, f32[2,4,64,256]{3,2,1,0:T(8,128)S(1)}) custom-call(s32[1]{0:T(128)} %bitcast.13.first_row, s32[5]{0:T(128)S(1)} %stack.19.where, s32[32]{0:T(128)S(1)} %bitcast.85, s32[32]{0:T(128)S(1)} %bitcast.88, s32[32]{0:T(128)S(1)} %bitcast.94, s32[1]{0:T(128)} %bitcast.79.count, f32[32,128,128]{2,1,0:T(8,128)S(1)} %bitcast.90, ...), custom_call_target="tpu_custom_call" | custom-call | flops 5368709120 | bytes 10000000 | tf_op jit(solution)/shard_map/pallas_call | solution.py:199
  42.5 0.5 collective-permute-start.1
  43.0 0.0 collective-permute-done
  43.0 1.0 %fusion.8 = f32[4,64,256]{2,1,0:T(8,128)S(1)} fusion(f32[2,4,64,256]{3,2,1,0:T(8,128)} %collective-permute-done, f32[2,4,64,256]{3,2,1,0:T(8,128)S(1)} %copy-done.3), kind=kLoop, calls=%fused_computation.14 | loop fusion | flops 65536 | bytes 786432 | tf_op jit(solution)/shard_map/add | solution.py:285
  44.0 2.6 %collective-permute-start.3 = (f32[4,64,256]{2,1,0:T(8,128)S(1)}, f32[4,64,256]{2,1,0:T(8,128)S(1)}, u32[]{:S(2)}, u32[]{:S(2)}) collective-permute-start(f32[4,64,256]{2,1,0:T(8,128)S(1)} %fusion.8), channel_id=1, source_target_pairs={{0,16},{8,24},{16,0},{24,8},{1,17},{9,25},{17,1},{25,9},{2,18},{10... | collective-permute-start | bytes 786440 | tf_op jit(solution)/shard_map/ppermute | solution.py:244
  46.6 0.0 collective-permute-done.1
  46.6 0.1 fusion.9
  46.7 1.6 %collective-permute-start.2 = (f32[4,64,256]{2,1,0:T(8,128)S(1)}, f32[4,64,256]{2,1,0:T(8,128)S(1)}, u32[]{:S(2)}, u32[]{:S(2)}) collective-permute-start(f32[4,64,256]{2,1,0:T(8,128)S(1)} %get-tuple-element.21), channel_id=1, source_target_pairs={{0,8},{8,0},{16,24},{24,16},{1,9},{9,1},{17,25},{25,17},{2,10},{10... | collective-permute-start | bytes 786440 | tf_op jit(solution)/shard_map/ppermute | solution.py:244
  48.3 0.8 collective-permute-start.4
  49.0 0.0 collective-permute-done.8
  49.0 1.2 %fusion.2 = (f32[4,64,256]{2,1,0:T(8,128)S(1)}, f32[4,64,256]{2,1,0:T(8,128)S(1)}, f32[4,64,256]{2,1,0:T(8,128)S(1)}) fusion(f32[2,2,4,64,256]{4,3,2,1,0:T(8,128)} %collective-permute-done.8, f32[2,2,4,64,256]{4,3,2,1,0:T(8,128)S(1)} %get-tuple-element.16), kind=kLoop, calls=%fused_computation.5 | loop fusion | flops 196608 | bytes 2359296 | tf_op jit(solution)/shard_map/add | solution.py:262
  50.3 1.3 %collective-permute-start.10 = (f32[4,64,256]{2,1,0:T(8,128)S(1)}, f32[4,64,256]{2,1,0:T(8,128)S(1)}, u32[]{:S(2)}, u32[]{:S(2)}) collective-permute-start(f32[4,64,256]{2,1,0:T(8,128)S(1)} %get-tuple-element.20), channel_id=1, source_target_pairs={{0,16},{8,24},{16,0},{24,8},{1,17},{9,25},{17,1},{25,9},{2,18},{10... | collective-permute-start | bytes 786440 | tf_op jit(solution)/shard_map/ppermute | solution.py:244
  51.5 1.7 %collective-permute-start.11 = (f32[4,64,256]{2,1,0:T(8,128)S(1)}, f32[4,64,256]{2,1,0:T(8,128)S(1)}, u32[]{:S(2)}, u32[]{:S(2)}) collective-permute-start(f32[4,64,256]{2,1,0:T(8,128)S(1)} %get-tuple-element.19), channel_id=1, source_target_pairs={{0,24},{8,16},{16,8},{24,0},{1,25},{9,17},{17,9},{25,1},{2,26},{10... | collective-permute-start | bytes 786440 | tf_op jit(solution)/shard_map/ppermute | solution.py:244
  53.3 0.5 collective-permute-done.3
  53.8 1.9 %collective-permute-start.9 = (f32[4,64,256]{2,1,0:T(8,128)S(1)}, f32[4,64,256]{2,1,0:T(8,128)S(1)}, u32[]{:S(2)}, u32[]{:S(2)}) collective-permute-start(f32[4,64,256]{2,1,0:T(8,128)S(1)} %get-tuple-element.18), channel_id=1, source_target_pairs={{0,8},{8,0},{16,24},{24,16},{1,9},{9,1},{17,25},{25,17},{2,10},{10... | collective-permute-start | bytes 786440 | tf_op jit(solution)/shard_map/ppermute | solution.py:244
  55.7 0.2 collective-permute-done.2
  55.9 6.0 %collective-permute-done.4 = f32[4,64,256]{2,1,0:T(8,128)S(1)} collective-permute-done((f32[4,64,256]{2,1,0:T(8,128)S(1)}, f32[4,64,256]{2,1,0:T(8,128)S(1)}, u32[]{:S(2)}, u32[]{:S(2)}) %collective-permute-start.4) | collective-permute-done | bytes 262176 | tf_op jit(solution)/shard_map/ppermute | solution.py:244
  61.9 1.0 %fusion.13 = f32[4,64,256]{2,1,0:T(8,128)S(1)} fusion(f32[4,64,256]{2,1,0:T(8,128)S(1)} %collective-permute-done.4, f32[4,64,256]{2,1,0:T(8,128)S(1)} %collective-permute-done.3, f32[4,64,256]{2,1,0:T(8,128)S(1)} %collective-permute-done.2, f32[2,4,64,256]{3,2,1,0:T(8,128)} %collective-permute-done, f32[2,4,64,256]{3,2,1,0:T(8,128)S(1)} %copy-done.3), kind=kLoop, calls=%fused_computation.21 | loop fusion | flops 262144 | bytes 1572864 | tf_op jit(solution)/shard_map/add | solution.py:287
  63.0 1.6 %collective-permute-start.5 = (f32[64,256]{1,0:T(8,128)S(1)}, f32[64,256]{1,0:T(8,128)S(1)}, u32[]{:S(2)}, u32[]{:S(2)}) collective-permute-start(f32[64,256]{1,0:T(8,128)S(1)} %get-tuple-element.26), channel_id=1, source_target_pairs={{0,2},{1,3},{2,4},{3,5},{4,6},{5,7},{6,0},{7,1},{8,10},{9,11},{10,... | collective-permute-start | bytes 196616 | tf_op jit(solution)/shard_map/ppermute | solution.py:247
  64.6 2.6 %collective-permute-start.6 = (f32[64,256]{1,0:T(8,128)S(1)}, f32[64,256]{1,0:T(8,128)S(1)}, u32[]{:S(2)}, u32[]{:S(2)}) collective-permute-start(f32[64,256]{1,0:T(8,128)S(1)} %get-tuple-element.28), channel_id=1, source_target_pairs={{0,4},{1,5},{2,6},{3,7},{4,0},{5,1},{6,2},{7,3},{8,12},{9,13},{10,... | collective-permute-start | bytes 196616 | tf_op jit(solution)/shard_map/ppermute | solution.py:247
  67.2 3.2 %collective-permute-done.10 = f32[4,64,256]{2,1,0:T(8,128)S(1)} collective-permute-done((f32[4,64,256]{2,1,0:T(8,128)S(1)}, f32[4,64,256]{2,1,0:T(8,128)S(1)}, u32[]{:S(2)}, u32[]{:S(2)}) %collective-permute-start.10) | collective-permute-done | bytes 262176 | tf_op jit(solution)/shard_map/ppermute | solution.py:244
  70.4 3.8 %collective-permute-start.7 = (f32[64,256]{1,0:T(8,128)S(1)}, f32[64,256]{1,0:T(8,128)S(1)}, u32[]{:S(2)}, u32[]{:S(2)}) collective-permute-start(f32[64,256]{1,0:T(8,128)S(1)} %get-tuple-element.27), channel_id=1, source_target_pairs={{0,6},{1,7},{2,0},{3,1},{4,2},{5,3},{6,4},{7,5},{8,14},{9,15},{10,... | collective-permute-start | bytes 196616 | tf_op jit(solution)/shard_map/ppermute | solution.py:247
  74.2 0.0 collective-permute-done.11
  74.2 0.0 collective-permute-done.9
  74.2 1.0 %fusion.6 = f32[4,64,256]{2,1,0:T(8,128)S(1)} fusion(f32[4,64,256]{2,1,0:T(8,128)S(1)} %collective-permute-done.11, f32[4,64,256]{2,1,0:T(8,128)S(1)} %collective-permute-done.10, f32[4,64,256]{2,1,0:T(8,128)S(1)} %collective-permute-done.9, f32[2,2,4,64,256]{4,3,2,1,0:T(8,128)} %collective-permute-done.8, f32[2,2,4,64,256]{4,3,2,1,0:T(8,128)S(1)} %get-tuple-element.16), kind=kLoop, calls=%fused_computation.10 | loop fusion | flops 262144 | bytes 1572864 | tf_op jit(solution)/shard_map/add | solution.py:264
  75.3 0.1 collective-permute-start.12
  75.4 2.0 %collective-permute-start.13 = (f32[64,256]{1,0:T(8,128)S(1)}, f32[64,256]{1,0:T(8,128)S(1)}, u32[]{:S(2)}, u32[]{:S(2)}) collective-permute-start(f32[64,256]{1,0:T(8,128)S(1)} %get-tuple-element.25), channel_id=1, source_target_pairs={{0,4},{1,5},{2,6},{3,7},{4,0},{5,1},{6,2},{7,3},{8,12},{9,13},{10,... | collective-permute-start | bytes 196616 | tf_op jit(solution)/shard_map/ppermute | solution.py:247
  77.4 0.0 collective-permute-done.5
  77.4 1.8 %collective-permute-start.14 = (f32[64,256]{1,0:T(8,128)S(1)}, f32[64,256]{1,0:T(8,128)S(1)}, u32[]{:S(2)}, u32[]{:S(2)}) collective-permute-start(f32[64,256]{1,0:T(8,128)S(1)} %get-tuple-element.24), channel_id=1, source_target_pairs={{0,6},{1,7},{2,0},{3,1},{4,2},{5,3},{6,4},{7,5},{8,14},{9,15},{10,... | collective-permute-start | bytes 196616 | tf_op jit(solution)/shard_map/ppermute | solution.py:247
  79.2 0.0 collective-permute-done.6
  79.2 0.0 collective-permute-done.7
  79.2 0.6 fusion.21
  79.8 2.1 %collective-permute-done.12 = f32[64,256]{1,0:T(8,128)S(1)} collective-permute-done((f32[64,256]{1,0:T(8,128)S(1)}, f32[64,256]{1,0:T(8,128)S(1)}, u32[]{:S(2)}, u32[]{:S(2)}) %collective-permute-start.12) | collective-permute-done | bytes 65568 | tf_op jit(solution)/shard_map/ppermute | solution.py:247
  82.0 1.3 %collective-permute-done.13 = f32[64,256]{1,0:T(8,128)S(1)} collective-permute-done((f32[64,256]{1,0:T(8,128)S(1)}, f32[64,256]{1,0:T(8,128)S(1)}, u32[]{:S(2)}, u32[]{:S(2)}) %collective-permute-start.13) | collective-permute-done | bytes 65568 | tf_op jit(solution)/shard_map/ppermute | solution.py:247
  83.3 0.0 collective-permute-done.14
  83.3 0.6 fusion.17
  (21 shorter events, 0.1 us)
Async XLA Ops:
  0.6 11.0 %copy-start.7 = (s32[1,1,32]{2,1,0:T(1,128)S(1)}, s32[1,1,32]{2,1,0:T(1,128)}, u32[]{:S(2)}) copy-start(s32[1,1,32]{2,1,0:T(1,128)} %param.11) | copy-start | bytes 388
  0.6 11.0 %copy-start.9 = (s32[1,1,32]{2,1,0:T(1,128)S(1)}, s32[1,1,32]{2,1,0:T(1,128)}, u32[]{:S(2)}) copy-start(s32[1,1,32]{2,1,0:T(1,128)} %param.12) | copy-start | bytes 388
  0.7 11.0 %copy-start.20 = (s32[1,1,32]{2,1,0:T(1,128)S(1)}, s32[1,1,32]{2,1,0:T(1,128)}, u32[]{:S(2)}) copy-start(s32[1,1,32]{2,1,0:T(1,128)} %param.13) | copy-start | bytes 388
  1.4 1.6 %copy-start = (f32[1,1,32,128,128]{4,3,2,1,0:T(8,128)S(1)}, f32[1,1,32,128,128]{4,3,2,1,0:T(8,128)}, u32[]{:S(2)}) copy-start(f32[1,1,32,128,128]{4,3,2,1,0:T(8,128)} %param.10) | copy-start | bytes 6291460
  3.0 0.7 copy-start.4
  3.7 0.7 copy-start.5
  4.4 0.7 copy-start.6
  5.1 0.7 copy-start.8
  5.7 5.9 %copy-start.1 = (f32[1,1,32,128,128]{4,3,2,1,0:T(8,128)S(1)}, f32[1,1,32,128,128]{4,3,2,1,0:T(8,128)}, u32[]{:S(2)}) copy-start(f32[1,1,32,128,128]{4,3,2,1,0:T(8,128)} %param.10) | copy-start | bytes 6291460
  9.2 1.0 %copy-start.12 = (bf16[16,128,256]{2,1,0:T(8,128)(2,1)}, bf16[16,128,256]{2,1,0:T(8,128)(2,1)S(1)}, u32[]{:S(2)}) copy-start(bf16[16,128,256]{2,1,0:T(8,128)(2,1)S(1)} %get-tuple-element.10.col_band) | copy-start | bytes 3145732
  10.2 1.0 %copy-start.15 = (bf16[16,256,128]{2,1,0:T(8,128)(2,1)}, bf16[16,256,128]{2,1,0:T(8,128)(2,1)S(1)}, u32[]{:S(2)}) copy-start(bf16[16,256,128]{2,1,0:T(8,128)(2,1)S(1)} %get-tuple-element.11.row_band) | copy-start | bytes 3145732
  11.2 37.9 %collective-permute-start.8 = (f32[2,2,4,64,256]{4,3,2,1,0:T(8,128)}, f32[2,2,4,64,256]{4,3,2,1,0:T(8,128)}, u32[]{:S(2)}, u32[]{:S(2)}) collective-permute-start(f32[2,2,4,64,256]{4,3,2,1,0:T(8,128)} %get-tuple-element.17), channel_id=1, source_target_pairs={{0,1},{1,0},{2,3},{3,2},{4,5},{5,4},{6,7},{7,6},{8,9},{9,8},{10,11... | collective-permute-start | bytes 3145736 | tf_op jit(solution)/shard_map/ppermute | solution.py:241
  11.6 1.6 %copy-start.10 = (f32[1,1,32,128,128]{4,3,2,1,0:T(8,128)S(1)}, f32[1,1,32,128,128]{4,3,2,1,0:T(8,128)}, u32[]{:S(2)}) copy-start(f32[1,1,32,128,128]{4,3,2,1,0:T(8,128)} %param.9) | copy-start | bytes 6291460
  13.2 1.2 %copy-start.13 = (bf16[16,128,256]{2,1,0:T(8,128)(2,1)S(1)}, bf16[16,128,256]{2,1,0:T(8,128)(2,1)}, u32[]{:S(2)}) copy-start(bf16[16,128,256]{2,1,0:T(8,128)(2,1)} %copy-done.12) | copy-start | bytes 3145732
  14.5 1.2 %copy-start.16 = (bf16[16,256,128]{2,1,0:T(8,128)(2,1)S(1)}, bf16[16,256,128]{2,1,0:T(8,128)(2,1)}, u32[]{:S(2)}) copy-start(bf16[16,256,128]{2,1,0:T(8,128)(2,1)} %copy-done.15) | copy-start | bytes 3145732
  15.7 1.0 %copy-start.18 = (f32[800,16,6]{0,1,2:T(8,128)S(1)}, f32[800,16,6]{0,1,2:T(8,128)}, u32[]{:S(2)}) copy-start(f32[800,16,6]{0,1,2:T(8,128)} %param.15) | copy-start | bytes 921604
  16.7 11.7 %copy-start.19 = (f32[800,16,6]{0,1,2:T(8,128)S(1)}, f32[800,16,6]{0,1,2:T(8,128)}, u32[]{:S(2)}) copy-start(f32[800,16,6]{0,1,2:T(8,128)} %param.15) | copy-start | bytes 921604
  27.5 0.8 copy-start.2
  28.3 14.7 %collective-permute-start = (f32[2,4,64,256]{3,2,1,0:T(8,128)}, f32[2,4,64,256]{3,2,1,0:T(8,128)}, u32[]{:S(2)}, u32[]{:S(2)}) collective-permute-start(f32[2,4,64,256]{3,2,1,0:T(8,128)} %get-tuple-element.13), channel_id=1, source_target_pairs={{0,1},{1,0},{2,3},{3,2},{4,5},{5,4},{6,7},{7,6},{8,9},{9,8},{10,11... | collective-permute-start | bytes 1572872 | tf_op jit(solution)/shard_map/ppermute | solution.py:241
  28.3 1.6 %copy-start.11 = (f32[1,1,32,128,128]{4,3,2,1,0:T(8,128)S(1)}, f32[1,1,32,128,128]{4,3,2,1,0:T(8,128)}, u32[]{:S(2)}) copy-start(f32[1,1,32,128,128]{4,3,2,1,0:T(8,128)} %param.9) | copy-start | bytes 6291460
  29.9 1.2 %copy-start.14 = (bf16[16,128,256]{2,1,0:T(8,128)(2,1)S(1)}, bf16[16,128,256]{2,1,0:T(8,128)(2,1)}, u32[]{:S(2)}) copy-start(bf16[16,128,256]{2,1,0:T(8,128)(2,1)} %copy-done.12) | copy-start | bytes 3145732
  31.2 1.2 %copy-start.17 = (bf16[16,256,128]{2,1,0:T(8,128)(2,1)S(1)}, bf16[16,256,128]{2,1,0:T(8,128)(2,1)}, u32[]{:S(2)}) copy-start(bf16[16,256,128]{2,1,0:T(8,128)(2,1)} %copy-done.15) | copy-start | bytes 3145732
  32.4 10.6 %copy-start.3 = (f32[2,4,64,256]{3,2,1,0:T(8,128)S(1)}, f32[2,4,64,256]{3,2,1,0:T(8,128)}, u32[]{:S(2)}) copy-start(f32[2,4,64,256]{3,2,1,0:T(8,128)} %copy-done.2) | copy-start | bytes 1572868
  42.5 4.1 %collective-permute-start.1 = (f32[2,4,64,256]{3,2,1,0:T(8,128)S(1)}, f32[2,4,64,256]{3,2,1,0:T(8,128)S(1)}, u32[]{:S(2)}, u32[]{:S(2)}) collective-permute-start(f32[2,4,64,256]{3,2,1,0:T(8,128)S(1)} %get-tuple-element.15), channel_id=1, source_target_pairs={{0,1},{1,0},{2,3},{3,2},{4,5},{5,4},{6,7},{7,6},{8,9},{9,8},{10,11... | collective-permute-start | bytes 1572872 | tf_op jit(solution)/shard_map/ppermute | solution.py:241
  44.0 9.8 %collective-permute-start.3 = (f32[4,64,256]{2,1,0:T(8,128)S(1)}, f32[4,64,256]{2,1,0:T(8,128)S(1)}, u32[]{:S(2)}, u32[]{:S(2)}) collective-permute-start(f32[4,64,256]{2,1,0:T(8,128)S(1)} %fusion.8), channel_id=1, source_target_pairs={{0,16},{8,24},{16,0},{24,8},{1,17},{9,25},{17,1},{25,9},{2,18},{10... | collective-permute-start | bytes 786440 | tf_op jit(solution)/shard_map/ppermute | solution.py:244
  46.7 9.2 %collective-permute-start.2 = (f32[4,64,256]{2,1,0:T(8,128)S(1)}, f32[4,64,256]{2,1,0:T(8,128)S(1)}, u32[]{:S(2)}, u32[]{:S(2)}) collective-permute-start(f32[4,64,256]{2,1,0:T(8,128)S(1)} %get-tuple-element.21), channel_id=1, source_target_pairs={{0,8},{8,0},{16,24},{24,16},{1,9},{9,1},{17,25},{25,17},{2,10},{10... | collective-permute-start | bytes 786440 | tf_op jit(solution)/shard_map/ppermute | solution.py:244
  48.3 13.6 %collective-permute-start.4 = (f32[4,64,256]{2,1,0:T(8,128)S(1)}, f32[4,64,256]{2,1,0:T(8,128)S(1)}, u32[]{:S(2)}, u32[]{:S(2)}) collective-permute-start(f32[4,64,256]{2,1,0:T(8,128)S(1)} %get-tuple-element.22), channel_id=1, source_target_pairs={{0,24},{8,16},{16,8},{24,0},{1,25},{9,17},{17,9},{25,1},{2,26},{10... | collective-permute-start | bytes 786440 | tf_op jit(solution)/shard_map/ppermute | solution.py:244
  50.3 20.1 %collective-permute-start.10 = (f32[4,64,256]{2,1,0:T(8,128)S(1)}, f32[4,64,256]{2,1,0:T(8,128)S(1)}, u32[]{:S(2)}, u32[]{:S(2)}) collective-permute-start(f32[4,64,256]{2,1,0:T(8,128)S(1)} %get-tuple-element.20), channel_id=1, source_target_pairs={{0,16},{8,24},{16,0},{24,8},{1,17},{9,25},{17,1},{25,9},{2,18},{10... | collective-permute-start | bytes 786440 | tf_op jit(solution)/shard_map/ppermute | solution.py:244
  51.5 22.7 %collective-permute-start.11 = (f32[4,64,256]{2,1,0:T(8,128)S(1)}, f32[4,64,256]{2,1,0:T(8,128)S(1)}, u32[]{:S(2)}, u32[]{:S(2)}) collective-permute-start(f32[4,64,256]{2,1,0:T(8,128)S(1)} %get-tuple-element.19), channel_id=1, source_target_pairs={{0,24},{8,16},{16,8},{24,0},{1,25},{9,17},{17,9},{25,1},{2,26},{10... | collective-permute-start | bytes 786440 | tf_op jit(solution)/shard_map/ppermute | solution.py:244
  53.8 20.5 %collective-permute-start.9 = (f32[4,64,256]{2,1,0:T(8,128)S(1)}, f32[4,64,256]{2,1,0:T(8,128)S(1)}, u32[]{:S(2)}, u32[]{:S(2)}) collective-permute-start(f32[4,64,256]{2,1,0:T(8,128)S(1)} %get-tuple-element.18), channel_id=1, source_target_pairs={{0,8},{8,0},{16,24},{24,16},{1,9},{9,1},{17,25},{25,17},{2,10},{10... | collective-permute-start | bytes 786440 | tf_op jit(solution)/shard_map/ppermute | solution.py:244
  63.0 14.4 %collective-permute-start.5 = (f32[64,256]{1,0:T(8,128)S(1)}, f32[64,256]{1,0:T(8,128)S(1)}, u32[]{:S(2)}, u32[]{:S(2)}) collective-permute-start(f32[64,256]{1,0:T(8,128)S(1)} %get-tuple-element.26), channel_id=1, source_target_pairs={{0,2},{1,3},{2,4},{3,5},{4,6},{5,7},{6,0},{7,1},{8,10},{9,11},{10,... | collective-permute-start | bytes 196616 | tf_op jit(solution)/shard_map/ppermute | solution.py:247
  64.6 14.6 %collective-permute-start.6 = (f32[64,256]{1,0:T(8,128)S(1)}, f32[64,256]{1,0:T(8,128)S(1)}, u32[]{:S(2)}, u32[]{:S(2)}) collective-permute-start(f32[64,256]{1,0:T(8,128)S(1)} %get-tuple-element.28), channel_id=1, source_target_pairs={{0,4},{1,5},{2,6},{3,7},{4,0},{5,1},{6,2},{7,3},{8,12},{9,13},{10,... | collective-permute-start | bytes 196616 | tf_op jit(solution)/shard_map/ppermute | solution.py:247
  70.4 8.8 %collective-permute-start.7 = (f32[64,256]{1,0:T(8,128)S(1)}, f32[64,256]{1,0:T(8,128)S(1)}, u32[]{:S(2)}, u32[]{:S(2)}) collective-permute-start(f32[64,256]{1,0:T(8,128)S(1)} %get-tuple-element.27), channel_id=1, source_target_pairs={{0,6},{1,7},{2,0},{3,1},{4,2},{5,3},{6,4},{7,5},{8,14},{9,15},{10,... | collective-permute-start | bytes 196616 | tf_op jit(solution)/shard_map/ppermute | solution.py:247
  75.3 6.7 %collective-permute-start.12 = (f32[64,256]{1,0:T(8,128)S(1)}, f32[64,256]{1,0:T(8,128)S(1)}, u32[]{:S(2)}, u32[]{:S(2)}) collective-permute-start(f32[64,256]{1,0:T(8,128)S(1)} %get-tuple-element.23), channel_id=1, source_target_pairs={{0,2},{1,3},{2,4},{3,5},{4,6},{5,7},{6,0},{7,1},{8,10},{9,11},{10,... | collective-permute-start | bytes 196616 | tf_op jit(solution)/shard_map/ppermute | solution.py:247
  75.4 7.9 %collective-permute-start.13 = (f32[64,256]{1,0:T(8,128)S(1)}, f32[64,256]{1,0:T(8,128)S(1)}, u32[]{:S(2)}, u32[]{:S(2)}) collective-permute-start(f32[64,256]{1,0:T(8,128)S(1)} %get-tuple-element.25), channel_id=1, source_target_pairs={{0,4},{1,5},{2,6},{3,7},{4,0},{5,1},{6,2},{7,3},{8,12},{9,13},{10,... | collective-permute-start | bytes 196616 | tf_op jit(solution)/shard_map/ppermute | solution.py:247
  77.4 5.9 %collective-permute-start.14 = (f32[64,256]{1,0:T(8,128)S(1)}, f32[64,256]{1,0:T(8,128)S(1)}, u32[]{:S(2)}, u32[]{:S(2)}) collective-permute-start(f32[64,256]{1,0:T(8,128)S(1)} %get-tuple-element.24), channel_id=1, source_target_pairs={{0,6},{1,7},{2,0},{3,1},{4,2},{5,3},{6,4},{7,5},{8,14},{9,15},{10,... | collective-permute-start | bytes 196616 | tf_op jit(solution)/shard_map/ppermute | solution.py:247

commit v2 on v1

v2 whole, which is shorter than its diff:
```python
import functools

import jax
import jax.numpy as jnp
from jax import lax
from jax.experimental import pallas as pl
from jax.experimental.pallas import tpu as pltpu
from jax.sharding import PartitionSpec as P

f32 = jnp.float32
bf16 = jnp.bfloat16

SHARE = 1.0 / 32.0
KEEP = 1.0 - SHARE
VMEM_BYTES = 40 * 2**20
GROUP_ROWS = 256


def split_left(value):
    first = value.astype(bf16)
    return first, (value - KEEP * first.astype(f32)).astype(bf16)


def split_right(value):
    first = (KEEP * value).astype(bf16)
    return first, ((value - first.astype(f32)) * (1.0 / SHARE)).astype(bf16)


def relative(depth, own, depths):
    if depths & (depths - 1) == 0:
        return depth ^ own
    return lax.rem(depth - own + depths, depths)


def my_place(depths):
    patch_at = lax.axis_index("patch")
    visit_at = lax.axis_index("visit")
    return lax.rem(patch_at, 2), patch_at // 2, depths, visit_at // 2, lax.rem(visit_at, 2)


def place_of(where, target, quarter):
    core = lax.rem(target, 2) ^ where[0]
    depth = relative(target // 2, where[1], where[2])
    return core, depth, (quarter // 2) ^ where[3], lax.rem(quarter, 2)


def start_all(copies):
    for copy in copies:
        copy.start()


def wait_all(copies):
    for copy in copies:
        copy.wait()


def weight_kernel(
    targets_in, quarters_in, count_in, variance_in, keep_out, send_out,
    targets, quarters, count, variance, canvas, scalar_done, block_done, out_done,
):
    blocks, side, _ = variance.shape
    half = side // 2
    chunks = block_done.shape[0]
    size = blocks // chunks
    scalars = [
        pltpu.make_async_copy(a, b, scalar_done.at[i])
        for i, (a, b) in enumerate(
            [(targets_in, targets), (quarters_in, quarters), (count_in, count)]
        )
    ]
    arrays = [
        pltpu.make_async_copy(
            variance_in.at[pl.ds(i * size, size)],
            variance.at[pl.ds(i * size, size)],
            block_done.at[i],
        )
        for i in range(chunks)
    ]
    start_all(scalars)
    start_all(arrays)
    canvas[...] = jnp.zeros_like(canvas)
    where = my_place(canvas.shape[4])
    wait_all(scalars)

    def add_block(n, carry):
        live = jnp.where(n < count[0], 1.0, 0.0).astype(f32)
        inverse = live / variance[n]
        core, depth, down, across = place_of(where, targets[n], quarters[n])
        column = pl.ds(pl.multiple_of(across * side, side), side)
        for part in range(2):
            canvas[core, part ^ where[4], down, 0, depth, :, column] += inverse[
                part * half : (part + 1) * half
            ]
        return carry

    for i in range(chunks):
        arrays[i].wait()
        lax.fori_loop(i * size, (i + 1) * size, add_block, 0, unroll=2)
    outs = [
        pltpu.make_async_copy(canvas.at[1, :, :, 0], send_out, out_done.at[0]),
        pltpu.make_async_copy(canvas.at[0, :, :, 0], keep_out, out_done.at[1]),
    ]
    start_all(outs)
    wait_all(outs)


def sum_weights(targets, quarters, count, variance, depths):
    blocks, side, _ = variance.shape
    half = side // 2
    part = jax.ShapeDtypeStruct((2, 2, depths, half, 2 * side), f32)
    anywhere = pl.BlockSpec(memory_space=pltpu.HBM)
    return pl.pallas_call(
        weight_kernel,
        out_shape=(part, part),
        in_specs=[anywhere] * 4,
        out_specs=[anywhere] * 2,
        scratch_shapes=[
            pltpu.SMEM(targets.shape, jnp.int32),
            pltpu.SMEM(quarters.shape, jnp.int32),
            pltpu.SMEM(count.shape, jnp.int32),
            pltpu.VMEM(variance.shape, f32),
            pltpu.VMEM((2, 2, 2, 1, depths, half, 2 * side), f32),
            pltpu.SemaphoreType.DMA((3,)),
            pltpu.SemaphoreType.DMA((4,)),
            pltpu.SemaphoreType.DMA((2,)),
        ],
        compiler_params=pltpu.CompilerParams(vmem_limit_bytes=62 * 2**20),
        cost_estimate=pl.CostEstimate(flops=10**9, bytes_accessed=0, transcendentals=0),
    )(targets, quarters, count, variance)


def band_kernel(
    row_taps_in, col_taps_in, col_out, row_out, row_padded, col_padded, col_band, row_band, done
):
    nbasis, taps = row_taps_in.shape
    side = row_padded.shape[1]
    radius = (taps - 1) // 2
    row_padded[...] = jnp.zeros_like(row_padded)
    col_padded[...] = jnp.zeros_like(col_padded)
    row_padded[:, :taps] = row_taps_in[...]
    col_padded[:, :taps] = col_taps_in[...]
    row = lax.broadcasted_iota(jnp.int32, (side, side), 0)
    column = lax.broadcasted_iota(jnp.int32, (side, side), 1)
    near = jnp.abs(row - column) <= radius
    row_placed = pltpu.roll(row_padded[...], side - radius, 1)
    turn = (lax.rem(column - radius + row + side, side) == 0).astype(f32)
    col_placed = jnp.dot(
        col_padded[...], turn, precision=lax.Precision.HIGHEST, preferred_element_type=f32
    )
    for k in range(nbasis):
        base = jnp.broadcast_to(col_placed[k : k + 1], (side, side))
        band = jnp.where(near, pltpu.roll(base, 0, 1, stride=1, stride_axis=0), 0.0)
        first, second = split_left(band)
        col_band[k, :, :side] = first
        col_band[k, :, side:] = second
    col_copy = pltpu.make_async_copy(col_band, col_out, done.at[0])
    col_copy.start()
    for k in range(nbasis):
        base = jnp.broadcast_to(row_placed[k : k + 1], (side, side))
        band = jnp.where(near, pltpu.roll(base, 0, 1, stride=1, stride_axis=0), 0.0)
        first, second = split_right(band)
        row_band[k, :side, :] = first
        row_band[k, side:, :] = second
    row_copy = pltpu.make_async_copy(row_band, row_out, done.at[1])
    row_copy.start()
    col_copy.wait()
    row_copy.wait()


def make_bands(row_taps, col_taps, side):
    nbasis, taps = row_taps.shape
    anywhere = pl.BlockSpec(memory_space=pltpu.HBM)
    col_shape, row_shape = (nbasis, side, 2 * side), (nbasis, 2 * side, side)
    tap_block = pl.BlockSpec((nbasis, taps), lambda i: (0, 0))
    return pl.pallas_call(
        band_kernel,
        grid=(1,),
        out_shape=(
            jax.ShapeDtypeStruct(col_shape, bf16),
            jax.ShapeDtypeStruct(row_shape, bf16),
        ),
        in_specs=[tap_block] * 2,
        out_specs=[anywhere] * 2,
        scratch_shapes=[
            pltpu.VMEM((nbasis, side), f32),
            pltpu.VMEM((nbasis, side), f32),
            pltpu.VMEM(col_shape, bf16),
            pltpu.VMEM(row_shape, bf16),
            pltpu.SemaphoreType.DMA((2,)),
        ],
        compiler_params=pltpu.CompilerParams(vmem_limit_bytes=VMEM_BYTES),
        cost_estimate=pl.CostEstimate(flops=10**9, bytes_accessed=0, transcendentals=0),
    )(row_taps, col_taps)


def match_kernel(
    offset, targets_in, quarters_in, rows_in, count_in, pixels_in, variance_in, table_in,
    col_in, row_in, keep_out, send_out,
    targets, quarters, table_rows, count, pixels, variance, table, col_band, row_band, canvas,
    total, coefficients, scalar_done, array_done, pixel_done, variance_done, out_done,
):
    blocks, side, _ = pixels.shape
    nbasis, rows, _ = col_band.shape
    group = total.shape[0]
    far, start = offset
    where = my_place(canvas.shape[2])
    top = pl.multiple_of((where[4] ^ far) * (side // 2) + start, rows)
    scalars = [
        pltpu.make_async_copy(a, b, scalar_done.at[i])
        for i, (a, b) in enumerate(
            [(targets_in, targets), (quarters_in, quarters), (rows_in, table_rows),
             (count_in, count)]
        )
    ]
    copy_col = pltpu.make_async_copy(col_in.at[:, pl.ds(top, rows)], col_band, array_done.at[0])
    copy_row = pltpu.make_async_copy(row_in, row_band, array_done.at[1])
    copy_table = pltpu.make_async_copy(table_in, table, array_done.at[2])

    def pixel_copy(j):
        at = pl.ds(j * group, group)
        return pltpu.make_async_copy(pixels_in.at[at], pixels.at[at], pixel_done.at[j])

    def variance_copy(j):
        at = pl.ds(j * group, group)
        return pltpu.make_async_copy(
            variance_in.at[at, pl.ds(top, rows)], variance.at[at], variance_done.at[j]
        )

    start_all(scalars)
    copy_table.start()
    copy_col.start()
    pixel_copy(0).start()
    copy_row.start()
    variance_copy(0).start()
    for j in range(1, blocks // group):
        pixel_copy(j).start()
        variance_copy(j).start()
    canvas[...] = jnp.zeros_like(canvas)
    entries = table.shape[2]
    copy_table.wait()
    coefficients[:, :, :entries] = table[...]
    lane = lax.broadcasted_iota(jnp.int32, (1, side), 1).astype(f32)
    sub = lax.broadcasted_iota(jnp.int32, (8, side), 0).astype(f32)
    step = 8.0 / side
    wait_all(scalars)
    copy_col.wait()
    copy_row.wait()

    def add_group(j, carry):
        pixel_copy(j).wait()
        variance_copy(j).wait()
        terms = []
        for member in range(group):
            n = group * j + member
            quarter = quarters[n]
            across = (lane + 0.5) / side - 1.0 + lax.rem(quarter, 2).astype(f32)
            down = (sub + 0.5 + top.astype(f32)) / side - 1.0 + (quarter // 2).astype(f32)
            entry = table_rows[n]
            chunk = coefficients[:, :, pl.ds(pl.multiple_of((entry // 128) * 128, 128), 128)]
            chunk = chunk.reshape(-1, 128)
            chunk = pltpu.roll(chunk, lax.rem(128 - lax.rem(entry, 128), 128), 1)
            poly = jnp.broadcast_to(chunk[:, :1], (chunk.shape[0], side))
            poly = [poly[i * nbasis : (i + 1) * nbasis] for i in range(chunk.shape[0] // nbasis)]
            constant = poly[0] + across * (poly[1] + across * poly[3])
            linear = poly[2] + across * poly[4]
            terms.append((constant, linear, poly[5], down))
        left = col_band[...].reshape(nbasis * rows, 2 * side)
        halves = []
        for pair in range(group // 2):
            n = group * j + 2 * pair
            both = jnp.concatenate([pixels[n], pixels[n + 1]], axis=1)
            right = jnp.concatenate(split_right(both), axis=0)
            convolved = jnp.dot(left, right, preferred_element_type=f32)
            halves.append(split_left(convolved))
        for k in range(nbasis):
            at = slice(k * rows, (k + 1) * rows)
            stacked = []
            for member in range(group):
                first, second = halves[member // 2]
                lanes = slice((member % 2) * side, (member % 2 + 1) * side)
                stacked.append(jnp.concatenate([first[at, lanes], second[at, lanes]], axis=1))
            spread = jnp.dot(
                jnp.concatenate(stacked, axis=0), row_band[k], preferred_element_type=f32
            )
            for member in range(group):
                constant, linear, square, down = terms[member]
                b, d = linear[k : k + 1], square[k : k + 1]
                weight = constant[k : k + 1] + down * (b + down * d)
                change = step * b + d * (2.0 * step * down + step * step)
                second_change = (2.0 * step * step) * d
                for i in range(rows // 8):
                    value = weight * spread[member * rows + 8 * i : member * rows + 8 * i + 8]
                    if k == 0:
                        total[member, 8 * i : 8 * i + 8] = value
                    else:
                        total[member, 8 * i : 8 * i + 8] += value
                    if i < rows // 8 - 1:
                        weight = weight + change
                        change = change + second_change
        for member in range(group):
            n = group * j + member
            live = jnp.where(n < count[0], 1.0, 0.0).astype(f32)
            core, depth, down, across = place_of(where, targets[n], quarters[n])
            column = pl.ds(pl.multiple_of(across * side, side), side)
            canvas[core, down, depth, :, column] += (live / variance[n]) * total[member]
        return carry

    lax.fori_loop(0, blocks // group, add_group, 0)
    outs = [
        pltpu.make_async_copy(canvas.at[1], send_out, out_done.at[0]),
        pltpu.make_async_copy(canvas.at[0], keep_out, out_done.at[1]),
    ]
    start_all(outs)
    wait_all(outs)


def match(
    offset, rows, targets, quarters, table_rows, count, pixels, variance, table,
    col_band, row_band, depths,
):
    blocks, side, _ = pixels.shape
    nbasis = col_band.shape[0]
    group = min(blocks, GROUP_ROWS // rows)
    part = jax.ShapeDtypeStruct((2, depths, rows, 2 * side), f32)
    anywhere = pl.BlockSpec(memory_space=pltpu.HBM)
    entries = -(-table.shape[2] // 128) * 128
    scalars = (targets, quarters, table_rows, count)
    return pl.pallas_call(
        functools.partial(match_kernel, offset),
        out_shape=(part, part),
        in_specs=[anywhere] * 9,
        out_specs=[anywhere] * 2,
        scratch_shapes=[pltpu.SMEM(a.shape, jnp.int32) for a in scalars]
        + [
            pltpu.VMEM(pixels.shape, f32),
            pltpu.VMEM((blocks, rows, side), f32),
            pltpu.VMEM(table.shape, f32),
            pltpu.VMEM((nbasis, rows, 2 * side), bf16),
            pltpu.VMEM(row_band.shape, bf16),
            pltpu.VMEM((2, 2, depths, rows, 2 * side), f32),
            pltpu.VMEM((group, rows, side), f32),
            pltpu.VMEM(table.shape[:2] + (entries,), f32),
            pltpu.SemaphoreType.DMA((4,)),
            pltpu.SemaphoreType.DMA((3,)),
            pltpu.SemaphoreType.DMA((blocks // group,)),
            pltpu.SemaphoreType.DMA((blocks // group,)),
            pltpu.SemaphoreType.DMA((2,)),
        ],
        compiler_params=pltpu.CompilerParams(vmem_limit_bytes=VMEM_BYTES),
        cost_estimate=pl.CostEstimate(
            flops=blocks * rows * side * 40960, bytes_accessed=10**7, transcendentals=0
        ),
    )(*scalars, pixels, variance, table, col_band, row_band)


def on_device(
    image, variance, dest_patch, quadrant, coef_index, block_count, coef_table, row_taps, col_taps
):
    pixels = image[0, 0]
    variances = variance[0, 0]
    targets = dest_patch[0, 0]
    quarters = quadrant[0, 0]
    table_rows = coef_index[0, 0]
    count = block_count[0]
    owners = lax.axis_size("patch")
    visits = lax.axis_size("visit")
    depths = owners // 2
    side = pixels.shape[1]
    half = side // 2
    table = jnp.transpose(coef_table, (2, 1, 0))
    together = lax.optimization_barrier

    def over_core(value):
        return lax.ppermute(value, "patch", [(i, i ^ 1) for i in range(owners)])

    def over_visit(value, flip):
        return lax.ppermute(value, "visit", [(i, i ^ flip) for i in range(visits)])

    def over_depth(value, shift):
        if depths & (depths - 1) == 0:
            pairs = [(i, i ^ (2 * shift)) for i in range(owners)]
        else:
            pairs = [(i, (i + 2 * shift) % owners) for i in range(owners)]
        return lax.ppermute(value, "patch", pairs)

    def pieces_of(value):
        return [over_depth(value[s], s) for s in range(1, depths)]

    def run(offset, rows, bands):
        return match(
            offset, rows, targets, quarters, table_rows, count, pixels, variances,
            table, bands[0], bands[1], depths,
        )

    keep, send = sum_weights(targets, quarters, count, variances, depths)
    got = over_core(send)
    row_taps, col_taps, keep = together((row_taps, col_taps, keep))
    bands = make_bands(row_taps, col_taps, side)
    got, bands = together((got, bands))
    weight_far, weight_near = keep[1] + got[1], keep[0] + got[0]
    weight_far, weight_near, bands = together((weight_far, weight_near, bands))
    weight_x = over_visit(weight_far, 1)
    keep_far, send_far = run((1, 0), half, bands)
    keep_far, send_far, weight_x = together((keep_far, send_far, weight_x))
    got_far = over_core(send_far)
    weight_near, weight_next = weight_near[0] + weight_x[0], weight_near[1] + weight_x[1]
    weight_near, weight_next, got_far = together((weight_near, weight_next, got_far))
    weight_y = over_visit(weight_next, 2)
    far = keep_far + got_far
    far, bands = together((far, bands))
    far_x = over_visit(far, 1)
    keep_near, send_near = run((0, 0), half, bands)
    keep_near, send_near, weight_y, far_x = together((keep_near, send_near, weight_y, far_x))
    got_near = over_core(send_near)
    weight_part = weight_near + weight_y
    weight_part, got_near = together((weight_part, got_near))
    near = [keep_near[y] + got_near[y] + far_x[y] for y in range(2)]
    near_y = over_visit(near[1], 2)
    weight_part, near = together((weight_part, near))
    weight_pieces = pieces_of(weight_part)
    part = near[0] + near_y
    weighted_sum = functools.reduce(jnp.add, pieces_of(part), part[0])
    weight_sum = functools.reduce(jnp.add, weight_pieces, weight_part[0])
    return weighted_sum[None], weight_sum[None]


def solution(mesh):
    placed = (
        P("visit", "patch", None, None, None),
        P("visit", "patch", None, None, None),
        P("visit", "patch", None),
        P("visit", "patch", None),
        P("visit", "patch", None),
        P("visit", "patch"),
        P(),
        P(),
        P(),
    )
    return jax.shard_map(
        on_device,
        mesh=mesh,
        in_specs=placed,
        out_specs=(P("patch", "visit", None), P("patch", "visit", None)),
        check_vma=False,
    )
```

time: 84.6 us -> 61.7 us (0.73)
  local copies, waits for them, and re-layouts: 16.3 us -> 0.08 us
  starting transfers between devices: 22.8 us -> 15.8 us
  waiting for transfers between devices: 13.4 us -> 17.5 us
  other arithmetic: 5.67 us -> 1.77 us
    unnamed x42 -> x18, local copies, waits for them, and re-layouts: 16.2 us -> 0.05 us
    ppermute x3, waiting for transfers between devices: 0.01 us -> 5.09 us  [over_core(): return lax.ppermute(value, 'patch', [(i, i ^ 1) for i in range(owners)])]
    add x5 -> x6, other arithmetic: 4.38 us -> 0.47 us  [the longest x1 0.15 us: on_device(): weight_far, weight_near = (keep[1] + got[1], keep[0] + got[0])]
    ppermute x6, starting transfers between devices: 11.9 us -> 8.62 us  [over_depth(): return lax.ppermute(value, 'patch', pairs)]
    ppermute x6 -> x4, starting transfers between devices: 9.9 us -> 6.67 us  [over_visit(): return lax.ppermute(value, 'visit', [(i, i ^ flip) for i in range(visits)])]
    ppermute x6 -> x4, waiting for transfers between devices: 9.92 us -> 7.23 us  [over_visit(): return lax.ppermute(value, 'visit', [(i, i ^ flip) for i in range(visits)])]
    ppermute x6, waiting for transfers between devices: 3.47 us -> 5.18 us  [over_depth(): return lax.ppermute(value, 'patch', pairs)]
    pallas_call x3 -> x4, Pallas kernels: 24.3 us -> 24.8 us  [the longest x2 20.7 us: match(): pl.pallas_call(functools.partial(match_kernel, offset), out_shape=(part,...]
  transfers between devices with their start and end apart: 15 -> 13, of which waited for: 6 -> 8; matrix products, arithmetic and copies ran while one was open for 6% -> 1% of each run, Pallas kernels for 25% -> 35%
where the time goes in v2:
time: 61.7 us; the launch traced here: 61.5 us
  Pallas kernels  24.8 us (40%)
  waiting for transfers between devices  17.5 us (28%)
  starting transfers between devices  15.8 us (26%)
  other arithmetic  1.77 us (3%)
  between operations  1.47 us (2%)
    pallas_call x2, Pallas kernels, match(): pl.pallas_call(functools.partial(match_kernel, offset), out_shape=(part,...  20.7 us
    ppermute x6, starting transfers between devices, over_depth(): return lax.ppermute(value, 'patch', pairs)  8.62 us
    ppermute x4, waiting for transfers between devices, over_visit(): return lax.ppermute(value, 'visit', [(i, i ^ flip) for i in range(visits)])  7.23 us
    ppermute x4, starting transfers between devices, over_visit(): return lax.ppermute(value, 'visit', [(i, i ^ flip) for i in range(visits)])  6.67 us
    ppermute x6, waiting for transfers between devices, over_depth(): return lax.ppermute(value, 'patch', pairs)  5.18 us
    ppermute x3, waiting for transfers between devices, over_core(): return lax.ppermute(value, 'patch', [(i, i ^ 1) for i in range(owners)])  5.09 us
    pallas_call x1, Pallas kernels, sum_weights(): pl.pallas_call(weight_kernel, out_shape=(part, part), in_specs=[anywhere]...  3.09 us
    broadcast_in_dim x2, other arithmetic, on_device(): return (weighted_sum[None], weight_sum[None])  1.29 us
  transfers between devices with their start and end apart: 13, of which 8 were waited for; matrix products, arithmetic and copies ran while one was open for 1% of the time, Pallas kernels for 35%

profile of v2, /device:TPU:0, one launch (start us, length us, event | category | flops | bytes accessed | tf_op | source)
XLA Modules:
  0.0 61.5 jit_solution(3398087626944592508)
XLA Ops:
  0.6 0.0 copy-start.4
  0.6 0.0 copy-start.3
  1.3 3.1 %shard_map.104 = (f32[2,2,4,64,256]{4,3,2,1,0:T(8,128)}, f32[2,2,4,64,256]{4,3,2,1,0:T(8,128)}) custom-call(s32[32]{0:T(128)} %bitcast.63, s32[32]{0:T(128)} %bitcast.66, s32[1]{0:T(128)} %bitcast.53.count_in, f32[32,128,128]{2,1,0:T(8,128)} %bitcast.58), custom_call_target="tpu_custom_call" | custom-call | flops 1000000000 | tf_op jit(solution)/shard_map/pallas_call | solution.py:112
  4.4 0.0 copy-start.8
  4.4 0.5 collective-permute-start
  4.9 0.0 copy-done.4
  4.9 0.0 copy-done.3
  4.9 0.0 copy-start.1
  4.9 1.0 %shard_map.105 = (bf16[16,128,256]{2,1,0:T(8,128)(2,1)S(1)}, bf16[16,256,128]{2,1,0:T(8,128)(2,1)S(1)}) custom-call(f32[16,41]{1,0:T(8,128)S(1)} %copy-done.3, f32[16,41]{1,0:T(8,128)S(1)} %copy-done.4), custom_call_target="tpu_custom_call" | custom-call | flops 1000000000 | tf_op jit(solution)/shard_map/pallas_call | solution.py:175
  6.0 0.0 copy-start
  6.0 0.0 copy-start.2
  6.0 0.0 copy-start.5
  6.0 0.0 copy-start.6
  6.0 0.0 copy-start.7
  6.1 1.4 %collective-permute-done = f32[2,2,4,64,256]{4,3,2,1,0:T(8,128)S(1)} collective-permute-done((f32[2,2,4,64,256]{4,3,2,1,0:T(8,128)}, f32[2,2,4,64,256]{4,3,2,1,0:T(8,128)S(1)}, u32[]{:S(2)}, u32[]{:S(2)}) %collective-permute-start) | collective-permute-done | bytes 1048608 | tf_op jit(solution)/shard_map/ppermute | solution.py:374
  7.4 0.0 copy-done.8
  7.4 0.2 add_bitcast_fusion
  7.6 2.9 %collective-permute-start.1 = (f32[2,4,64,256]{3,2,1,0:T(8,128)S(1)}, f32[2,4,64,256]{3,2,1,0:T(8,128)S(1)}, u32[]{:S(2)}, u32[]{:S(2)}) collective-permute-start(f32[2,4,64,256]{3,2,1,0:T(8,128)S(1)} %get-tuple-element.52), channel_id=1, source_target_pairs={{0,8},{8,0},{16,24},{24,16},{1,9},{9,1},{17,25},{25,17},{2,10},{10... | collective-permute-start | bytes 1572872 | tf_op jit(solution)/shard_map/ppermute | solution.py:377
  10.5 0.0 copy-done.1
  10.5 0.0 copy-done
  10.5 0.0 copy-done.2
  10.5 0.0 copy-done.5
  10.5 0.0 copy-done.6
  10.5 0.0 copy-done.7
  10.6 10.4 %shard_map.106 = (f32[2,4,64,256]{3,2,1,0:T(8,128)S(1)}, f32[2,4,64,256]{3,2,1,0:T(8,128)S(1)}) custom-call(s32[32]{0:T(128)S(1)} %bitcast.64, s32[32]{0:T(128)S(1)} %bitcast.67, s32[32]{0:T(128)S(1)} %bitcast.69, s32[1]{0:T(128)} %bitcast.54.count_in, f32[32,128,128]{2,1,0:T(8,128)S(1)} %bitcast.56, f32[32,128,128]{2,1,0:T(8,128)S(1)} %bitcast.59, ...), custom_call_target="tpu_custom_call" | custom-call | flops 10737418240 | bytes 10000000 | tf_op jit(solution)/shard_map/pallas_call | solution.py:328
  20.9 1.8 %collective-permute-done.1 = f32[2,4,64,256]{3,2,1,0:T(8,128)S(1)} collective-permute-done((f32[2,4,64,256]{3,2,1,0:T(8,128)S(1)}, f32[2,4,64,256]{3,2,1,0:T(8,128)S(1)}, u32[]{:S(2)}, u32[]{:S(2)}) %collective-permute-start.1) | collective-permute-done | bytes 524320 | tf_op jit(solution)/shard_map/ppermute | solution.py:377
  22.8 0.0 collective-permute-start.2
  22.8 0.1 add_bitcast_fusion.4
  22.8 1.8 %collective-permute-done.2 = f32[2,4,64,256]{3,2,1,0:T(8,128)S(1)} collective-permute-done((f32[2,4,64,256]{3,2,1,0:T(8,128)S(1)}, f32[2,4,64,256]{3,2,1,0:T(8,128)S(1)}, u32[]{:S(2)}, u32[]{:S(2)}) %collective-permute-start.2) | collective-permute-done | bytes 524320 | tf_op jit(solution)/shard_map/ppermute | solution.py:374
  24.7 0.1 add.79
  24.7 1.8 %collective-permute-start.3 = (f32[4,64,256]{2,1,0:T(8,128)S(1)}, f32[4,64,256]{2,1,0:T(8,128)S(1)}, u32[]{:S(2)}, u32[]{:S(2)}) collective-permute-start(f32[4,64,256]{2,1,0:T(8,128)S(1)} %get-tuple-element.62), channel_id=1, source_target_pairs={{0,16},{8,24},{16,0},{24,8},{1,17},{9,25},{17,1},{25,9},{2,18},{10... | collective-permute-start | bytes 786440 | tf_op jit(solution)/shard_map/ppermute | solution.py:377
  26.6 1.5 %collective-permute-start.4 = (f32[2,4,64,256]{3,2,1,0:T(8,128)S(1)}, f32[2,4,64,256]{3,2,1,0:T(8,128)S(1)}, u32[]{:S(2)}, u32[]{:S(2)}) collective-permute-start(f32[2,4,64,256]{3,2,1,0:T(8,128)S(1)} %add.79), channel_id=1, source_target_pairs={{0,8},{8,0},{16,24},{24,16},{1,9},{9,1},{17,25},{25,17},{2,10},{10... | collective-permute-start | bytes 1572872 | tf_op jit(solution)/shard_map/ppermute | solution.py:377
  28.1 10.3 %shard_map.107 = (f32[2,4,64,256]{3,2,1,0:T(8,128)S(1)}, f32[2,4,64,256]{3,2,1,0:T(8,128)S(1)}) custom-call(s32[32]{0:T(128)S(1)} %bitcast.65, s32[32]{0:T(128)S(1)} %bitcast.68, s32[32]{0:T(128)S(1)} %bitcast.70, s32[1]{0:T(128)} %bitcast.55.count_in, f32[32,128,128]{2,1,0:T(8,128)S(1)} %bitcast.57, f32[32,128,128]{2,1,0:T(8,128)S(1)} %bitcast.60, ...), custom_call_target="tpu_custom_call" | custom-call | flops 10737418240 | bytes 10000000 | tf_op jit(solution)/shard_map/pallas_call | solution.py:328
  38.4 0.0 collective-permute-done.3
  38.4 1.8 %collective-permute-done.4 = f32[2,4,64,256]{3,2,1,0:T(8,128)S(1)} collective-permute-done((f32[2,4,64,256]{3,2,1,0:T(8,128)S(1)}, f32[2,4,64,256]{3,2,1,0:T(8,128)S(1)}, u32[]{:S(2)}, u32[]{:S(2)}) %collective-permute-start.4) | collective-permute-done | bytes 524320 | tf_op jit(solution)/shard_map/ppermute | solution.py:377
  40.3 0.0 collective-permute-start.5
  40.3 1.9 %collective-permute-done.5 = f32[2,4,64,256]{3,2,1,0:T(8,128)S(1)} collective-permute-done((f32[2,4,64,256]{3,2,1,0:T(8,128)S(1)}, f32[2,4,64,256]{3,2,1,0:T(8,128)S(1)}, u32[]{:S(2)}, u32[]{:S(2)}) %collective-permute-start.5) | collective-permute-done | bytes 524320 | tf_op jit(solution)/shard_map/ppermute | solution.py:374
  42.2 0.1 add_bitcast_fusion.2
  42.3 0.4 collective-permute-start.6
  42.7 1.8 %collective-permute-start.10 = (f32[64,256]{1,0:T(8,128)S(1)}, f32[64,256]{1,0:T(8,128)S(1)}, u32[]{:S(2)}, u32[]{:S(2)}) collective-permute-start(f32[64,256]{1,0:T(8,128)S(1)} %get-tuple-element.78), channel_id=1, source_target_pairs={{0,2},{1,3},{2,0},{3,1},{4,6},{5,7},{6,4},{7,5},{8,10},{9,11},{10,... | collective-permute-start | bytes 196616 | tf_op jit(solution)/shard_map/ppermute | solution.py:384
  44.5 2.5 %collective-permute-start.12 = (f32[64,256]{1,0:T(8,128)S(1)}, f32[64,256]{1,0:T(8,128)S(1)}, u32[]{:S(2)}, u32[]{:S(2)}) collective-permute-start(f32[64,256]{1,0:T(8,128)S(1)} %get-tuple-element.79), channel_id=1, source_target_pairs={{0,6},{1,7},{2,4},{3,5},{4,2},{5,3},{6,0},{7,1},{8,14},{9,15},{10,... | collective-permute-start | bytes 196616 | tf_op jit(solution)/shard_map/ppermute | solution.py:384
  47.0 0.1 collective-permute-start.11
  47.1 3.6 %collective-permute-done.6 = f32[4,64,256]{2,1,0:T(8,128)S(1)} collective-permute-done((f32[4,64,256]{2,1,0:T(8,128)S(1)}, f32[4,64,256]{2,1,0:T(8,128)S(1)}, u32[]{:S(2)}, u32[]{:S(2)}) %collective-permute-start.6) | collective-permute-done | bytes 262176 | tf_op jit(solution)/shard_map/ppermute | solution.py:377
  50.8 1.6 %collective-permute-start.7 = (f32[64,256]{1,0:T(8,128)S(1)}, f32[64,256]{1,0:T(8,128)S(1)}, u32[]{:S(2)}, u32[]{:S(2)}) collective-permute-start(f32[64,256]{1,0:T(8,128)S(1)} %get-tuple-element.81), channel_id=1, source_target_pairs={{0,2},{1,3},{2,0},{3,1},{4,6},{5,7},{6,4},{7,5},{8,10},{9,11},{10,... | collective-permute-start | bytes 196616 | tf_op jit(solution)/shard_map/ppermute | solution.py:384
  52.4 2.5 %collective-permute-start.9 = (f32[64,256]{1,0:T(8,128)S(1)}, f32[64,256]{1,0:T(8,128)S(1)}, u32[]{:S(2)}, u32[]{:S(2)}) collective-permute-start(f32[64,256]{1,0:T(8,128)S(1)} %get-tuple-element.82), channel_id=1, source_target_pairs={{0,6},{1,7},{2,4},{3,5},{4,2},{5,3},{6,0},{7,1},{8,14},{9,15},{10,... | collective-permute-start | bytes 196616 | tf_op jit(solution)/shard_map/ppermute | solution.py:384
  54.9 0.0 collective-permute-done.10
  54.9 0.1 collective-permute-start.8
  55.0 0.0 collective-permute-done.12
  55.0 0.0 collective-permute-done.11
  55.0 0.6 %fusion.6 = f32[1,64,256]{2,1,0:T(8,128)} fusion(f32[64,256]{1,0:T(8,128)S(1)} %collective-permute-done.12, f32[64,256]{1,0:T(8,128)S(1)} %collective-permute-done.11, f32[64,256]{1,0:T(8,128)S(1)} %collective-permute-done.10, f32[4,64,256]{2,1,0:T(8,128)S(1)} %add.80), kind=kLoop, calls=%fused_computation.17 | loop fusion | flops 49152 | bytes 327680 | tf_op jit(solution)/shard_map/broadcast_in_dim | solution.py:424
  55.7 0.0 collective-permute-done.7
  55.7 3.1 %collective-permute-done.9 = f32[64,256]{1,0:T(8,128)S(1)} collective-permute-done((f32[64,256]{1,0:T(8,128)S(1)}, f32[64,256]{1,0:T(8,128)S(1)}, u32[]{:S(2)}, u32[]{:S(2)}) %collective-permute-start.9) | collective-permute-done | bytes 65568 | tf_op jit(solution)/shard_map/ppermute | solution.py:384
  58.7 2.1 %collective-permute-done.8 = f32[64,256]{1,0:T(8,128)S(1)} collective-permute-done((f32[64,256]{1,0:T(8,128)S(1)}, f32[64,256]{1,0:T(8,128)S(1)}, u32[]{:S(2)}, u32[]{:S(2)}) %collective-permute-start.8) | collective-permute-done | bytes 65568 | tf_op jit(solution)/shard_map/ppermute | solution.py:384
  60.8 0.6 %fusion.3 = f32[1,64,256]{2,1,0:T(8,128)} fusion(f32[64,256]{1,0:T(8,128)S(1)} %collective-permute-done.9, f32[64,256]{1,0:T(8,128)S(1)} %collective-permute-done.8, f32[64,256]{1,0:T(8,128)S(1)} %collective-permute-done.7, f32[4,64,256]{2,1,0:T(8,128)S(1)} %add.87), kind=kLoop, calls=%fused_computation.13 | loop fusion | flops 49152 | bytes 327680 | tf_op jit(solution)/shard_map/broadcast_in_dim | solution.py:424
  (4 shorter events, 0.1 us)
Async XLA Ops:
  0.6 4.3 %copy-start.4 = (f32[16,41]{1,0:T(8,128)S(1)}, f32[16,41]{1,0:T(8,128)}, u32[]{:S(2)}) copy-start(f32[16,41]{1,0:T(8,128)} %col_taps_in) | copy-start | bytes 7876
  0.6 4.3 %copy-start.3 = (f32[16,41]{1,0:T(8,128)S(1)}, f32[16,41]{1,0:T(8,128)}, u32[]{:S(2)}) copy-start(f32[16,41]{1,0:T(8,128)} %row_taps_in) | copy-start | bytes 7876
  4.4 3.0 %copy-start.8 = (f32[2,2,4,64,256]{4,3,2,1,0:T(8,128)S(1)}, f32[2,2,4,64,256]{4,3,2,1,0:T(8,128)}, u32[]{:S(2)}) copy-start(f32[2,2,4,64,256]{4,3,2,1,0:T(8,128)} %get-tuple-element.38) | copy-start | bytes 3145732
  4.4 3.0 %collective-permute-start = (f32[2,2,4,64,256]{4,3,2,1,0:T(8,128)}, f32[2,2,4,64,256]{4,3,2,1,0:T(8,128)S(1)}, u32[]{:S(2)}, u32[]{:S(2)}) collective-permute-start(f32[2,2,4,64,256]{4,3,2,1,0:T(8,128)} %get-tuple-element.39), channel_id=1, source_target_pairs={{0,1},{1,0},{2,3},{3,2},{4,5},{5,4},{6,7},{7,6},{8,9},{9,8},{10,11... | collective-permute-start | bytes 3145736 | tf_op jit(solution)/shard_map/ppermute | solution.py:374
  4.9 5.6 %copy-start.1 = (f32[1,1,32,128,128]{4,3,2,1,0:T(8,128)S(1)}, f32[1,1,32,128,128]{4,3,2,1,0:T(8,128)}, u32[]{:S(2)}) copy-start(f32[1,1,32,128,128]{4,3,2,1,0:T(8,128)} %param.10) | copy-start | bytes 6291460
  6.0 4.5 %copy-start = (f32[1,1,32,128,128]{4,3,2,1,0:T(8,128)S(1)}, f32[1,1,32,128,128]{4,3,2,1,0:T(8,128)}, u32[]{:S(2)}) copy-start(f32[1,1,32,128,128]{4,3,2,1,0:T(8,128)} %param.9) | copy-start | bytes 6291460
  6.0 4.5 %copy-start.2 = (f32[800,16,6]{0,1,2:T(8,128)S(1)}, f32[800,16,6]{0,1,2:T(8,128)}, u32[]{:S(2)}) copy-start(f32[800,16,6]{0,1,2:T(8,128)} %param.15) | copy-start | bytes 921604
  6.0 4.5 %copy-start.5 = (s32[1,1,32]{2,1,0:T(1,128)S(1)}, s32[1,1,32]{2,1,0:T(1,128)}, u32[]{:S(2)}) copy-start(s32[1,1,32]{2,1,0:T(1,128)} %param.11) | copy-start | bytes 388
  6.0 4.5 %copy-start.6 = (s32[1,1,32]{2,1,0:T(1,128)S(1)}, s32[1,1,32]{2,1,0:T(1,128)}, u32[]{:S(2)}) copy-start(s32[1,1,32]{2,1,0:T(1,128)} %param.12) | copy-start | bytes 388
  6.0 4.5 %copy-start.7 = (s32[1,1,32]{2,1,0:T(1,128)S(1)}, s32[1,1,32]{2,1,0:T(1,128)}, u32[]{:S(2)}) copy-start(s32[1,1,32]{2,1,0:T(1,128)} %param.13) | copy-start | bytes 388
  7.6 15.2 %collective-permute-start.1 = (f32[2,4,64,256]{3,2,1,0:T(8,128)S(1)}, f32[2,4,64,256]{3,2,1,0:T(8,128)S(1)}, u32[]{:S(2)}, u32[]{:S(2)}) collective-permute-start(f32[2,4,64,256]{3,2,1,0:T(8,128)S(1)} %get-tuple-element.52), channel_id=1, source_target_pairs={{0,8},{8,0},{16,24},{24,16},{1,9},{9,1},{17,25},{25,17},{2,10},{10... | collective-permute-start | bytes 1572872 | tf_op jit(solution)/shard_map/ppermute | solution.py:377
  22.8 1.9 %collective-permute-start.2 = (f32[2,4,64,256]{3,2,1,0:T(8,128)S(1)}, f32[2,4,64,256]{3,2,1,0:T(8,128)S(1)}, u32[]{:S(2)}, u32[]{:S(2)}) collective-permute-start(f32[2,4,64,256]{3,2,1,0:T(8,128)S(1)} %get-tuple-element.54), channel_id=1, source_target_pairs={{0,1},{1,0},{2,3},{3,2},{4,5},{5,4},{6,7},{7,6},{8,9},{9,8},{10,11... | collective-permute-start | bytes 1572872 | tf_op jit(solution)/shard_map/ppermute | solution.py:374
  24.7 13.7 %collective-permute-start.3 = (f32[4,64,256]{2,1,0:T(8,128)S(1)}, f32[4,64,256]{2,1,0:T(8,128)S(1)}, u32[]{:S(2)}, u32[]{:S(2)}) collective-permute-start(f32[4,64,256]{2,1,0:T(8,128)S(1)} %get-tuple-element.62), channel_id=1, source_target_pairs={{0,16},{8,24},{16,0},{24,8},{1,17},{9,25},{17,1},{25,9},{2,18},{10... | collective-permute-start | bytes 786440 | tf_op jit(solution)/shard_map/ppermute | solution.py:377
  26.6 13.7 %collective-permute-start.4 = (f32[2,4,64,256]{3,2,1,0:T(8,128)S(1)}, f32[2,4,64,256]{3,2,1,0:T(8,128)S(1)}, u32[]{:S(2)}, u32[]{:S(2)}) collective-permute-start(f32[2,4,64,256]{3,2,1,0:T(8,128)S(1)} %add.79), channel_id=1, source_target_pairs={{0,8},{8,0},{16,24},{24,16},{1,9},{9,1},{17,25},{25,17},{2,10},{10... | collective-permute-start | bytes 1572872 | tf_op jit(solution)/shard_map/ppermute | solution.py:377
  40.3 1.9 %collective-permute-start.5 = (f32[2,4,64,256]{3,2,1,0:T(8,128)S(1)}, f32[2,4,64,256]{3,2,1,0:T(8,128)S(1)}, u32[]{:S(2)}, u32[]{:S(2)}) collective-permute-start(f32[2,4,64,256]{3,2,1,0:T(8,128)S(1)} %get-tuple-element.65), channel_id=1, source_target_pairs={{0,1},{1,0},{2,3},{3,2},{4,5},{5,4},{6,7},{7,6},{8,9},{9,8},{10,11... | collective-permute-start | bytes 1572872 | tf_op jit(solution)/shard_map/ppermute | solution.py:374
  42.3 8.4 %collective-permute-start.6 = (f32[4,64,256]{2,1,0:T(8,128)S(1)}, f32[4,64,256]{2,1,0:T(8,128)S(1)}, u32[]{:S(2)}, u32[]{:S(2)}) collective-permute-start(f32[4,64,256]{2,1,0:T(8,128)S(1)} %get-tuple-element.74), channel_id=1, source_target_pairs={{0,16},{8,24},{16,0},{24,8},{1,17},{9,25},{17,1},{25,9},{2,18},{10... | collective-permute-start | bytes 786440 | tf_op jit(solution)/shard_map/ppermute | solution.py:377
  42.7 12.2 %collective-permute-start.10 = (f32[64,256]{1,0:T(8,128)S(1)}, f32[64,256]{1,0:T(8,128)S(1)}, u32[]{:S(2)}, u32[]{:S(2)}) collective-permute-start(f32[64,256]{1,0:T(8,128)S(1)} %get-tuple-element.78), channel_id=1, source_target_pairs={{0,2},{1,3},{2,0},{3,1},{4,6},{5,7},{6,4},{7,5},{8,10},{9,11},{10,... | collective-permute-start | bytes 196616 | tf_op jit(solution)/shard_map/ppermute | solution.py:384
  44.5 10.5 %collective-permute-start.12 = (f32[64,256]{1,0:T(8,128)S(1)}, f32[64,256]{1,0:T(8,128)S(1)}, u32[]{:S(2)}, u32[]{:S(2)}) collective-permute-start(f32[64,256]{1,0:T(8,128)S(1)} %get-tuple-element.79), channel_id=1, source_target_pairs={{0,6},{1,7},{2,4},{3,5},{4,2},{5,3},{6,0},{7,1},{8,14},{9,15},{10,... | collective-permute-start | bytes 196616 | tf_op jit(solution)/shard_map/ppermute | solution.py:384
  47.0 8.0 %collective-permute-start.11 = (f32[64,256]{1,0:T(8,128)S(1)}, f32[64,256]{1,0:T(8,128)S(1)}, u32[]{:S(2)}, u32[]{:S(2)}) collective-permute-start(f32[64,256]{1,0:T(8,128)S(1)} %get-tuple-element.80), channel_id=1, source_target_pairs={{0,4},{1,5},{2,6},{3,7},{4,0},{5,1},{6,2},{7,3},{8,12},{9,13},{10,... | collective-permute-start | bytes 196616 | tf_op jit(solution)/shard_map/ppermute | solution.py:384
  50.8 4.9 %collective-permute-start.7 = (f32[64,256]{1,0:T(8,128)S(1)}, f32[64,256]{1,0:T(8,128)S(1)}, u32[]{:S(2)}, u32[]{:S(2)}) collective-permute-start(f32[64,256]{1,0:T(8,128)S(1)} %get-tuple-element.81), channel_id=1, source_target_pairs={{0,2},{1,3},{2,0},{3,1},{4,6},{5,7},{6,4},{7,5},{8,10},{9,11},{10,... | collective-permute-start | bytes 196616 | tf_op jit(solution)/shard_map/ppermute | solution.py:384
  52.4 6.3 %collective-permute-start.9 = (f32[64,256]{1,0:T(8,128)S(1)}, f32[64,256]{1,0:T(8,128)S(1)}, u32[]{:S(2)}, u32[]{:S(2)}) collective-permute-start(f32[64,256]{1,0:T(8,128)S(1)} %get-tuple-element.82), channel_id=1, source_target_pairs={{0,6},{1,7},{2,4},{3,5},{4,2},{5,3},{6,0},{7,1},{8,14},{9,15},{10,... | collective-permute-start | bytes 196616 | tf_op jit(solution)/shard_map/ppermute | solution.py:384
  54.9 5.9 %collective-permute-start.8 = (f32[64,256]{1,0:T(8,128)S(1)}, f32[64,256]{1,0:T(8,128)S(1)}, u32[]{:S(2)}, u32[]{:S(2)}) collective-permute-start(f32[64,256]{1,0:T(8,128)S(1)} %get-tuple-element.83), channel_id=1, source_target_pairs={{0,4},{1,5},{2,6},{3,7},{4,0},{5,1},{6,2},{7,3},{8,12},{9,13},{10,... | collective-permute-start | bytes 196616 | tf_op jit(solution)/shard_map/ppermute | solution.py:384

commit v3 on v2

--- a/solution.py
+++ b/solution.py
@@ -13,7 +13,7 @@
 SHARE = 1.0 / 32.0
 KEEP = 1.0 - SHARE
 VMEM_BYTES = 40 * 2**20
-GROUP_ROWS = 256
+GROUP_ROWS = 512
 
 
 def split_left(value):
@@ -401,26 +401,29 @@
     weight_far, weight_near, bands = together((weight_far, weight_near, bands))
     weight_x = over_visit(weight_far, 1)
     keep_far, send_far = run((1, 0), half, bands)
-    keep_far, send_far, weight_x = together((keep_far, send_far, weight_x))
     got_far = over_core(send_far)
+    keep_far, weight_x = together((keep_far, weight_x))
     weight_near, weight_next = weight_near[0] + weight_x[0], weight_near[1] + weight_x[1]
     weight_near, weight_next, got_far = together((weight_near, weight_next, got_far))
+    far = keep_far + got_far
+    far, weight_next, bands = together((far, weight_next, bands))
     weight_y = over_visit(weight_next, 2)
-    far = keep_far + got_far
-    far, bands = together((far, bands))
     far_x = over_visit(far, 1)
     keep_near, send_near = run((0, 0), half, bands)
-    keep_near, send_near, weight_y, far_x = together((keep_near, send_near, weight_y, far_x))
+    send_near, weight_y = together((send_near, weight_y))
     got_near = over_core(send_near)
     weight_part = weight_near + weight_y
-    weight_part, got_near = together((weight_part, got_near))
-    near = [keep_near[y] + got_near[y] + far_x[y] for y in range(2)]
+    keep_near, weight_part, far_x = together((keep_near, weight_part, far_x))
+    weight_pieces = pieces_of(weight_part)
+    near = [keep_near[y] + far_x[y] for y in range(2)]
+    near, got_near = together((near, got_near))
+    near = [near[y] + got_near[y] for y in range(2)]
     near_y = over_visit(near[1], 2)
-    weight_part, near = together((weight_part, near))
-    weight_pieces = pieces_of(weight_part)
     part = near[0] + near_y
-    weighted_sum = functools.reduce(jnp.add, pieces_of(part), part[0])
+    pieces = pieces_of(part)
+    weight_part, part = together((weight_part, part))
     weight_sum = functools.reduce(jnp.add, weight_pieces, weight_part[0])
+    weighted_sum = functools.reduce(jnp.add, pieces, part[0])
     return weighted_sum[None], weight_sum[None]
 
 

time: 61.7 us -> 56.9 us (0.922)
  waiting for transfers between devices: 17.5 us -> 14.6 us
  Pallas kernels: 24.8 us -> 22.8 us
    ppermute x3, waiting for transfers between devices: 5.09 us -> 1.39 us  [over_core(): return lax.ppermute(value, 'patch', [(i, i ^ 1) for i in range(owners)])]
    pallas_call x2, Pallas kernels: 20.7 us -> 18.7 us  [match(): pl.pallas_call(functools.partial(match_kernel, offset), out_shape=(part,...]
    ppermute x4, waiting for transfers between devices: 7.23 us -> 8.1 us  [over_visit(): return lax.ppermute(value, 'visit', [(i, i ^ flip) for i in range(visits)])]
  transfers between devices with their start and end apart: 13 -> 13, of which waited for: 8 -> 6; matrix products, arithmetic and copies ran while one was open for 1% -> 2% of each run, Pallas kernels for 35% -> 35%
where the time goes in v3:
time: 56.9 us; the launch traced here: 56.8 us
  Pallas kernels  22.8 us (40%)
  starting transfers between devices  16 us (28%)
  waiting for transfers between devices  14.6 us (26%)
  other arithmetic  1.79 us (3%)
  between operations  1.51 us (3%)
    pallas_call x2, Pallas kernels, match(): pl.pallas_call(functools.partial(match_kernel, offset), out_shape=(part,...  18.7 us
    ppermute x6, starting transfers between devices, over_depth(): return lax.ppermute(value, 'patch', pairs)  8.43 us
    ppermute x4, waiting for transfers between devices, over_visit(): return lax.ppermute(value, 'visit', [(i, i ^ flip) for i in range(visits)])  8.1 us
    ppermute x4, starting transfers between devices, over_visit(): return lax.ppermute(value, 'visit', [(i, i ^ flip) for i in range(visits)])  6.89 us
    ppermute x6, waiting for transfers between devices, over_depth(): return lax.ppermute(value, 'patch', pairs)  5.1 us
    pallas_call x1, Pallas kernels, sum_weights(): pl.pallas_call(weight_kernel, out_shape=(part, part), in_specs=[anywhere]...  3.09 us
    ppermute x3, waiting for transfers between devices, over_core(): return lax.ppermute(value, 'patch', [(i, i ^ 1) for i in range(owners)])  1.39 us
    broadcast_in_dim x2, other arithmetic, on_device(): return (weighted_sum[None], weight_sum[None])  1.29 us
  transfers between devices with their start and end apart: 13, of which 6 were waited for; matrix products, arithmetic and copies ran while one was open for 2% of the time, Pallas kernels for 35%

profile of v3, /device:TPU:0, one launch (start us, length us, event | category | flops | bytes accessed | tf_op | source)
XLA Modules:
  0.0 56.8 jit_solution(14024890683466769855)
XLA Ops:
  0.6 0.0 copy-start.4
  0.6 0.0 copy-start.3
  1.3 3.1 %shard_map.104 = (f32[2,2,4,64,256]{4,3,2,1,0:T(8,128)}, f32[2,2,4,64,256]{4,3,2,1,0:T(8,128)}) custom-call(s32[32]{0:T(128)} %bitcast.67, s32[32]{0:T(128)} %bitcast.70, s32[1]{0:T(128)} %bitcast.57.count_in, f32[32,128,128]{2,1,0:T(8,128)} %bitcast.62), custom_call_target="tpu_custom_call" | custom-call | flops 1000000000 | tf_op jit(solution)/shard_map/pallas_call | solution.py:112
  4.4 0.0 copy-start.8
  4.4 0.5 collective-permute-start
  4.9 0.0 copy-done.4
  4.9 0.0 copy-done.3
  4.9 0.0 copy-start.1
  4.9 1.0 %shard_map.105 = (bf16[16,128,256]{2,1,0:T(8,128)(2,1)S(1)}, bf16[16,256,128]{2,1,0:T(8,128)(2,1)S(1)}) custom-call(f32[16,41]{1,0:T(8,128)S(1)} %copy-done.3, f32[16,41]{1,0:T(8,128)S(1)} %copy-done.4), custom_call_target="tpu_custom_call" | custom-call | flops 1000000000 | tf_op jit(solution)/shard_map/pallas_call | solution.py:175
  6.0 0.0 copy-start
  6.0 0.0 copy-start.2
  6.0 0.0 copy-start.5
  6.0 0.0 copy-start.6
  6.0 0.0 copy-start.7
  6.1 1.4 %collective-permute-done = f32[2,2,4,64,256]{4,3,2,1,0:T(8,128)S(1)} collective-permute-done((f32[2,2,4,64,256]{4,3,2,1,0:T(8,128)}, f32[2,2,4,64,256]{4,3,2,1,0:T(8,128)S(1)}, u32[]{:S(2)}, u32[]{:S(2)}) %collective-permute-start) | collective-permute-done | bytes 1048608 | tf_op jit(solution)/shard_map/ppermute | solution.py:374
  7.4 0.0 copy-done.8
  7.4 0.2 add_bitcast_fusion
  7.6 2.9 %collective-permute-start.1 = (f32[2,4,64,256]{3,2,1,0:T(8,128)S(1)}, f32[2,4,64,256]{3,2,1,0:T(8,128)S(1)}, u32[]{:S(2)}, u32[]{:S(2)}) collective-permute-start(f32[2,4,64,256]{3,2,1,0:T(8,128)S(1)} %get-tuple-element.52), channel_id=1, source_target_pairs={{0,8},{8,0},{16,24},{24,16},{1,9},{9,1},{17,25},{25,17},{2,10},{10... | collective-permute-start | bytes 1572872 | tf_op jit(solution)/shard_map/ppermute | solution.py:377
  10.5 0.0 copy-done.1
  10.5 0.0 copy-done
  10.5 0.0 copy-done.2
  10.5 0.0 copy-done.5
  10.5 0.0 copy-done.6
  10.5 0.0 copy-done.7
  10.6 9.4 %shard_map.106 = (f32[2,4,64,256]{3,2,1,0:T(8,128)S(1)}, f32[2,4,64,256]{3,2,1,0:T(8,128)S(1)}) custom-call(s32[32]{0:T(128)S(1)} %bitcast.68, s32[32]{0:T(128)S(1)} %bitcast.71, s32[32]{0:T(128)S(1)} %bitcast.73, s32[1]{0:T(128)} %bitcast.58.count_in, f32[32,128,128]{2,1,0:T(8,128)S(1)} %bitcast.60, f32[32,128,128]{2,1,0:T(8,128)S(1)} %bitcast.63, ...), custom_call_target="tpu_custom_call" | custom-call | flops 10737418240 | bytes 10000000 | tf_op jit(solution)/shard_map/pallas_call | solution.py:328
  19.9 0.1 collective-permute-start.2
  20.0 2.7 %collective-permute-done.1 = f32[2,4,64,256]{3,2,1,0:T(8,128)S(1)} collective-permute-done((f32[2,4,64,256]{3,2,1,0:T(8,128)S(1)}, f32[2,4,64,256]{3,2,1,0:T(8,128)S(1)}, u32[]{:S(2)}, u32[]{:S(2)}) %collective-permute-start.1) | collective-permute-done | bytes 524320 | tf_op jit(solution)/shard_map/ppermute | solution.py:377
  22.8 0.1 add_bitcast_fusion.4
  22.8 0.0 collective-permute-done.2
  22.8 0.1 add.77
  22.9 1.8 %collective-permute-start.3 = (f32[4,64,256]{2,1,0:T(8,128)S(1)}, f32[4,64,256]{2,1,0:T(8,128)S(1)}, u32[]{:S(2)}, u32[]{:S(2)}) collective-permute-start(f32[4,64,256]{2,1,0:T(8,128)S(1)} %get-tuple-element.64), channel_id=1, source_target_pairs={{0,16},{8,24},{16,0},{24,8},{1,17},{9,25},{17,1},{25,9},{2,18},{10... | collective-permute-start | bytes 786440 | tf_op jit(solution)/shard_map/ppermute | solution.py:377
  24.7 1.5 %collective-permute-start.4 = (f32[2,4,64,256]{3,2,1,0:T(8,128)S(1)}, f32[2,4,64,256]{3,2,1,0:T(8,128)S(1)}, u32[]{:S(2)}, u32[]{:S(2)}) collective-permute-start(f32[2,4,64,256]{3,2,1,0:T(8,128)S(1)} %add.77), channel_id=1, source_target_pairs={{0,8},{8,0},{16,24},{24,16},{1,9},{9,1},{17,25},{25,17},{2,10},{10... | collective-permute-start | bytes 1572872 | tf_op jit(solution)/shard_map/ppermute | solution.py:377
  26.2 9.3 %shard_map.107 = (f32[2,4,64,256]{3,2,1,0:T(8,128)S(1)}, f32[2,4,64,256]{3,2,1,0:T(8,128)S(1)}) custom-call(s32[32]{0:T(128)S(1)} %bitcast.69, s32[32]{0:T(128)S(1)} %bitcast.72, s32[32]{0:T(128)S(1)} %bitcast.74, s32[1]{0:T(128)} %bitcast.59.count_in, f32[32,128,128]{2,1,0:T(8,128)S(1)} %bitcast.61, f32[32,128,128]{2,1,0:T(8,128)S(1)} %bitcast.64, ...), custom_call_target="tpu_custom_call" | custom-call | flops 10737418240 | bytes 10000000 | tf_op jit(solution)/shard_map/pallas_call | solution.py:328
  35.6 0.0 collective-permute-done.3
  35.6 0.1 collective-permute-start.5
  35.7 1.9 %collective-permute-done.4 = f32[2,4,64,256]{3,2,1,0:T(8,128)S(1)} collective-permute-done((f32[2,4,64,256]{3,2,1,0:T(8,128)S(1)}, f32[2,4,64,256]{3,2,1,0:T(8,128)S(1)}, u32[]{:S(2)}, u32[]{:S(2)}) %collective-permute-start.4) | collective-permute-done | bytes 524320 | tf_op jit(solution)/shard_map/ppermute | solution.py:377
  37.6 0.1 add_bitcast_fusion.2
  37.7 0.0 collective-permute-done.5
  37.7 0.6 %collective-permute-start.6 = (f32[4,64,256]{2,1,0:T(8,128)S(1)}, f32[4,64,256]{2,1,0:T(8,128)S(1)}, u32[]{:S(2)}, u32[]{:S(2)}) collective-permute-start(f32[4,64,256]{2,1,0:T(8,128)S(1)} %bitcast_add_fusion), channel_id=1, source_target_pairs={{0,16},{8,24},{16,0},{24,8},{1,17},{9,25},{17,1},{25,9},{2,18},{10... | collective-permute-start | bytes 786440 | tf_op jit(solution)/shard_map/ppermute | solution.py:377
  38.4 1.6 %collective-permute-start.10 = (f32[64,256]{1,0:T(8,128)S(1)}, f32[64,256]{1,0:T(8,128)S(1)}, u32[]{:S(2)}, u32[]{:S(2)}) collective-permute-start(f32[64,256]{1,0:T(8,128)S(1)} %get-tuple-element.82), channel_id=1, source_target_pairs={{0,2},{1,3},{2,0},{3,1},{4,6},{5,7},{6,4},{7,5},{8,10},{9,11},{10,... | collective-permute-start | bytes 196616 | tf_op jit(solution)/shard_map/ppermute | solution.py:384
  40.0 2.5 %collective-permute-start.12 = (f32[64,256]{1,0:T(8,128)S(1)}, f32[64,256]{1,0:T(8,128)S(1)}, u32[]{:S(2)}, u32[]{:S(2)}) collective-permute-start(f32[64,256]{1,0:T(8,128)S(1)} %get-tuple-element.83), channel_id=1, source_target_pairs={{0,6},{1,7},{2,4},{3,5},{4,2},{5,3},{6,0},{7,1},{8,14},{9,15},{10,... | collective-permute-start | bytes 196616 | tf_op jit(solution)/shard_map/ppermute | solution.py:384
  42.4 0.1 collective-permute-start.11
  42.6 3.5 %collective-permute-done.6 = f32[4,64,256]{2,1,0:T(8,128)S(1)} collective-permute-done((f32[4,64,256]{2,1,0:T(8,128)S(1)}, f32[4,64,256]{2,1,0:T(8,128)S(1)}, u32[]{:S(2)}, u32[]{:S(2)}) %collective-permute-start.6) | collective-permute-done | bytes 262176 | tf_op jit(solution)/shard_map/ppermute | solution.py:377
  46.0 0.1 fusion
  46.1 1.7 %collective-permute-start.7 = (f32[64,256]{1,0:T(8,128)S(1)}, f32[64,256]{1,0:T(8,128)S(1)}, u32[]{:S(2)}, u32[]{:S(2)}) collective-permute-start(f32[64,256]{1,0:T(8,128)S(1)} %get-tuple-element.85), channel_id=1, source_target_pairs={{0,2},{1,3},{2,0},{3,1},{4,6},{5,7},{6,4},{7,5},{8,10},{9,11},{10,... | collective-permute-start | bytes 196616 | tf_op jit(solution)/shard_map/ppermute | solution.py:384
  47.8 2.5 %collective-permute-start.9 = (f32[64,256]{1,0:T(8,128)S(1)}, f32[64,256]{1,0:T(8,128)S(1)}, u32[]{:S(2)}, u32[]{:S(2)}) collective-permute-start(f32[64,256]{1,0:T(8,128)S(1)} %get-tuple-element.86), channel_id=1, source_target_pairs={{0,6},{1,7},{2,4},{3,5},{4,2},{5,3},{6,0},{7,1},{8,14},{9,15},{10,... | collective-permute-start | bytes 196616 | tf_op jit(solution)/shard_map/ppermute | solution.py:384
  50.2 0.0 collective-permute-done.10
  50.2 0.1 collective-permute-start.8
  50.4 0.0 collective-permute-done.12
  50.4 0.0 collective-permute-done.11
  50.4 0.6 %fusion.3 = f32[1,64,256]{2,1,0:T(8,128)} fusion(f32[64,256]{1,0:T(8,128)S(1)} %collective-permute-done.12, f32[64,256]{1,0:T(8,128)S(1)} %collective-permute-done.11, f32[64,256]{1,0:T(8,128)S(1)} %collective-permute-done.10, f32[4,64,256]{2,1,0:T(8,128)S(1)} %add.78), kind=kLoop, calls=%fused_computation.15 | loop fusion | flops 49152 | bytes 327680 | tf_op jit(solution)/shard_map/broadcast_in_dim | solution.py:427
  51.0 0.0 collective-permute-done.7
  51.0 3.0 %collective-permute-done.9 = f32[64,256]{1,0:T(8,128)S(1)} collective-permute-done((f32[64,256]{1,0:T(8,128)S(1)}, f32[64,256]{1,0:T(8,128)S(1)}, u32[]{:S(2)}, u32[]{:S(2)}) %collective-permute-start.9) | collective-permute-done | bytes 65568 | tf_op jit(solution)/shard_map/ppermute | solution.py:384
  54.0 2.1 %collective-permute-done.8 = f32[64,256]{1,0:T(8,128)S(1)} collective-permute-done((f32[64,256]{1,0:T(8,128)S(1)}, f32[64,256]{1,0:T(8,128)S(1)}, u32[]{:S(2)}, u32[]{:S(2)}) %collective-permute-start.8) | collective-permute-done | bytes 65568 | tf_op jit(solution)/shard_map/ppermute | solution.py:384
  56.1 0.6 %fusion.6 = f32[1,64,256]{2,1,0:T(8,128)} fusion(f32[64,256]{1,0:T(8,128)S(1)} %collective-permute-done.9, f32[64,256]{1,0:T(8,128)S(1)} %collective-permute-done.8, f32[64,256]{1,0:T(8,128)S(1)} %collective-permute-done.7, f32[4,64,256]{2,1,0:T(8,128)S(1)} %fusion), kind=kLoop, calls=%fused_computation.19 | loop fusion | flops 49152 | bytes 327680 | tf_op jit(solution)/shard_map/broadcast_in_dim | solution.py:427
  (4 shorter events, 0.1 us)
Async XLA Ops:
  0.6 4.3 %copy-start.4 = (f32[16,41]{1,0:T(8,128)S(1)}, f32[16,41]{1,0:T(8,128)}, u32[]{:S(2)}) copy-start(f32[16,41]{1,0:T(8,128)} %col_taps_in) | copy-start | bytes 7876
  0.6 4.3 %copy-start.3 = (f32[16,41]{1,0:T(8,128)S(1)}, f32[16,41]{1,0:T(8,128)}, u32[]{:S(2)}) copy-start(f32[16,41]{1,0:T(8,128)} %row_taps_in) | copy-start | bytes 7876
  4.4 3.0 %copy-start.8 = (f32[2,2,4,64,256]{4,3,2,1,0:T(8,128)S(1)}, f32[2,2,4,64,256]{4,3,2,1,0:T(8,128)}, u32[]{:S(2)}) copy-start(f32[2,2,4,64,256]{4,3,2,1,0:T(8,128)} %get-tuple-element.40) | copy-start | bytes 3145732
  4.4 3.0 %collective-permute-start = (f32[2,2,4,64,256]{4,3,2,1,0:T(8,128)}, f32[2,2,4,64,256]{4,3,2,1,0:T(8,128)S(1)}, u32[]{:S(2)}, u32[]{:S(2)}) collective-permute-start(f32[2,2,4,64,256]{4,3,2,1,0:T(8,128)} %get-tuple-element.41), channel_id=1, source_target_pairs={{0,1},{1,0},{2,3},{3,2},{4,5},{5,4},{6,7},{7,6},{8,9},{9,8},{10,11... | collective-permute-start | bytes 3145736 | tf_op jit(solution)/shard_map/ppermute | solution.py:374
  4.9 5.6 %copy-start.1 = (f32[1,1,32,128,128]{4,3,2,1,0:T(8,128)S(1)}, f32[1,1,32,128,128]{4,3,2,1,0:T(8,128)}, u32[]{:S(2)}) copy-start(f32[1,1,32,128,128]{4,3,2,1,0:T(8,128)} %param.10) | copy-start | bytes 6291460
  6.0 4.5 %copy-start = (f32[1,1,32,128,128]{4,3,2,1,0:T(8,128)S(1)}, f32[1,1,32,128,128]{4,3,2,1,0:T(8,128)}, u32[]{:S(2)}) copy-start(f32[1,1,32,128,128]{4,3,2,1,0:T(8,128)} %param.9) | copy-start | bytes 6291460
  6.0 4.5 %copy-start.2 = (f32[800,16,6]{0,1,2:T(8,128)S(1)}, f32[800,16,6]{0,1,2:T(8,128)}, u32[]{:S(2)}) copy-start(f32[800,16,6]{0,1,2:T(8,128)} %param.15) | copy-start | bytes 921604
  6.0 4.5 %copy-start.5 = (s32[1,1,32]{2,1,0:T(1,128)S(1)}, s32[1,1,32]{2,1,0:T(1,128)}, u32[]{:S(2)}) copy-start(s32[1,1,32]{2,1,0:T(1,128)} %param.11) | copy-start | bytes 388
  6.0 4.5 %copy-start.6 = (s32[1,1,32]{2,1,0:T(1,128)S(1)}, s32[1,1,32]{2,1,0:T(1,128)}, u32[]{:S(2)}) copy-start(s32[1,1,32]{2,1,0:T(1,128)} %param.12) | copy-start | bytes 388
  6.0 4.5 %copy-start.7 = (s32[1,1,32]{2,1,0:T(1,128)S(1)}, s32[1,1,32]{2,1,0:T(1,128)}, u32[]{:S(2)}) copy-start(s32[1,1,32]{2,1,0:T(1,128)} %param.13) | copy-start | bytes 388
  7.6 15.2 %collective-permute-start.1 = (f32[2,4,64,256]{3,2,1,0:T(8,128)S(1)}, f32[2,4,64,256]{3,2,1,0:T(8,128)S(1)}, u32[]{:S(2)}, u32[]{:S(2)}) collective-permute-start(f32[2,4,64,256]{3,2,1,0:T(8,128)S(1)} %get-tuple-element.52), channel_id=1, source_target_pairs={{0,8},{8,0},{16,24},{24,16},{1,9},{9,1},{17,25},{25,17},{2,10},{10... | collective-permute-start | bytes 1572872 | tf_op jit(solution)/shard_map/ppermute | solution.py:377
  19.9 2.9 %collective-permute-start.2 = (f32[2,4,64,256]{3,2,1,0:T(8,128)S(1)}, f32[2,4,64,256]{3,2,1,0:T(8,128)S(1)}, u32[]{:S(2)}, u32[]{:S(2)}) collective-permute-start(f32[2,4,64,256]{3,2,1,0:T(8,128)S(1)} %get-tuple-element.56), channel_id=1, source_target_pairs={{0,1},{1,0},{2,3},{3,2},{4,5},{5,4},{6,7},{7,6},{8,9},{9,8},{10,11... | collective-permute-start | bytes 1572872 | tf_op jit(solution)/shard_map/ppermute | solution.py:374
  22.9 12.7 %collective-permute-start.3 = (f32[4,64,256]{2,1,0:T(8,128)S(1)}, f32[4,64,256]{2,1,0:T(8,128)S(1)}, u32[]{:S(2)}, u32[]{:S(2)}) collective-permute-start(f32[4,64,256]{2,1,0:T(8,128)S(1)} %get-tuple-element.64), channel_id=1, source_target_pairs={{0,16},{8,24},{16,0},{24,8},{1,17},{9,25},{17,1},{25,9},{2,18},{10... | collective-permute-start | bytes 786440 | tf_op jit(solution)/shard_map/ppermute | solution.py:377
  24.7 12.9 %collective-permute-start.4 = (f32[2,4,64,256]{3,2,1,0:T(8,128)S(1)}, f32[2,4,64,256]{3,2,1,0:T(8,128)S(1)}, u32[]{:S(2)}, u32[]{:S(2)}) collective-permute-start(f32[2,4,64,256]{3,2,1,0:T(8,128)S(1)} %add.77), channel_id=1, source_target_pairs={{0,8},{8,0},{16,24},{24,16},{1,9},{9,1},{17,25},{25,17},{2,10},{10... | collective-permute-start | bytes 1572872 | tf_op jit(solution)/shard_map/ppermute | solution.py:377
  35.6 2.1 %collective-permute-start.5 = (f32[2,4,64,256]{3,2,1,0:T(8,128)S(1)}, f32[2,4,64,256]{3,2,1,0:T(8,128)S(1)}, u32[]{:S(2)}, u32[]{:S(2)}) collective-permute-start(f32[2,4,64,256]{3,2,1,0:T(8,128)S(1)} %get-tuple-element.70), channel_id=1, source_target_pairs={{0,1},{1,0},{2,3},{3,2},{4,5},{5,4},{6,7},{7,6},{8,9},{9,8},{10,11... | collective-permute-start | bytes 1572872 | tf_op jit(solution)/shard_map/ppermute | solution.py:374
  37.7 8.3 %collective-permute-start.6 = (f32[4,64,256]{2,1,0:T(8,128)S(1)}, f32[4,64,256]{2,1,0:T(8,128)S(1)}, u32[]{:S(2)}, u32[]{:S(2)}) collective-permute-start(f32[4,64,256]{2,1,0:T(8,128)S(1)} %bitcast_add_fusion), channel_id=1, source_target_pairs={{0,16},{8,24},{16,0},{24,8},{1,17},{9,25},{17,1},{25,9},{2,18},{10... | collective-permute-start | bytes 786440 | tf_op jit(solution)/shard_map/ppermute | solution.py:377
  38.4 11.9 %collective-permute-start.10 = (f32[64,256]{1,0:T(8,128)S(1)}, f32[64,256]{1,0:T(8,128)S(1)}, u32[]{:S(2)}, u32[]{:S(2)}) collective-permute-start(f32[64,256]{1,0:T(8,128)S(1)} %get-tuple-element.82), channel_id=1, source_target_pairs={{0,2},{1,3},{2,0},{3,1},{4,6},{5,7},{6,4},{7,5},{8,10},{9,11},{10,... | collective-permute-start | bytes 196616 | tf_op jit(solution)/shard_map/ppermute | solution.py:384
  40.0 10.4 %collective-permute-start.12 = (f32[64,256]{1,0:T(8,128)S(1)}, f32[64,256]{1,0:T(8,128)S(1)}, u32[]{:S(2)}, u32[]{:S(2)}) collective-permute-start(f32[64,256]{1,0:T(8,128)S(1)} %get-tuple-element.83), channel_id=1, source_target_pairs={{0,6},{1,7},{2,4},{3,5},{4,2},{5,3},{6,0},{7,1},{8,14},{9,15},{10,... | collective-permute-start | bytes 196616 | tf_op jit(solution)/shard_map/ppermute | solution.py:384
  42.4 7.9 %collective-permute-start.11 = (f32[64,256]{1,0:T(8,128)S(1)}, f32[64,256]{1,0:T(8,128)S(1)}, u32[]{:S(2)}, u32[]{:S(2)}) collective-permute-start(f32[64,256]{1,0:T(8,128)S(1)} %get-tuple-element.84), channel_id=1, source_target_pairs={{0,4},{1,5},{2,6},{3,7},{4,0},{5,1},{6,2},{7,3},{8,12},{9,13},{10,... | collective-permute-start | bytes 196616 | tf_op jit(solution)/shard_map/ppermute | solution.py:384
  46.1 4.9 %collective-permute-start.7 = (f32[64,256]{1,0:T(8,128)S(1)}, f32[64,256]{1,0:T(8,128)S(1)}, u32[]{:S(2)}, u32[]{:S(2)}) collective-permute-start(f32[64,256]{1,0:T(8,128)S(1)} %get-tuple-element.85), channel_id=1, source_target_pairs={{0,2},{1,3},{2,0},{3,1},{4,6},{5,7},{6,4},{7,5},{8,10},{9,11},{10,... | collective-permute-start | bytes 196616 | tf_op jit(solution)/shard_map/ppermute | solution.py:384
  47.8 6.2 %collective-permute-start.9 = (f32[64,256]{1,0:T(8,128)S(1)}, f32[64,256]{1,0:T(8,128)S(1)}, u32[]{:S(2)}, u32[]{:S(2)}) collective-permute-start(f32[64,256]{1,0:T(8,128)S(1)} %get-tuple-element.86), channel_id=1, source_target_pairs={{0,6},{1,7},{2,4},{3,5},{4,2},{5,3},{6,0},{7,1},{8,14},{9,15},{10,... | collective-permute-start | bytes 196616 | tf_op jit(solution)/shard_map/ppermute | solution.py:384
  50.2 5.9 %collective-permute-start.8 = (f32[64,256]{1,0:T(8,128)S(1)}, f32[64,256]{1,0:T(8,128)S(1)}, u32[]{:S(2)}, u32[]{:S(2)}) collective-permute-start(f32[64,256]{1,0:T(8,128)S(1)} %get-tuple-element.87), channel_id=1, source_target_pairs={{0,4},{1,5},{2,6},{3,7},{4,0},{5,1},{6,2},{7,3},{8,12},{9,13},{10,... | collective-permute-start | bytes 196616 | tf_op jit(solution)/shard_map/ppermute | solution.py:384

commit v4 on v3

--- a/solution.py
+++ b/solution.py
@@ -79,7 +79,7 @@
     start_all(scalars)
     start_all(arrays)
     canvas[...] = jnp.zeros_like(canvas)
-    where = my_place(canvas.shape[4])
+    where = my_place(2 * canvas.shape[4])
     wait_all(scalars)
 
     def add_block(n, carry):
@@ -88,7 +88,9 @@
         core, depth, down, across = place_of(where, targets[n], quarters[n])
         column = pl.ds(pl.multiple_of(across * side, side), side)
         for part in range(2):
-            canvas[core, part ^ where[4], down, 0, depth, :, column] += inverse[
+            canvas[
+                core, lax.rem(depth, 2), part ^ where[4], down, depth // 2, :, column
+            ] += inverse[
                 part * half : (part + 1) * half
             ]
         return carry
@@ -97,8 +99,8 @@
         arrays[i].wait()
         lax.fori_loop(i * size, (i + 1) * size, add_block, 0, unroll=2)
     outs = [
-        pltpu.make_async_copy(canvas.at[1, :, :, 0], send_out, out_done.at[0]),
-        pltpu.make_async_copy(canvas.at[0, :, :, 0], keep_out, out_done.at[1]),
+        pltpu.make_async_copy(canvas.at[1], send_out, out_done.at[0]),
+        pltpu.make_async_copy(canvas.at[0], keep_out, out_done.at[1]),
     ]
     start_all(outs)
     wait_all(outs)
@@ -107,7 +109,7 @@
 def sum_weights(targets, quarters, count, variance, depths):
     blocks, side, _ = variance.shape
     half = side // 2
-    part = jax.ShapeDtypeStruct((2, 2, depths, half, 2 * side), f32)
+    part = jax.ShapeDtypeStruct((2, 2, 2, depths // 2, half, 2 * side), f32)
     anywhere = pl.BlockSpec(memory_space=pltpu.HBM)
     return pl.pallas_call(
         weight_kernel,
@@ -119,12 +121,12 @@
             pltpu.SMEM(quarters.shape, jnp.int32),
             pltpu.SMEM(count.shape, jnp.int32),
             pltpu.VMEM(variance.shape, f32),
-            pltpu.VMEM((2, 2, 2, 1, depths, half, 2 * side), f32),
+            pltpu.VMEM((2,) + part.shape, f32),
             pltpu.SemaphoreType.DMA((3,)),
             pltpu.SemaphoreType.DMA((4,)),
             pltpu.SemaphoreType.DMA((2,)),
         ],
-        compiler_params=pltpu.CompilerParams(vmem_limit_bytes=62 * 2**20),
+        compiler_params=pltpu.CompilerParams(vmem_limit_bytes=VMEM_BYTES),
         cost_estimate=pl.CostEstimate(flops=10**9, bytes_accessed=0, transcendentals=0),
     )(targets, quarters, count, variance)
 
@@ -194,14 +196,14 @@
 
 
 def match_kernel(
-    offset, targets_in, quarters_in, rows_in, count_in, pixels_in, variance_in, table_in,
-    col_in, row_in, keep_out, send_out,
-    targets, quarters, table_rows, count, pixels, variance, table, col_band, row_band, canvas,
-    total, coefficients, scalar_done, array_done, pixel_done, variance_done, out_done,
+    offset, targets_in, quarters_in, rows_in, count_in, pixels, variance, table,
+    col_band, row_band, keep_out, send_out,
+    targets, quarters, table_rows, count, canvas, total, coefficients, scalar_done, out_done,
 ):
-    blocks, side, _ = pixels.shape
-    nbasis, rows, _ = col_band.shape
-    group = total.shape[0]
+    side = pixels.shape[1]
+    nbasis = col_band.shape[0]
+    blocks = pixels.shape[0]
+    group, rows, _ = total.shape
     far, start = offset
     where = my_place(canvas.shape[2])
     top = pl.multiple_of((where[4] ^ far) * (side // 2) + start, rows)
@@ -212,43 +214,15 @@
              (count_in, count)]
         )
     ]
-    copy_col = pltpu.make_async_copy(col_in.at[:, pl.ds(top, rows)], col_band, array_done.at[0])
-    copy_row = pltpu.make_async_copy(row_in, row_band, array_done.at[1])
-    copy_table = pltpu.make_async_copy(table_in, table, array_done.at[2])
-
-    def pixel_copy(j):
-        at = pl.ds(j * group, group)
-        return pltpu.make_async_copy(pixels_in.at[at], pixels.at[at], pixel_done.at[j])
-
-    def variance_copy(j):
-        at = pl.ds(j * group, group)
-        return pltpu.make_async_copy(
-            variance_in.at[at, pl.ds(top, rows)], variance.at[at], variance_done.at[j]
-        )
-
     start_all(scalars)
-    copy_table.start()
-    copy_col.start()
-    pixel_copy(0).start()
-    copy_row.start()
-    variance_copy(0).start()
-    for j in range(1, blocks // group):
-        pixel_copy(j).start()
-        variance_copy(j).start()
     canvas[...] = jnp.zeros_like(canvas)
-    entries = table.shape[2]
-    copy_table.wait()
-    coefficients[:, :, :entries] = table[...]
+    coefficients[:, :, : table.shape[2]] = table[...]
     lane = lax.broadcasted_iota(jnp.int32, (1, side), 1).astype(f32)
     sub = lax.broadcasted_iota(jnp.int32, (8, side), 0).astype(f32)
     step = 8.0 / side
     wait_all(scalars)
-    copy_col.wait()
-    copy_row.wait()
 
     def add_group(j, carry):
-        pixel_copy(j).wait()
-        variance_copy(j).wait()
         terms = []
         for member in range(group):
             n = group * j + member
@@ -264,7 +238,7 @@
             constant = poly[0] + across * (poly[1] + across * poly[3])
             linear = poly[2] + across * poly[4]
             terms.append((constant, linear, poly[5], down))
-        left = col_band[...].reshape(nbasis * rows, 2 * side)
+        left = col_band[:, pl.ds(top, rows), :].reshape(nbasis * rows, 2 * side)
         halves = []
         for pair in range(group // 2):
             n = group * j + 2 * pair
@@ -302,7 +276,9 @@
             live = jnp.where(n < count[0], 1.0, 0.0).astype(f32)
             core, depth, down, across = place_of(where, targets[n], quarters[n])
             column = pl.ds(pl.multiple_of(across * side, side), side)
-            canvas[core, down, depth, :, column] += (live / variance[n]) * total[member]
+            canvas[core, down, depth, :, column] += (
+                live / variance[n, pl.ds(top, rows), :]
+            ) * total[member]
         return carry
 
     lax.fori_loop(0, blocks // group, add_group, 0)
@@ -323,27 +299,20 @@
     group = min(blocks, GROUP_ROWS // rows)
     part = jax.ShapeDtypeStruct((2, depths, rows, 2 * side), f32)
     anywhere = pl.BlockSpec(memory_space=pltpu.HBM)
+    vector = pl.BlockSpec(memory_space=pltpu.VMEM)
     entries = -(-table.shape[2] // 128) * 128
     scalars = (targets, quarters, table_rows, count)
     return pl.pallas_call(
         functools.partial(match_kernel, offset),
         out_shape=(part, part),
-        in_specs=[anywhere] * 9,
+        in_specs=[anywhere] * 4 + [vector] * 5,
         out_specs=[anywhere] * 2,
         scratch_shapes=[pltpu.SMEM(a.shape, jnp.int32) for a in scalars]
         + [
-            pltpu.VMEM(pixels.shape, f32),
-            pltpu.VMEM((blocks, rows, side), f32),
-            pltpu.VMEM(table.shape, f32),
-            pltpu.VMEM((nbasis, rows, 2 * side), bf16),
-            pltpu.VMEM(row_band.shape, bf16),
             pltpu.VMEM((2, 2, depths, rows, 2 * side), f32),
             pltpu.VMEM((group, rows, side), f32),
             pltpu.VMEM(table.shape[:2] + (entries,), f32),
             pltpu.SemaphoreType.DMA((4,)),
-            pltpu.SemaphoreType.DMA((3,)),
-            pltpu.SemaphoreType.DMA((blocks // group,)),
-            pltpu.SemaphoreType.DMA((blocks // group,)),
             pltpu.SemaphoreType.DMA((2,)),
         ],
         compiler_params=pltpu.CompilerParams(vmem_limit_bytes=VMEM_BYTES),
@@ -384,7 +353,8 @@
         return lax.ppermute(value, "patch", pairs)
 
     def pieces_of(value):
-        return [over_depth(value[s], s) for s in range(1, depths)]
+        order = [depths - 1] + list(range(1, depths - 1))
+        return [over_depth(value[s], s) for s in order]
 
     def run(offset, rows, bands):
         return match(
@@ -392,38 +362,43 @@
             table, bands[0], bands[1], depths,
         )
 
+    def over_core_parts(value):
+        return [over_core(value[y]) for y in range(2)]
+
+    bands = make_bands(row_taps, col_taps, side)
+    variances, bands = together((variances, bands))
     keep, send = sum_weights(targets, quarters, count, variances, depths)
     got = over_core(send)
-    row_taps, col_taps, keep = together((row_taps, col_taps, keep))
-    bands = make_bands(row_taps, col_taps, side)
-    got, bands = together((got, bands))
-    weight_far, weight_near = keep[1] + got[1], keep[0] + got[0]
-    weight_far, weight_near, bands = together((weight_far, weight_near, bands))
-    weight_x = over_visit(weight_far, 1)
+    keep, bands = together((keep, bands))
     keep_far, send_far = run((1, 0), half, bands)
-    got_far = over_core(send_far)
-    keep_far, weight_x = together((keep_far, weight_x))
-    weight_near, weight_next = weight_near[0] + weight_x[0], weight_near[1] + weight_x[1]
-    weight_near, weight_next, got_far = together((weight_near, weight_next, got_far))
-    far = keep_far + got_far
-    far, weight_next, bands = together((far, weight_next, bands))
-    weight_y = over_visit(weight_next, 2)
+    got_far = over_core_parts(send_far)
+    far = keep_far + jnp.stack(got_far)
+    far, got = together((far, got))
     far_x = over_visit(far, 1)
+    weight_odd, weights = keep[1] + got[1], keep[0] + got[0]
+    far, weight_odd, weights, bands = together((far, weight_odd, weights, bands))
+    weight_depth = over_depth(weight_odd, 1)
     keep_near, send_near = run((0, 0), half, bands)
-    send_near, weight_y = together((send_near, weight_y))
-    got_near = over_core(send_near)
-    weight_part = weight_near + weight_y
-    keep_near, weight_part, far_x = together((keep_near, weight_part, far_x))
-    weight_pieces = pieces_of(weight_part)
+    got_near = over_core_parts(send_near)
+    keep_near, far_x = together((keep_near, far_x))
     near = [keep_near[y] + far_x[y] for y in range(2)]
     near, got_near = together((near, got_near))
     near = [near[y] + got_near[y] for y in range(2)]
+    near, weights = together((near, weights))
     near_y = over_visit(near[1], 2)
-    part = near[0] + near_y
+    weights = [weights[x] + weight_depth[x] for x in range(2)]
+    weight_x = over_visit(weights[1], 1)
+    weight_own, near_own = together((weights[0], near[0]))
+    weights = [weight_own[y] + weight_x[y] for y in range(2)]
+    weight_y = over_visit(weights[1], 2)
+    part = near_own + near_y
     pieces = pieces_of(part)
-    weight_part, part = together((weight_part, part))
-    weight_sum = functools.reduce(jnp.add, weight_pieces, weight_part[0])
+    weight_own, part = together((weights[0], part))
+    weights = weight_own + weight_y
+    weight_pieces = [over_depth(weights[s], 2 * s) for s in range(1, depths // 2)]
     weighted_sum = functools.reduce(jnp.add, pieces, part[0])
+    weighted_sum, weights = together((weighted_sum, weights))
+    weight_sum = functools.reduce(jnp.add, weight_pieces, weights[0])
     return weighted_sum[None], weight_sum[None]
 
 

time: 56.9 us -> 56 us (0.984)
  waiting for transfers between devices: 14.6 us -> 13 us
  local copies, waits for them, and re-layouts: 0.08 us -> 1.51 us
  Pallas kernels: 22.8 us -> 21.6 us
    ppermute x4, waiting for transfers between devices: 8.1 us -> 6.13 us  [over_visit(): return lax.ppermute(value, 'visit', [(i, i ^ flip) for i in range(visits)])]
    pallas_call x1, Pallas kernels: 3.09 us -> 1.6 us  [sum_weights(): pl.pallas_call(weight_kernel, out_shape=(part, part), in_specs=[anywhere]...]
    unnamed x18 -> x16, local copies, waits for them, and re-layouts: 0.05 us -> 1.42 us
    ppermute x3 -> x5, starting transfers between devices: 0.66 us -> 1.66 us  [over_core(): return lax.ppermute(value, 'patch', [(i, i ^ 1) for i in range(owners)])]
    ppermute x3 -> x5, waiting for transfers between devices: 1.39 us -> 2.2 us  [over_core(): return lax.ppermute(value, 'patch', [(i, i ^ 1) for i in range(owners)])]
    add x5 -> x7, other arithmetic: 0.39 us -> 1.04 us  [the longest x1 0.65 us: on_device(): weighted_sum = functools.reduce(jnp.add, pieces, part[0])]
    broadcast_in_dim x2 -> x1, other arithmetic: 1.29 us -> 0.64 us  [on_device(): return (weighted_sum[None], weight_sum[None])]
    ppermute x6 -> x5, waiting for transfers between devices: 5.1 us -> 4.64 us  [over_depth(): return lax.ppermute(value, 'patch', pairs)]
  transfers between devices with their start and end apart: 13 -> 14, of which waited for: 6 -> 9; matrix products, arithmetic and copies ran while one was open for 2% -> 2% of each run, Pallas kernels for 35% -> 34%
where the time goes in v4:
time: 56 us; the launch traced here: 55.7 us
  Pallas kernels  21.6 us (39%)
  starting transfers between devices  16.2 us (29%)
  waiting for transfers between devices  13 us (23%)
  other arithmetic  1.85 us (3%)
  between operations  1.61 us (3%)
  local copies, waits for them, and re-layouts  1.51 us (3%)
    pallas_call x2, Pallas kernels, match(): pl.pallas_call(functools.partial(match_kernel, offset), out_shape=(part,...  19 us
    ppermute x5, starting transfers between devices, over_depth(): return lax.ppermute(value, 'patch', pairs)  8.12 us
    ppermute x4, starting transfers between devices, over_visit(): return lax.ppermute(value, 'visit', [(i, i ^ flip) for i in range(visits)])  6.41 us
    ppermute x4, waiting for transfers between devices, over_visit(): return lax.ppermute(value, 'visit', [(i, i ^ flip) for i in range(visits)])  6.13 us
    ppermute x5, waiting for transfers between devices, over_depth(): return lax.ppermute(value, 'patch', pairs)  4.64 us
    ppermute x5, waiting for transfers between devices, over_core(): return lax.ppermute(value, 'patch', [(i, i ^ 1) for i in range(owners)])  2.2 us
    ppermute x5, starting transfers between devices, over_core(): return lax.ppermute(value, 'patch', [(i, i ^ 1) for i in range(owners)])  1.66 us
    pallas_call x1, Pallas kernels, sum_weights(): pl.pallas_call(weight_kernel, out_shape=(part, part), in_specs=[anywhere]...  1.6 us
  transfers between devices with their start and end apart: 14, of which 9 were waited for; matrix products, arithmetic and copies ran while one was open for 2% of the time, Pallas kernels for 34%

profile of v4, /device:TPU:0, one launch (start us, length us, event | category | flops | bytes accessed | tf_op | source)
XLA Modules:
  0.0 55.7 jit_solution(413737209058884740)
XLA Ops:
  0.6 0.0 copy-start.1
  1.4 0.0 copy-start.3
  1.4 0.7 %copy-done.3 = f32[16,41]{1,0:T(8,128)S(1)} copy-done((f32[16,41]{1,0:T(8,128)S(1)}, f32[16,41]{1,0:T(8,128)}, u32[]{:S(2)}) %copy-start.3) | copy-done | bytes 2648
  2.1 0.0 copy-start.4
  2.1 0.7 %copy-done.4 = f32[16,41]{1,0:T(8,128)S(1)} copy-done((f32[16,41]{1,0:T(8,128)S(1)}, f32[16,41]{1,0:T(8,128)}, u32[]{:S(2)}) %copy-start.4) | copy-done | bytes 2648
  2.8 0.0 copy-start.5
  2.8 0.0 copy-start.6
  2.8 1.0 %shard_map.104 = (bf16[16,128,256]{2,1,0:T(8,128)(2,1)S(1)}, bf16[16,256,128]{2,1,0:T(8,128)(2,1)S(1)}) custom-call(f32[16,41]{1,0:T(8,128)S(1)} %copy-done.3, f32[16,41]{1,0:T(8,128)S(1)} %copy-done.4), custom_call_target="tpu_custom_call" | custom-call | flops 1000000000 | tf_op jit(solution)/shard_map/pallas_call | solution.py:177
  3.9 0.0 copy-start
  3.9 0.0 copy-start.2
  3.9 0.0 copy-start.7
  3.9 0.0 copy-done.1
  3.9 0.0 copy-done.5
  3.9 0.0 copy-done.6
  3.9 1.6 %shard_map.105 = (f32[2,2,2,2,64,256]{5,4,3,2,1,0:T(8,128)S(1)}, f32[2,2,2,2,64,256]{5,4,3,2,1,0:T(8,128)S(1)}) custom-call(s32[32]{0:T(128)S(1)} %bitcast.64, s32[32]{0:T(128)S(1)} %bitcast.67, s32[1]{0:T(128)} %bitcast.54.count_in, f32[32,128,128]{2,1,0:T(8,128)S(1)} %bitcast.59), custom_call_target="tpu_custom_call" | custom-call | flops 1000000000 | tf_op jit(solution)/shard_map/pallas_call | solution.py:114
  5.6 0.5 collective-permute-start.2
  6.1 0.0 copy-done
  6.1 0.0 copy-done.2
  6.1 0.0 copy-done.7
  6.1 9.5 %shard_map.106 = (f32[2,4,64,256]{3,2,1,0:T(8,128)S(1)}, f32[2,4,64,256]{3,2,1,0:T(8,128)S(1)}) custom-call(s32[32]{0:T(128)S(1)} %bitcast.65, s32[32]{0:T(128)S(1)} %bitcast.68, s32[32]{0:T(128)S(1)} %bitcast.70, s32[1]{0:T(128)} %bitcast.55.count_in, f32[32,128,128]{2,1,0:T(8,128)S(1)} %bitcast.57, f32[32,128,128]{2,1,0:T(8,128)S(1)} %bitcast.60, ...), custom_call_target="tpu_custom_call" | custom-call | flops 10737418240 | bytes 10000000 | tf_op jit(solution)/shard_map/pallas_call | solution.py:305
  15.6 0.1 collective-permute-start
  15.8 0.4 collective-permute-start.1
  16.2 1.0 %collective-permute-done = f32[4,64,256]{2,1,0:T(8,128)S(1)} collective-permute-done((f32[4,64,256]{2,1,0:T(8,128)S(1)}, f32[4,64,256]{2,1,0:T(8,128)S(1)}, u32[]{:S(2)}, u32[]{:S(2)}) %collective-permute-start) | collective-permute-done | bytes 262176 | tf_op jit(solution)/shard_map/ppermute | solution.py:343
  17.2 0.4 collective-permute-done.1
  17.6 0.1 maximum_add_fusion
  17.7 0.0 collective-permute-done.2
  17.7 2.7 %collective-permute-start.3 = (f32[2,4,64,256]{3,2,1,0:T(8,128)S(1)}, f32[2,4,64,256]{3,2,1,0:T(8,128)S(1)}, u32[]{:S(2)}, u32[]{:S(2)}) collective-permute-start(f32[2,4,64,256]{3,2,1,0:T(8,128)S(1)} %maximum_add_fusion), channel_id=1, source_target_pairs={{0,8},{8,0},{16,24},{24,16},{1,9},{9,1},{17,25},{25,17},{2,10},{10... | collective-permute-start | bytes 1572872 | tf_op jit(solution)/shard_map/ppermute | solution.py:346
  20.4 0.1 add_bitcast_fusion
  20.5 1.7 %collective-permute-start.6 = (f32[2,2,2,64,256]{4,3,2,1,0:T(8,128)S(1)}, f32[2,2,2,64,256]{4,3,2,1,0:T(8,128)S(1)}, u32[]{:S(2)}, u32[]{:S(2)}) collective-permute-start(f32[2,2,2,64,256]{4,3,2,1,0:T(8,128)S(1)} %get-tuple-element.63), channel_id=1, source_target_pairs={{0,2},{1,3},{2,0},{3,1},{4,6},{5,7},{6,4},{7,5},{8,10},{9,11},{10,... | collective-permute-start | bytes 1572872 | tf_op jit(solution)/shard_map/ppermute | solution.py:353
  22.2 9.5 %shard_map.107 = (f32[2,4,64,256]{3,2,1,0:T(8,128)S(1)}, f32[2,4,64,256]{3,2,1,0:T(8,128)S(1)}) custom-call(s32[32]{0:T(128)S(1)} %bitcast.66, s32[32]{0:T(128)S(1)} %bitcast.69, s32[32]{0:T(128)S(1)} %bitcast.71, s32[1]{0:T(128)} %bitcast.56.count_in, f32[32,128,128]{2,1,0:T(8,128)S(1)} %bitcast.58, f32[32,128,128]{2,1,0:T(8,128)S(1)} %bitcast.61, ...), custom_call_target="tpu_custom_call" | custom-call | flops 10737418240 | bytes 10000000 | tf_op jit(solution)/shard_map/pallas_call | solution.py:305
  31.7 0.1 collective-permute-start.5
  31.8 0.5 collective-permute-start.4
  32.3 0.5 collective-permute-done.3
  32.8 0.1 add_bitcast_fusion.2
  32.9 0.4 collective-permute-done.5
  33.3 0.4 collective-permute-done.4
  33.8 0.7 %collective-permute-done.6 = f32[2,2,2,64,256]{4,3,2,1,0:T(8,128)S(1)} collective-permute-done((f32[2,2,2,64,256]{4,3,2,1,0:T(8,128)S(1)}, f32[2,2,2,64,256]{4,3,2,1,0:T(8,128)S(1)}, u32[]{:S(2)}, u32[]{:S(2)}) %collective-permute-start.6) | collective-permute-done | bytes 524320 | tf_op jit(solution)/shard_map/ppermute | solution.py:353
  34.5 0.1 fusion
  34.6 0.4 collective-permute-start.7
  35.0 1.7 %collective-permute-start.8 = (f32[4,64,256]{2,1,0:T(8,128)S(1)}, f32[4,64,256]{2,1,0:T(8,128)S(1)}, u32[]{:S(2)}, u32[]{:S(2)}) collective-permute-start(f32[4,64,256]{2,1,0:T(8,128)S(1)} %add.85), channel_id=1, source_target_pairs={{0,16},{8,24},{16,0},{24,8},{1,17},{9,25},{17,1},{25,9},{2,18},{10... | collective-permute-start | bytes 786440 | tf_op jit(solution)/shard_map/ppermute | solution.py:346
  36.7 5.6 %collective-permute-done.7 = f32[2,2,64,256]{3,2,1,0:T(8,128)S(1)} collective-permute-done((f32[2,2,64,256]{3,2,1,0:T(8,128)S(1)}, f32[2,2,64,256]{3,2,1,0:T(8,128)S(1)}, u32[]{:S(2)}, u32[]{:S(2)}) %collective-permute-start.7) | collective-permute-done | bytes 262176 | tf_op jit(solution)/shard_map/ppermute | solution.py:346
  42.4 1.6 %collective-permute-start.12 = (f32[2,64,256]{2,1,0:T(8,128)S(1)}, f32[2,64,256]{2,1,0:T(8,128)S(1)}, u32[]{:S(2)}, u32[]{:S(2)}) collective-permute-start(f32[2,64,256]{2,1,0:T(8,128)S(1)} %get-tuple-element.78), channel_id=1, source_target_pairs={{0,16},{8,24},{16,0},{24,8},{1,17},{9,25},{17,1},{25,9},{2,18},{10... | collective-permute-start | bytes 393224 | tf_op jit(solution)/shard_map/ppermute | solution.py:346
  43.9 0.0 collective-permute-done.8
  44.0 3.5 %collective-permute-start.9 = (f32[64,256]{1,0:T(8,128)S(1)}, f32[64,256]{1,0:T(8,128)S(1)}, u32[]{:S(2)}, u32[]{:S(2)}) collective-permute-start(f32[64,256]{1,0:T(8,128)S(1)} %get-tuple-element.84), channel_id=1, source_target_pairs={{0,6},{1,7},{2,4},{3,5},{4,2},{5,3},{6,0},{7,1},{8,14},{9,15},{10,... | collective-permute-start | bytes 196616 | tf_op jit(solution)/shard_map/ppermute | solution.py:353
  47.5 0.0 collective-permute-start.11
  47.5 1.0 %collective-permute-start.10 = (f32[64,256]{1,0:T(8,128)S(1)}, f32[64,256]{1,0:T(8,128)S(1)}, u32[]{:S(2)}, u32[]{:S(2)}) collective-permute-start(f32[64,256]{1,0:T(8,128)S(1)} %get-tuple-element.86), channel_id=1, source_target_pairs={{0,2},{1,3},{2,0},{3,1},{4,6},{5,7},{6,4},{7,5},{8,10},{9,11},{10,... | collective-permute-start | bytes 196616 | tf_op jit(solution)/shard_map/ppermute | solution.py:353
  48.5 0.0 collective-permute-done.12
  48.5 2.0 %collective-permute-start.13 = (f32[64,256]{1,0:T(8,128)S(1)}, f32[64,256]{1,0:T(8,128)S(1)}, u32[]{:S(2)}, u32[]{:S(2)}) collective-permute-start(f32[64,256]{1,0:T(8,128)S(1)} %slice_bitcast_fusion.4), channel_id=1, source_target_pairs={{0,4},{1,5},{2,6},{3,7},{4,0},{5,1},{6,2},{7,3},{8,12},{9,13},{10,... | collective-permute-start | bytes 196616 | tf_op jit(solution)/shard_map/ppermute | solution.py:353
  50.5 0.0 collective-permute-done.9
  50.5 3.2 %collective-permute-done.11 = f32[64,256]{1,0:T(8,128)S(1)} collective-permute-done((f32[64,256]{1,0:T(8,128)S(1)}, f32[64,256]{1,0:T(8,128)S(1)}, u32[]{:S(2)}, u32[]{:S(2)}) %collective-permute-start.11) | collective-permute-done | bytes 65568 | tf_op jit(solution)/shard_map/ppermute | solution.py:353
  53.7 0.0 collective-permute-done.10
  53.7 0.6 %fusion.6 = f32[64,256]{1,0:T(8,128)} fusion(f32[64,256]{1,0:T(8,128)S(1)} %collective-permute-done.11, f32[64,256]{1,0:T(8,128)S(1)} %collective-permute-done.10, f32[64,256]{1,0:T(8,128)S(1)} %collective-permute-done.9, f32[4,64,256]{2,1,0:T(8,128)S(1)} %add.92), kind=kLoop, calls=%fused_computation.25 | loop fusion | flops 49152 | bytes 327680 | tf_op jit(solution)/shard_map/add | solution.py:399
  54.3 0.8 %collective-permute-done.13 = f32[64,256]{1,0:T(8,128)S(1)} collective-permute-done((f32[64,256]{1,0:T(8,128)S(1)}, f32[64,256]{1,0:T(8,128)S(1)}, u32[]{:S(2)}, u32[]{:S(2)}) %collective-permute-start.13) | collective-permute-done | bytes 65568 | tf_op jit(solution)/shard_map/ppermute | solution.py:353
  55.1 0.6 %fusion.4 = f32[1,64,256]{2,1,0:T(8,128)} fusion(f32[64,256]{1,0:T(8,128)S(1)} %collective-permute-done.13, f32[2,64,256]{2,1,0:T(8,128)S(1)} %add.98), kind=kLoop, calls=%fused_computation.22 | loop fusion | flops 16384 | bytes 196608 | tf_op jit(solution)/shard_map/broadcast_in_dim | solution.py:402
  (9 shorter events, 0.3 us)
Async XLA Ops:
  0.6 3.3 %copy-start.1 = (f32[1,1,32,128,128]{4,3,2,1,0:T(8,128)S(1)}, f32[1,1,32,128,128]{4,3,2,1,0:T(8,128)}, u32[]{:S(2)}) copy-start(f32[1,1,32,128,128]{4,3,2,1,0:T(8,128)} %param.10) | copy-start | bytes 6291460
  1.4 0.7 %copy-start.3 = (f32[16,41]{1,0:T(8,128)S(1)}, f32[16,41]{1,0:T(8,128)}, u32[]{:S(2)}) copy-start(f32[16,41]{1,0:T(8,128)} %row_taps_in.1) | copy-start | bytes 7876
  2.1 0.7 %copy-start.4 = (f32[16,41]{1,0:T(8,128)S(1)}, f32[16,41]{1,0:T(8,128)}, u32[]{:S(2)}) copy-start(f32[16,41]{1,0:T(8,128)} %col_taps_in.1) | copy-start | bytes 7876
  2.8 1.1 %copy-start.5 = (s32[1,1,32]{2,1,0:T(1,128)S(1)}, s32[1,1,32]{2,1,0:T(1,128)}, u32[]{:S(2)}) copy-start(s32[1,1,32]{2,1,0:T(1,128)} %param.11) | copy-start | bytes 388
  2.8 1.1 %copy-start.6 = (s32[1,1,32]{2,1,0:T(1,128)S(1)}, s32[1,1,32]{2,1,0:T(1,128)}, u32[]{:S(2)}) copy-start(s32[1,1,32]{2,1,0:T(1,128)} %param.12) | copy-start | bytes 388
  3.9 2.2 %copy-start = (f32[1,1,32,128,128]{4,3,2,1,0:T(8,128)S(1)}, f32[1,1,32,128,128]{4,3,2,1,0:T(8,128)}, u32[]{:S(2)}) copy-start(f32[1,1,32,128,128]{4,3,2,1,0:T(8,128)} %param.9) | copy-start | bytes 6291460
  3.9 2.2 %copy-start.2 = (f32[800,16,6]{0,1,2:T(8,128)S(1)}, f32[800,16,6]{0,1,2:T(8,128)}, u32[]{:S(2)}) copy-start(f32[800,16,6]{0,1,2:T(8,128)} %param.15) | copy-start | bytes 921604
  3.9 2.2 %copy-start.7 = (s32[1,1,32]{2,1,0:T(1,128)S(1)}, s32[1,1,32]{2,1,0:T(1,128)}, u32[]{:S(2)}) copy-start(s32[1,1,32]{2,1,0:T(1,128)} %param.13) | copy-start | bytes 388
  5.6 12.1 %collective-permute-start.2 = (f32[2,2,2,2,64,256]{5,4,3,2,1,0:T(8,128)S(1)}, f32[2,2,2,2,64,256]{5,4,3,2,1,0:T(8,128)S(1)}, u32[]{:S(2)}, u32[]{:S(2)}) collective-permute-start(f32[2,2,2,2,64,256]{5,4,3,2,1,0:T(8,128)S(1)} %get-tuple-element.47), channel_id=1, source_target_pairs={{0,1},{1,0},{2,3},{3,2},{4,5},{5,4},{6,7},{7,6},{8,9},{9,8},{10,11... | collective-permute-start | bytes 3145736 | tf_op jit(solution)/shard_map/ppermute | solution.py:343
  15.6 1.6 %collective-permute-start = (f32[4,64,256]{2,1,0:T(8,128)S(1)}, f32[4,64,256]{2,1,0:T(8,128)S(1)}, u32[]{:S(2)}, u32[]{:S(2)}) collective-permute-start(f32[4,64,256]{2,1,0:T(8,128)S(1)} %get-tuple-element.82), channel_id=1, source_target_pairs={{0,1},{1,0},{2,3},{3,2},{4,5},{5,4},{6,7},{7,6},{8,9},{9,8},{10,11... | collective-permute-start | bytes 786440 | tf_op jit(solution)/shard_map/ppermute | solution.py:343
  15.8 1.8 %collective-permute-start.1 = (f32[4,64,256]{2,1,0:T(8,128)S(1)}, f32[4,64,256]{2,1,0:T(8,128)S(1)}, u32[]{:S(2)}, u32[]{:S(2)}) collective-permute-start(f32[4,64,256]{2,1,0:T(8,128)S(1)} %get-tuple-element.83), channel_id=1, source_target_pairs={{0,1},{1,0},{2,3},{3,2},{4,5},{5,4},{6,7},{7,6},{8,9},{9,8},{10,11... | collective-permute-start | bytes 786440 | tf_op jit(solution)/shard_map/ppermute | solution.py:343
  17.7 15.2 %collective-permute-start.3 = (f32[2,4,64,256]{3,2,1,0:T(8,128)S(1)}, f32[2,4,64,256]{3,2,1,0:T(8,128)S(1)}, u32[]{:S(2)}, u32[]{:S(2)}) collective-permute-start(f32[2,4,64,256]{3,2,1,0:T(8,128)S(1)} %maximum_add_fusion), channel_id=1, source_target_pairs={{0,8},{8,0},{16,24},{24,16},{1,9},{9,1},{17,25},{25,17},{2,10},{10... | collective-permute-start | bytes 1572872 | tf_op jit(solution)/shard_map/ppermute | solution.py:346
  20.5 14.0 %collective-permute-start.6 = (f32[2,2,2,64,256]{4,3,2,1,0:T(8,128)S(1)}, f32[2,2,2,64,256]{4,3,2,1,0:T(8,128)S(1)}, u32[]{:S(2)}, u32[]{:S(2)}) collective-permute-start(f32[2,2,2,64,256]{4,3,2,1,0:T(8,128)S(1)} %get-tuple-element.63), channel_id=1, source_target_pairs={{0,2},{1,3},{2,0},{3,1},{4,6},{5,7},{6,4},{7,5},{8,10},{9,11},{10,... | collective-permute-start | bytes 1572872 | tf_op jit(solution)/shard_map/ppermute | solution.py:353
  31.7 1.6 %collective-permute-start.5 = (f32[4,64,256]{2,1,0:T(8,128)S(1)}, f32[4,64,256]{2,1,0:T(8,128)S(1)}, u32[]{:S(2)}, u32[]{:S(2)}) collective-permute-start(f32[4,64,256]{2,1,0:T(8,128)S(1)} %get-tuple-element.80), channel_id=1, source_target_pairs={{0,1},{1,0},{2,3},{3,2},{4,5},{5,4},{6,7},{7,6},{8,9},{9,8},{10,11... | collective-permute-start | bytes 786440 | tf_op jit(solution)/shard_map/ppermute | solution.py:343
  31.8 1.9 %collective-permute-start.4 = (f32[4,64,256]{2,1,0:T(8,128)S(1)}, f32[4,64,256]{2,1,0:T(8,128)S(1)}, u32[]{:S(2)}, u32[]{:S(2)}) collective-permute-start(f32[4,64,256]{2,1,0:T(8,128)S(1)} %get-tuple-element.81), channel_id=1, source_target_pairs={{0,1},{1,0},{2,3},{3,2},{4,5},{5,4},{6,7},{7,6},{8,9},{9,8},{10,11... | collective-permute-start | bytes 786440 | tf_op jit(solution)/shard_map/ppermute | solution.py:343
  34.6 7.7 %collective-permute-start.7 = (f32[2,2,64,256]{3,2,1,0:T(8,128)S(1)}, f32[2,2,64,256]{3,2,1,0:T(8,128)S(1)}, u32[]{:S(2)}, u32[]{:S(2)}) collective-permute-start(f32[2,2,64,256]{3,2,1,0:T(8,128)S(1)} %get-tuple-element.74), channel_id=1, source_target_pairs={{0,8},{8,0},{16,24},{24,16},{1,9},{9,1},{17,25},{25,17},{2,10},{10... | collective-permute-start | bytes 786440 | tf_op jit(solution)/shard_map/ppermute | solution.py:346
  35.0 8.9 %collective-permute-start.8 = (f32[4,64,256]{2,1,0:T(8,128)S(1)}, f32[4,64,256]{2,1,0:T(8,128)S(1)}, u32[]{:S(2)}, u32[]{:S(2)}) collective-permute-start(f32[4,64,256]{2,1,0:T(8,128)S(1)} %add.85), channel_id=1, source_target_pairs={{0,16},{8,24},{16,0},{24,8},{1,17},{9,25},{17,1},{25,9},{2,18},{10... | collective-permute-start | bytes 786440 | tf_op jit(solution)/shard_map/ppermute | solution.py:346
  42.4 6.1 %collective-permute-start.12 = (f32[2,64,256]{2,1,0:T(8,128)S(1)}, f32[2,64,256]{2,1,0:T(8,128)S(1)}, u32[]{:S(2)}, u32[]{:S(2)}) collective-permute-start(f32[2,64,256]{2,1,0:T(8,128)S(1)} %get-tuple-element.78), channel_id=1, source_target_pairs={{0,16},{8,24},{16,0},{24,8},{1,17},{9,25},{17,1},{25,9},{2,18},{10... | collective-permute-start | bytes 393224 | tf_op jit(solution)/shard_map/ppermute | solution.py:346
  44.0 6.5 %collective-permute-start.9 = (f32[64,256]{1,0:T(8,128)S(1)}, f32[64,256]{1,0:T(8,128)S(1)}, u32[]{:S(2)}, u32[]{:S(2)}) collective-permute-start(f32[64,256]{1,0:T(8,128)S(1)} %get-tuple-element.84), channel_id=1, source_target_pairs={{0,6},{1,7},{2,4},{3,5},{4,2},{5,3},{6,0},{7,1},{8,14},{9,15},{10,... | collective-permute-start | bytes 196616 | tf_op jit(solution)/shard_map/ppermute | solution.py:353
  47.5 6.2 %collective-permute-start.11 = (f32[64,256]{1,0:T(8,128)S(1)}, f32[64,256]{1,0:T(8,128)S(1)}, u32[]{:S(2)}, u32[]{:S(2)}) collective-permute-start(f32[64,256]{1,0:T(8,128)S(1)} %get-tuple-element.85), channel_id=1, source_target_pairs={{0,4},{1,5},{2,6},{3,7},{4,0},{5,1},{6,2},{7,3},{8,12},{9,13},{10,... | collective-permute-start | bytes 196616 | tf_op jit(solution)/shard_map/ppermute | solution.py:353
  47.5 6.2 %collective-permute-start.10 = (f32[64,256]{1,0:T(8,128)S(1)}, f32[64,256]{1,0:T(8,128)S(1)}, u32[]{:S(2)}, u32[]{:S(2)}) collective-permute-start(f32[64,256]{1,0:T(8,128)S(1)} %get-tuple-element.86), channel_id=1, source_target_pairs={{0,2},{1,3},{2,0},{3,1},{4,6},{5,7},{6,4},{7,5},{8,10},{9,11},{10,... | collective-permute-start | bytes 196616 | tf_op jit(solution)/shard_map/ppermute | solution.py:353
  48.5 6.6 %collective-permute-start.13 = (f32[64,256]{1,0:T(8,128)S(1)}, f32[64,256]{1,0:T(8,128)S(1)}, u32[]{:S(2)}, u32[]{:S(2)}) collective-permute-start(f32[64,256]{1,0:T(8,128)S(1)} %slice_bitcast_fusion.4), channel_id=1, source_target_pairs={{0,4},{1,5},{2,6},{3,7},{4,0},{5,1},{6,2},{7,3},{8,12},{9,13},{10,... | collective-permute-start | bytes 196616 | tf_op jit(solution)/shard_map/ppermute | solution.py:353

commit v5 on v4

--- a/solution.py
+++ b/solution.py
@@ -13,7 +13,7 @@
 SHARE = 1.0 / 32.0
 KEEP = 1.0 - SHARE
 VMEM_BYTES = 40 * 2**20
-GROUP_ROWS = 512
+GROUP_ROWS = 1024
 
 
 def split_left(value):

time: 56 us -> 54.3 us (0.970)
  Pallas kernels: 21.6 us -> 20.3 us
  waiting for transfers between devices: 13 us -> 12.3 us
    pallas_call x2, Pallas kernels: 19 us -> 17.6 us  [match(): pl.pallas_call(functools.partial(match_kernel, offset), out_shape=(part,...]
    ppermute x5, waiting for transfers between devices: 2.2 us -> 1.56 us  [over_core(): return lax.ppermute(value, 'patch', [(i, i ^ 1) for i in range(owners)])]
  transfers between devices with their start and end apart: 14 -> 14, of which waited for: 9 -> 8; matrix products, arithmetic and copies ran while one was open for 2% -> 2% of each run, Pallas kernels for 34% -> 33%
where the time goes in v5:
time: 54.3 us; the launch traced here: 54 us
  Pallas kernels  20.3 us (37%)
  starting transfers between devices  16.4 us (30%)
  waiting for transfers between devices  12.3 us (23%)
  other arithmetic  1.85 us (3%)
  between operations  1.62 us (3%)
  local copies, waits for them, and re-layouts  1.51 us (3%)
    pallas_call x2, Pallas kernels, match(): pl.pallas_call(functools.partial(match_kernel, offset), out_shape=(part,...  17.6 us
    ppermute x5, starting transfers between devices, over_depth(): return lax.ppermute(value, 'patch', pairs)  8.36 us
    ppermute x4, waiting for transfers between devices, over_visit(): return lax.ppermute(value, 'visit', [(i, i ^ flip) for i in range(visits)])  6.54 us
    ppermute x4, starting transfers between devices, over_visit(): return lax.ppermute(value, 'visit', [(i, i ^ flip) for i in range(visits)])  6.41 us
    ppermute x5, waiting for transfers between devices, over_depth(): return lax.ppermute(value, 'patch', pairs)  4.24 us
    ppermute x5, starting transfers between devices, over_core(): return lax.ppermute(value, 'patch', [(i, i ^ 1) for i in range(owners)])  1.66 us
    pallas_call x1, Pallas kernels, sum_weights(): pl.pallas_call(weight_kernel, out_shape=(part, part), in_specs=[anywhere]...  1.6 us
    ppermute x5, waiting for transfers between devices, over_core(): return lax.ppermute(value, 'patch', [(i, i ^ 1) for i in range(owners)])  1.56 us
  transfers between devices with their start and end apart: 14, of which 8 were waited for; matrix products, arithmetic and copies ran while one was open for 2% of the time, Pallas kernels for 33%

profile of v5, /device:TPU:0, one launch (start us, length us, event | category | flops | bytes accessed | tf_op | source)
XLA Modules:
  0.0 54.0 jit_solution(2264377864783234447)
XLA Ops:
  0.6 0.0 copy-start.1
  1.4 0.0 copy-start.3
  1.4 0.7 %copy-done.3 = f32[16,41]{1,0:T(8,128)S(1)} copy-done((f32[16,41]{1,0:T(8,128)S(1)}, f32[16,41]{1,0:T(8,128)}, u32[]{:S(2)}) %copy-start.3) | copy-done | bytes 2648
  2.1 0.0 copy-start.4
  2.1 0.7 %copy-done.4 = f32[16,41]{1,0:T(8,128)S(1)} copy-done((f32[16,41]{1,0:T(8,128)S(1)}, f32[16,41]{1,0:T(8,128)}, u32[]{:S(2)}) %copy-start.4) | copy-done | bytes 2648
  2.8 0.0 copy-start.5
  2.8 0.0 copy-start.6
  2.8 1.0 %shard_map.104 = (bf16[16,128,256]{2,1,0:T(8,128)(2,1)S(1)}, bf16[16,256,128]{2,1,0:T(8,128)(2,1)S(1)}) custom-call(f32[16,41]{1,0:T(8,128)S(1)} %copy-done.3, f32[16,41]{1,0:T(8,128)S(1)} %copy-done.4), custom_call_target="tpu_custom_call" | custom-call | flops 1000000000 | tf_op jit(solution)/shard_map/pallas_call | solution.py:177
  3.9 0.0 copy-start
  3.9 0.0 copy-start.2
  3.9 0.0 copy-start.7
  3.9 0.0 copy-done.1
  3.9 0.0 copy-done.5
  3.9 0.0 copy-done.6
  3.9 1.6 %shard_map.105 = (f32[2,2,2,2,64,256]{5,4,3,2,1,0:T(8,128)S(1)}, f32[2,2,2,2,64,256]{5,4,3,2,1,0:T(8,128)S(1)}) custom-call(s32[32]{0:T(128)S(1)} %bitcast.64, s32[32]{0:T(128)S(1)} %bitcast.67, s32[1]{0:T(128)} %bitcast.54.count_in, f32[32,128,128]{2,1,0:T(8,128)S(1)} %bitcast.59), custom_call_target="tpu_custom_call" | custom-call | flops 1000000000 | tf_op jit(solution)/shard_map/pallas_call | solution.py:114
  5.6 0.5 collective-permute-start.2
  6.1 0.0 copy-done
  6.1 0.0 copy-done.2
  6.1 0.0 copy-done.7
  6.1 8.8 %shard_map.106 = (f32[2,4,64,256]{3,2,1,0:T(8,128)S(1)}, f32[2,4,64,256]{3,2,1,0:T(8,128)S(1)}) custom-call(s32[32]{0:T(128)S(1)} %bitcast.65, s32[32]{0:T(128)S(1)} %bitcast.68, s32[32]{0:T(128)S(1)} %bitcast.70, s32[1]{0:T(128)} %bitcast.55.count_in, f32[32,128,128]{2,1,0:T(8,128)S(1)} %bitcast.57, f32[32,128,128]{2,1,0:T(8,128)S(1)} %bitcast.60, ...), custom_call_target="tpu_custom_call" | custom-call | flops 10737418240 | bytes 10000000 | tf_op jit(solution)/shard_map/pallas_call | solution.py:305
  15.0 0.1 collective-permute-start
  15.1 0.5 collective-permute-start.1
  15.5 1.0 %collective-permute-done = f32[4,64,256]{2,1,0:T(8,128)S(1)} collective-permute-done((f32[4,64,256]{2,1,0:T(8,128)S(1)}, f32[4,64,256]{2,1,0:T(8,128)S(1)}, u32[]{:S(2)}, u32[]{:S(2)}) %collective-permute-start) | collective-permute-done | bytes 262176 | tf_op jit(solution)/shard_map/ppermute | solution.py:343
  16.6 0.4 collective-permute-done.1
  16.9 0.1 maximum_add_fusion
  17.0 0.0 collective-permute-done.2
  17.0 2.7 %collective-permute-start.3 = (f32[2,4,64,256]{3,2,1,0:T(8,128)S(1)}, f32[2,4,64,256]{3,2,1,0:T(8,128)S(1)}, u32[]{:S(2)}, u32[]{:S(2)}) collective-permute-start(f32[2,4,64,256]{3,2,1,0:T(8,128)S(1)} %maximum_add_fusion), channel_id=1, source_target_pairs={{0,8},{8,0},{16,24},{24,16},{1,9},{9,1},{17,25},{25,17},{2,10},{10... | collective-permute-start | bytes 1572872 | tf_op jit(solution)/shard_map/ppermute | solution.py:346
  19.7 0.1 add_bitcast_fusion
  19.8 1.7 %collective-permute-start.6 = (f32[2,2,2,64,256]{4,3,2,1,0:T(8,128)S(1)}, f32[2,2,2,64,256]{4,3,2,1,0:T(8,128)S(1)}, u32[]{:S(2)}, u32[]{:S(2)}) collective-permute-start(f32[2,2,2,64,256]{4,3,2,1,0:T(8,128)S(1)} %get-tuple-element.63), channel_id=1, source_target_pairs={{0,2},{1,3},{2,0},{3,1},{4,6},{5,7},{6,4},{7,5},{8,10},{9,11},{10,... | collective-permute-start | bytes 1572872 | tf_op jit(solution)/shard_map/ppermute | solution.py:353
  21.5 8.8 %shard_map.107 = (f32[2,4,64,256]{3,2,1,0:T(8,128)S(1)}, f32[2,4,64,256]{3,2,1,0:T(8,128)S(1)}) custom-call(s32[32]{0:T(128)S(1)} %bitcast.66, s32[32]{0:T(128)S(1)} %bitcast.69, s32[32]{0:T(128)S(1)} %bitcast.71, s32[1]{0:T(128)} %bitcast.56.count_in, f32[32,128,128]{2,1,0:T(8,128)S(1)} %bitcast.58, f32[32,128,128]{2,1,0:T(8,128)S(1)} %bitcast.61, ...), custom_call_target="tpu_custom_call" | custom-call | flops 10737418240 | bytes 10000000 | tf_op jit(solution)/shard_map/pallas_call | solution.py:305
  30.4 0.1 collective-permute-start.5
  30.5 0.5 collective-permute-start.4
  31.0 1.2 %collective-permute-done.3 = f32[2,4,64,256]{3,2,1,0:T(8,128)S(1)} collective-permute-done((f32[2,4,64,256]{3,2,1,0:T(8,128)S(1)}, f32[2,4,64,256]{3,2,1,0:T(8,128)S(1)}, u32[]{:S(2)}, u32[]{:S(2)}) %collective-permute-start.3) | collective-permute-done | bytes 524320 | tf_op jit(solution)/shard_map/ppermute | solution.py:346
  32.1 0.1 add_bitcast_fusion.2
  32.2 0.0 collective-permute-done.5
  32.2 0.2 collective-permute-done.4
  32.5 1.3 %collective-permute-done.6 = f32[2,2,2,64,256]{4,3,2,1,0:T(8,128)S(1)} collective-permute-done((f32[2,2,2,64,256]{4,3,2,1,0:T(8,128)S(1)}, f32[2,2,2,64,256]{4,3,2,1,0:T(8,128)S(1)}, u32[]{:S(2)}, u32[]{:S(2)}) %collective-permute-start.6) | collective-permute-done | bytes 524320 | tf_op jit(solution)/shard_map/ppermute | solution.py:353
  33.8 0.1 fusion
  33.9 0.5 collective-permute-start.7
  34.4 1.7 %collective-permute-start.8 = (f32[4,64,256]{2,1,0:T(8,128)S(1)}, f32[4,64,256]{2,1,0:T(8,128)S(1)}, u32[]{:S(2)}, u32[]{:S(2)}) collective-permute-start(f32[4,64,256]{2,1,0:T(8,128)S(1)} %add.85), channel_id=1, source_target_pairs={{0,16},{8,24},{16,0},{24,8},{1,17},{9,25},{17,1},{25,9},{2,18},{10... | collective-permute-start | bytes 786440 | tf_op jit(solution)/shard_map/ppermute | solution.py:346
  36.0 5.4 %collective-permute-done.7 = f32[2,2,64,256]{3,2,1,0:T(8,128)S(1)} collective-permute-done((f32[2,2,64,256]{3,2,1,0:T(8,128)S(1)}, f32[2,2,64,256]{3,2,1,0:T(8,128)S(1)}, u32[]{:S(2)}, u32[]{:S(2)}) %collective-permute-start.7) | collective-permute-done | bytes 262176 | tf_op jit(solution)/shard_map/ppermute | solution.py:346
  41.4 1.6 %collective-permute-start.12 = (f32[2,64,256]{2,1,0:T(8,128)S(1)}, f32[2,64,256]{2,1,0:T(8,128)S(1)}, u32[]{:S(2)}, u32[]{:S(2)}) collective-permute-start(f32[2,64,256]{2,1,0:T(8,128)S(1)} %get-tuple-element.78), channel_id=1, source_target_pairs={{0,16},{8,24},{16,0},{24,8},{1,17},{9,25},{17,1},{25,9},{2,18},{10... | collective-permute-start | bytes 393224 | tf_op jit(solution)/shard_map/ppermute | solution.py:346
  43.1 0.0 collective-permute-done.8
  43.1 3.7 %collective-permute-start.9 = (f32[64,256]{1,0:T(8,128)S(1)}, f32[64,256]{1,0:T(8,128)S(1)}, u32[]{:S(2)}, u32[]{:S(2)}) collective-permute-start(f32[64,256]{1,0:T(8,128)S(1)} %get-tuple-element.84), channel_id=1, source_target_pairs={{0,6},{1,7},{2,4},{3,5},{4,2},{5,3},{6,0},{7,1},{8,14},{9,15},{10,... | collective-permute-start | bytes 196616 | tf_op jit(solution)/shard_map/ppermute | solution.py:353
  46.8 0.0 collective-permute-start.11
  46.8 0.8 %collective-permute-start.10 = (f32[64,256]{1,0:T(8,128)S(1)}, f32[64,256]{1,0:T(8,128)S(1)}, u32[]{:S(2)}, u32[]{:S(2)}) collective-permute-start(f32[64,256]{1,0:T(8,128)S(1)} %get-tuple-element.86), channel_id=1, source_target_pairs={{0,2},{1,3},{2,0},{3,1},{4,6},{5,7},{6,4},{7,5},{8,10},{9,11},{10,... | collective-permute-start | bytes 196616 | tf_op jit(solution)/shard_map/ppermute | solution.py:353
  47.6 0.0 collective-permute-done.12
  47.6 2.2 %collective-permute-start.13 = (f32[64,256]{1,0:T(8,128)S(1)}, f32[64,256]{1,0:T(8,128)S(1)}, u32[]{:S(2)}, u32[]{:S(2)}) collective-permute-start(f32[64,256]{1,0:T(8,128)S(1)} %slice_bitcast_fusion.4), channel_id=1, source_target_pairs={{0,4},{1,5},{2,6},{3,7},{4,0},{5,1},{6,2},{7,3},{8,12},{9,13},{10,... | collective-permute-start | bytes 196616 | tf_op jit(solution)/shard_map/ppermute | solution.py:353
  49.8 0.0 collective-permute-done.9
  49.8 2.9 %collective-permute-done.11 = f32[64,256]{1,0:T(8,128)S(1)} collective-permute-done((f32[64,256]{1,0:T(8,128)S(1)}, f32[64,256]{1,0:T(8,128)S(1)}, u32[]{:S(2)}, u32[]{:S(2)}) %collective-permute-start.11) | collective-permute-done | bytes 65568 | tf_op jit(solution)/shard_map/ppermute | solution.py:353
  52.7 0.0 collective-permute-done.10
  52.7 0.6 %fusion.6 = f32[64,256]{1,0:T(8,128)} fusion(f32[64,256]{1,0:T(8,128)S(1)} %collective-permute-done.11, f32[64,256]{1,0:T(8,128)S(1)} %collective-permute-done.10, f32[64,256]{1,0:T(8,128)S(1)} %collective-permute-done.9, f32[4,64,256]{2,1,0:T(8,128)S(1)} %add.92), kind=kLoop, calls=%fused_computation.25 | loop fusion | flops 49152 | bytes 327680 | tf_op jit(solution)/shard_map/add | solution.py:399
  53.4 0.1 collective-permute-done.13
  53.4 0.6 %fusion.4 = f32[1,64,256]{2,1,0:T(8,128)} fusion(f32[64,256]{1,0:T(8,128)S(1)} %collective-permute-done.13, f32[2,64,256]{2,1,0:T(8,128)S(1)} %add.98), kind=kLoop, calls=%fused_computation.22 | loop fusion | flops 16384 | bytes 196608 | tf_op jit(solution)/shard_map/broadcast_in_dim | solution.py:402
  (9 shorter events, 0.3 us)
Async XLA Ops:
  0.6 3.3 %copy-start.1 = (f32[1,1,32,128,128]{4,3,2,1,0:T(8,128)S(1)}, f32[1,1,32,128,128]{4,3,2,1,0:T(8,128)}, u32[]{:S(2)}) copy-start(f32[1,1,32,128,128]{4,3,2,1,0:T(8,128)} %param.10) | copy-start | bytes 6291460
  1.4 0.7 %copy-start.3 = (f32[16,41]{1,0:T(8,128)S(1)}, f32[16,41]{1,0:T(8,128)}, u32[]{:S(2)}) copy-start(f32[16,41]{1,0:T(8,128)} %row_taps_in.1) | copy-start | bytes 7876
  2.1 0.7 %copy-start.4 = (f32[16,41]{1,0:T(8,128)S(1)}, f32[16,41]{1,0:T(8,128)}, u32[]{:S(2)}) copy-start(f32[16,41]{1,0:T(8,128)} %col_taps_in.1) | copy-start | bytes 7876
  2.8 1.1 %copy-start.5 = (s32[1,1,32]{2,1,0:T(1,128)S(1)}, s32[1,1,32]{2,1,0:T(1,128)}, u32[]{:S(2)}) copy-start(s32[1,1,32]{2,1,0:T(1,128)} %param.11) | copy-start | bytes 388
  2.8 1.1 %copy-start.6 = (s32[1,1,32]{2,1,0:T(1,128)S(1)}, s32[1,1,32]{2,1,0:T(1,128)}, u32[]{:S(2)}) copy-start(s32[1,1,32]{2,1,0:T(1,128)} %param.12) | copy-start | bytes 388
  3.9 2.2 %copy-start = (f32[1,1,32,128,128]{4,3,2,1,0:T(8,128)S(1)}, f32[1,1,32,128,128]{4,3,2,1,0:T(8,128)}, u32[]{:S(2)}) copy-start(f32[1,1,32,128,128]{4,3,2,1,0:T(8,128)} %param.9) | copy-start | bytes 6291460
  3.9 2.2 %copy-start.2 = (f32[800,16,6]{0,1,2:T(8,128)S(1)}, f32[800,16,6]{0,1,2:T(8,128)}, u32[]{:S(2)}) copy-start(f32[800,16,6]{0,1,2:T(8,128)} %param.15) | copy-start | bytes 921604
  3.9 2.2 %copy-start.7 = (s32[1,1,32]{2,1,0:T(1,128)S(1)}, s32[1,1,32]{2,1,0:T(1,128)}, u32[]{:S(2)}) copy-start(s32[1,1,32]{2,1,0:T(1,128)} %param.13) | copy-start | bytes 388
  5.6 11.5 %collective-permute-start.2 = (f32[2,2,2,2,64,256]{5,4,3,2,1,0:T(8,128)S(1)}, f32[2,2,2,2,64,256]{5,4,3,2,1,0:T(8,128)S(1)}, u32[]{:S(2)}, u32[]{:S(2)}) collective-permute-start(f32[2,2,2,2,64,256]{5,4,3,2,1,0:T(8,128)S(1)} %get-tuple-element.47), channel_id=1, source_target_pairs={{0,1},{1,0},{2,3},{3,2},{4,5},{5,4},{6,7},{7,6},{8,9},{9,8},{10,11... | collective-permute-start | bytes 3145736 | tf_op jit(solution)/shard_map/ppermute | solution.py:343
  15.0 1.6 %collective-permute-start = (f32[4,64,256]{2,1,0:T(8,128)S(1)}, f32[4,64,256]{2,1,0:T(8,128)S(1)}, u32[]{:S(2)}, u32[]{:S(2)}) collective-permute-start(f32[4,64,256]{2,1,0:T(8,128)S(1)} %get-tuple-element.82), channel_id=1, source_target_pairs={{0,1},{1,0},{2,3},{3,2},{4,5},{5,4},{6,7},{7,6},{8,9},{9,8},{10,11... | collective-permute-start | bytes 786440 | tf_op jit(solution)/shard_map/ppermute | solution.py:343
  15.1 1.9 %collective-permute-start.1 = (f32[4,64,256]{2,1,0:T(8,128)S(1)}, f32[4,64,256]{2,1,0:T(8,128)S(1)}, u32[]{:S(2)}, u32[]{:S(2)}) collective-permute-start(f32[4,64,256]{2,1,0:T(8,128)S(1)} %get-tuple-element.83), channel_id=1, source_target_pairs={{0,1},{1,0},{2,3},{3,2},{4,5},{5,4},{6,7},{7,6},{8,9},{9,8},{10,11... | collective-permute-start | bytes 786440 | tf_op jit(solution)/shard_map/ppermute | solution.py:343
  17.0 15.1 %collective-permute-start.3 = (f32[2,4,64,256]{3,2,1,0:T(8,128)S(1)}, f32[2,4,64,256]{3,2,1,0:T(8,128)S(1)}, u32[]{:S(2)}, u32[]{:S(2)}) collective-permute-start(f32[2,4,64,256]{3,2,1,0:T(8,128)S(1)} %maximum_add_fusion), channel_id=1, source_target_pairs={{0,8},{8,0},{16,24},{24,16},{1,9},{9,1},{17,25},{25,17},{2,10},{10... | collective-permute-start | bytes 1572872 | tf_op jit(solution)/shard_map/ppermute | solution.py:346
  19.8 14.0 %collective-permute-start.6 = (f32[2,2,2,64,256]{4,3,2,1,0:T(8,128)S(1)}, f32[2,2,2,64,256]{4,3,2,1,0:T(8,128)S(1)}, u32[]{:S(2)}, u32[]{:S(2)}) collective-permute-start(f32[2,2,2,64,256]{4,3,2,1,0:T(8,128)S(1)} %get-tuple-element.63), channel_id=1, source_target_pairs={{0,2},{1,3},{2,0},{3,1},{4,6},{5,7},{6,4},{7,5},{8,10},{9,11},{10,... | collective-permute-start | bytes 1572872 | tf_op jit(solution)/shard_map/ppermute | solution.py:353
  30.4 1.8 %collective-permute-start.5 = (f32[4,64,256]{2,1,0:T(8,128)S(1)}, f32[4,64,256]{2,1,0:T(8,128)S(1)}, u32[]{:S(2)}, u32[]{:S(2)}) collective-permute-start(f32[4,64,256]{2,1,0:T(8,128)S(1)} %get-tuple-element.80), channel_id=1, source_target_pairs={{0,1},{1,0},{2,3},{3,2},{4,5},{5,4},{6,7},{7,6},{8,9},{9,8},{10,11... | collective-permute-start | bytes 786440 | tf_op jit(solution)/shard_map/ppermute | solution.py:343
  30.5 1.9 %collective-permute-start.4 = (f32[4,64,256]{2,1,0:T(8,128)S(1)}, f32[4,64,256]{2,1,0:T(8,128)S(1)}, u32[]{:S(2)}, u32[]{:S(2)}) collective-permute-start(f32[4,64,256]{2,1,0:T(8,128)S(1)} %get-tuple-element.81), channel_id=1, source_target_pairs={{0,1},{1,0},{2,3},{3,2},{4,5},{5,4},{6,7},{7,6},{8,9},{9,8},{10,11... | collective-permute-start | bytes 786440 | tf_op jit(solution)/shard_map/ppermute | solution.py:343
  33.9 7.5 %collective-permute-start.7 = (f32[2,2,64,256]{3,2,1,0:T(8,128)S(1)}, f32[2,2,64,256]{3,2,1,0:T(8,128)S(1)}, u32[]{:S(2)}, u32[]{:S(2)}) collective-permute-start(f32[2,2,64,256]{3,2,1,0:T(8,128)S(1)} %get-tuple-element.74), channel_id=1, source_target_pairs={{0,8},{8,0},{16,24},{24,16},{1,9},{9,1},{17,25},{25,17},{2,10},{10... | collective-permute-start | bytes 786440 | tf_op jit(solution)/shard_map/ppermute | solution.py:346
  34.4 8.7 %collective-permute-start.8 = (f32[4,64,256]{2,1,0:T(8,128)S(1)}, f32[4,64,256]{2,1,0:T(8,128)S(1)}, u32[]{:S(2)}, u32[]{:S(2)}) collective-permute-start(f32[4,64,256]{2,1,0:T(8,128)S(1)} %add.85), channel_id=1, source_target_pairs={{0,16},{8,24},{16,0},{24,8},{1,17},{9,25},{17,1},{25,9},{2,18},{10... | collective-permute-start | bytes 786440 | tf_op jit(solution)/shard_map/ppermute | solution.py:346
  41.4 6.2 %collective-permute-start.12 = (f32[2,64,256]{2,1,0:T(8,128)S(1)}, f32[2,64,256]{2,1,0:T(8,128)S(1)}, u32[]{:S(2)}, u32[]{:S(2)}) collective-permute-start(f32[2,64,256]{2,1,0:T(8,128)S(1)} %get-tuple-element.78), channel_id=1, source_target_pairs={{0,16},{8,24},{16,0},{24,8},{1,17},{9,25},{17,1},{25,9},{2,18},{10... | collective-permute-start | bytes 393224 | tf_op jit(solution)/shard_map/ppermute | solution.py:346
  43.1 6.7 %collective-permute-start.9 = (f32[64,256]{1,0:T(8,128)S(1)}, f32[64,256]{1,0:T(8,128)S(1)}, u32[]{:S(2)}, u32[]{:S(2)}) collective-permute-start(f32[64,256]{1,0:T(8,128)S(1)} %get-tuple-element.84), channel_id=1, source_target_pairs={{0,6},{1,7},{2,4},{3,5},{4,2},{5,3},{6,0},{7,1},{8,14},{9,15},{10,... | collective-permute-start | bytes 196616 | tf_op jit(solution)/shard_map/ppermute | solution.py:353
  46.8 5.9 %collective-permute-start.11 = (f32[64,256]{1,0:T(8,128)S(1)}, f32[64,256]{1,0:T(8,128)S(1)}, u32[]{:S(2)}, u32[]{:S(2)}) collective-permute-start(f32[64,256]{1,0:T(8,128)S(1)} %get-tuple-element.85), channel_id=1, source_target_pairs={{0,4},{1,5},{2,6},{3,7},{4,0},{5,1},{6,2},{7,3},{8,12},{9,13},{10,... | collective-permute-start | bytes 196616 | tf_op jit(solution)/shard_map/ppermute | solution.py:353
  46.8 5.9 %collective-permute-start.10 = (f32[64,256]{1,0:T(8,128)S(1)}, f32[64,256]{1,0:T(8,128)S(1)}, u32[]{:S(2)}, u32[]{:S(2)}) collective-permute-start(f32[64,256]{1,0:T(8,128)S(1)} %get-tuple-element.86), channel_id=1, source_target_pairs={{0,2},{1,3},{2,0},{3,1},{4,6},{5,7},{6,4},{7,5},{8,10},{9,11},{10,... | collective-permute-start | bytes 196616 | tf_op jit(solution)/shard_map/ppermute | solution.py:353
  47.6 5.8 %collective-permute-start.13 = (f32[64,256]{1,0:T(8,128)S(1)}, f32[64,256]{1,0:T(8,128)S(1)}, u32[]{:S(2)}, u32[]{:S(2)}) collective-permute-start(f32[64,256]{1,0:T(8,128)S(1)} %slice_bitcast_fusion.4), channel_id=1, source_target_pairs={{0,4},{1,5},{2,6},{3,7},{4,0},{5,1},{6,2},{7,3},{8,12},{9,13},{10,... | collective-permute-start | bytes 196616 | tf_op jit(solution)/shard_map/ppermute | solution.py:353

commit v6 on v5

--- a/solution.py
+++ b/solution.py
@@ -132,15 +132,15 @@
 
 
 def band_kernel(
-    row_taps_in, col_taps_in, col_out, row_out, row_padded, col_padded, col_band, row_band, done
+    taps_in, col_out, row_out, row_padded, col_padded, col_band, row_band, done
 ):
-    nbasis, taps = row_taps_in.shape
+    nbasis, taps = row_padded.shape[0], taps_in.shape[1]
     side = row_padded.shape[1]
     radius = (taps - 1) // 2
     row_padded[...] = jnp.zeros_like(row_padded)
     col_padded[...] = jnp.zeros_like(col_padded)
-    row_padded[:, :taps] = row_taps_in[...]
-    col_padded[:, :taps] = col_taps_in[...]
+    row_padded[:, :taps] = taps_in[:nbasis]
+    col_padded[:, :taps] = taps_in[nbasis:]
     row = lax.broadcasted_iota(jnp.int32, (side, side), 0)
     column = lax.broadcasted_iota(jnp.int32, (side, side), 1)
     near = jnp.abs(row - column) <= radius
@@ -173,7 +173,7 @@
     nbasis, taps = row_taps.shape
     anywhere = pl.BlockSpec(memory_space=pltpu.HBM)
     col_shape, row_shape = (nbasis, side, 2 * side), (nbasis, 2 * side, side)
-    tap_block = pl.BlockSpec((nbasis, taps), lambda i: (0, 0))
+    tap_block = pl.BlockSpec((2 * nbasis, taps), lambda i: (0, 0))
     return pl.pallas_call(
         band_kernel,
         grid=(1,),
@@ -181,7 +181,7 @@
             jax.ShapeDtypeStruct(col_shape, bf16),
             jax.ShapeDtypeStruct(row_shape, bf16),
         ),
-        in_specs=[tap_block] * 2,
+        in_specs=[tap_block],
         out_specs=[anywhere] * 2,
         scratch_shapes=[
             pltpu.VMEM((nbasis, side), f32),
@@ -192,7 +192,7 @@
         ],
         compiler_params=pltpu.CompilerParams(vmem_limit_bytes=VMEM_BYTES),
         cost_estimate=pl.CostEstimate(flops=10**9, bytes_accessed=0, transcendentals=0),
-    )(row_taps, col_taps)
+    )(jnp.concatenate([row_taps, col_taps], axis=0))
 
 
 def match_kernel(
@@ -384,7 +384,6 @@
     near = [keep_near[y] + far_x[y] for y in range(2)]
     near, got_near = together((near, got_near))
     near = [near[y] + got_near[y] for y in range(2)]
-    near, weights = together((near, weights))
     near_y = over_visit(near[1], 2)
     weights = [weights[x] + weight_depth[x] for x in range(2)]
     weight_x = over_visit(weights[1], 1)

time: 54.3 us -> 53.6 us (0.987)
  local copies, waits for them, and re-layouts: 1.51 us -> 0.13 us
  other arithmetic: 1.85 us -> 2.53 us
    ppermute x5, waiting for transfers between devices: 4.24 us -> 5.8 us  [over_depth(): return lax.ppermute(value, 'patch', pairs)]
    unnamed x16 -> x12, local copies, waits for them, and re-layouts: 1.42 us -> 0.03 us
    ppermute x4, waiting for transfers between devices: 6.54 us -> 5.18 us  [over_visit(): return lax.ppermute(value, 'visit', [(i, i ^ flip) for i in range(visits)])]
    concatenate x0 -> x1, other arithmetic: none -> 0.72 us  [make_bands(): jnp.concatenate([row_taps, col_taps], axis=0)]
  transfers between devices with their start and end apart: 14 -> 14, of which waited for: 8 -> 6; matrix products, arithmetic and copies ran while one was open for 2% -> 2% of each run, Pallas kernels for 33% -> 33%
where the time goes in v6:
time: 53.6 us; the launch traced here: 53.3 us
  Pallas kernels  20.2 us (38%)
  starting transfers between devices  16.4 us (31%)
  waiting for transfers between devices  12.4 us (23%)
  other arithmetic  2.53 us (5%)
  between operations  1.63 us (3%)
    pallas_call x2, Pallas kernels, match(): pl.pallas_call(functools.partial(match_kernel, offset), out_shape=(part,...  17.6 us
    ppermute x5, starting transfers between devices, over_depth(): return lax.ppermute(value, 'patch', pairs)  8.31 us
    ppermute x4, starting transfers between devices, over_visit(): return lax.ppermute(value, 'visit', [(i, i ^ flip) for i in range(visits)])  6.44 us
    ppermute x5, waiting for transfers between devices, over_depth(): return lax.ppermute(value, 'patch', pairs)  5.8 us
    ppermute x4, waiting for transfers between devices, over_visit(): return lax.ppermute(value, 'visit', [(i, i ^ flip) for i in range(visits)])  5.18 us
    ppermute x5, starting transfers between devices, over_core(): return lax.ppermute(value, 'patch', [(i, i ^ 1) for i in range(owners)])  1.66 us
    pallas_call x1, Pallas kernels, sum_weights(): pl.pallas_call(weight_kernel, out_shape=(part, part), in_specs=[anywhere]...  1.6 us
    ppermute x5, waiting for transfers between devices, over_core(): return lax.ppermute(value, 'patch', [(i, i ^ 1) for i in range(owners)])  1.41 us
  transfers between devices with their start and end apart: 14, of which 6 were waited for; matrix products, arithmetic and copies ran while one was open for 2% of the time, Pallas kernels for 33%

profile of v6, /device:TPU:0, one launch (start us, length us, event | category | flops | bytes accessed | tf_op | source)
XLA Modules:
  0.0 53.3 jit_solution(873921216338655577)
XLA Ops:
  0.6 0.0 copy-start.1
  0.6 0.0 copy-start.4
  0.7 0.0 copy-start.3
  1.5 0.7 %pad_maximum_fusion.taps_in = f32[32,41]{1,0:T(8,128)S(1)} fusion(f32[16,41]{1,0:T(8,128)} %param.17, f32[16,41]{1,0:T(8,128)} %param.16), kind=kLoop, calls=%fused_computation.26 | loop fusion | flops 1312 | bytes 10496 | tf_op jit(solution)/shard_map/concatenate | solution.py:195
  2.2 1.0 %shard_map.104 = (bf16[16,128,256]{2,1,0:T(8,128)(2,1)S(1)}, bf16[16,256,128]{2,1,0:T(8,128)(2,1)S(1)}) custom-call(f32[32,41]{1,0:T(8,128)S(1)} %pad_maximum_fusion.taps_in), custom_call_target="tpu_custom_call" | custom-call | flops 1000000000 | tf_op jit(solution)/shard_map/pallas_call | solution.py:177
  3.2 0.0 copy-start
  3.2 0.0 copy-start.2
  3.2 0.0 copy-start.5
  3.3 0.0 copy-done.1
  3.3 0.0 copy-done.4
  3.3 0.0 copy-done.3
  3.3 1.6 %shard_map.105 = (f32[2,2,2,2,64,256]{5,4,3,2,1,0:T(8,128)S(1)}, f32[2,2,2,2,64,256]{5,4,3,2,1,0:T(8,128)S(1)}) custom-call(s32[32]{0:T(128)S(1)} %bitcast.64, s32[32]{0:T(128)S(1)} %bitcast.67, s32[1]{0:T(128)} %bitcast.54.count_in, f32[32,128,128]{2,1,0:T(8,128)S(1)} %bitcast.59), custom_call_target="tpu_custom_call" | custom-call | flops 1000000000 | tf_op jit(solution)/shard_map/pallas_call | solution.py:114
  4.9 0.5 collective-permute-start.2
  5.4 0.0 copy-done
  5.4 0.0 copy-done.2
  5.4 0.0 copy-done.5
  5.4 8.8 %shard_map.106 = (f32[2,4,64,256]{3,2,1,0:T(8,128)S(1)}, f32[2,4,64,256]{3,2,1,0:T(8,128)S(1)}) custom-call(s32[32]{0:T(128)S(1)} %bitcast.65, s32[32]{0:T(128)S(1)} %bitcast.68, s32[32]{0:T(128)S(1)} %bitcast.70, s32[1]{0:T(128)} %bitcast.55.count_in, f32[32,128,128]{2,1,0:T(8,128)S(1)} %bitcast.57, f32[32,128,128]{2,1,0:T(8,128)S(1)} %bitcast.60, ...), custom_call_target="tpu_custom_call" | custom-call | flops 10737418240 | bytes 10000000 | tf_op jit(solution)/shard_map/pallas_call | solution.py:305
  14.3 0.1 collective-permute-start
  14.4 0.4 collective-permute-start.1
  14.8 1.0 %collective-permute-done = f32[4,64,256]{2,1,0:T(8,128)S(1)} collective-permute-done((f32[4,64,256]{2,1,0:T(8,128)S(1)}, f32[4,64,256]{2,1,0:T(8,128)S(1)}, u32[]{:S(2)}, u32[]{:S(2)}) %collective-permute-start) | collective-permute-done | bytes 262176 | tf_op jit(solution)/shard_map/ppermute | solution.py:343
  15.9 0.4 collective-permute-done.1
  16.2 0.1 maximum_add_fusion
  16.3 0.0 collective-permute-done.2
  16.3 2.7 %collective-permute-start.4 = (f32[2,4,64,256]{3,2,1,0:T(8,128)S(1)}, f32[2,4,64,256]{3,2,1,0:T(8,128)S(1)}, u32[]{:S(2)}, u32[]{:S(2)}) collective-permute-start(f32[2,4,64,256]{3,2,1,0:T(8,128)S(1)} %maximum_add_fusion), channel_id=1, source_target_pairs={{0,8},{8,0},{16,24},{24,16},{1,9},{9,1},{17,25},{25,17},{2,10},{10... | collective-permute-start | bytes 1572872 | tf_op jit(solution)/shard_map/ppermute | solution.py:346
  19.1 0.1 add_bitcast_fusion
  19.2 1.6 %collective-permute-start.3 = (f32[2,2,2,64,256]{4,3,2,1,0:T(8,128)S(1)}, f32[2,2,2,64,256]{4,3,2,1,0:T(8,128)S(1)}, u32[]{:S(2)}, u32[]{:S(2)}) collective-permute-start(f32[2,2,2,64,256]{4,3,2,1,0:T(8,128)S(1)} %get-tuple-element.49), channel_id=1, source_target_pairs={{0,2},{1,3},{2,0},{3,1},{4,6},{5,7},{6,4},{7,5},{8,10},{9,11},{10,... | collective-permute-start | bytes 1572872 | tf_op jit(solution)/shard_map/ppermute | solution.py:353
  20.9 8.8 %shard_map.107 = (f32[2,4,64,256]{3,2,1,0:T(8,128)S(1)}, f32[2,4,64,256]{3,2,1,0:T(8,128)S(1)}) custom-call(s32[32]{0:T(128)S(1)} %bitcast.66, s32[32]{0:T(128)S(1)} %bitcast.69, s32[32]{0:T(128)S(1)} %bitcast.71, s32[1]{0:T(128)} %bitcast.56.count_in, f32[32,128,128]{2,1,0:T(8,128)S(1)} %bitcast.58, f32[32,128,128]{2,1,0:T(8,128)S(1)} %bitcast.61, ...), custom_call_target="tpu_custom_call" | custom-call | flops 10737418240 | bytes 10000000 | tf_op jit(solution)/shard_map/pallas_call | solution.py:305
  29.7 0.1 collective-permute-start.6
  29.8 0.5 collective-permute-start.5
  30.3 2.9 %collective-permute-done.3 = f32[2,2,2,64,256]{4,3,2,1,0:T(8,128)S(1)} collective-permute-done((f32[2,2,2,64,256]{4,3,2,1,0:T(8,128)S(1)}, f32[2,2,2,64,256]{4,3,2,1,0:T(8,128)S(1)}, u32[]{:S(2)}, u32[]{:S(2)}) %collective-permute-start.3) | collective-permute-done | bytes 524320 | tf_op jit(solution)/shard_map/ppermute | solution.py:353
  33.2 0.1 fusion
  33.3 0.4 collective-permute-start.7
  33.7 0.0 collective-permute-done.4
  33.7 0.1 add_bitcast_fusion.2
  33.7 0.0 collective-permute-done.6
  33.8 0.0 collective-permute-done.5
  33.8 1.8 %collective-permute-start.8 = (f32[4,64,256]{2,1,0:T(8,128)S(1)}, f32[4,64,256]{2,1,0:T(8,128)S(1)}, u32[]{:S(2)}, u32[]{:S(2)}) collective-permute-start(f32[4,64,256]{2,1,0:T(8,128)S(1)} %add.91), channel_id=1, source_target_pairs={{0,16},{8,24},{16,0},{24,8},{1,17},{9,25},{17,1},{25,9},{2,18},{10... | collective-permute-start | bytes 786440 | tf_op jit(solution)/shard_map/ppermute | solution.py:346
  35.6 5.2 %collective-permute-done.7 = f32[2,2,64,256]{3,2,1,0:T(8,128)S(1)} collective-permute-done((f32[2,2,64,256]{3,2,1,0:T(8,128)S(1)}, f32[2,2,64,256]{3,2,1,0:T(8,128)S(1)}, u32[]{:S(2)}, u32[]{:S(2)}) %collective-permute-start.7) | collective-permute-done | bytes 262176 | tf_op jit(solution)/shard_map/ppermute | solution.py:346
  40.8 1.5 %collective-permute-start.12 = (f32[2,64,256]{2,1,0:T(8,128)S(1)}, f32[2,64,256]{2,1,0:T(8,128)S(1)}, u32[]{:S(2)}, u32[]{:S(2)}) collective-permute-start(f32[2,64,256]{2,1,0:T(8,128)S(1)} %get-tuple-element.72), channel_id=1, source_target_pairs={{0,16},{8,24},{16,0},{24,8},{1,17},{9,25},{17,1},{25,9},{2,18},{10... | collective-permute-start | bytes 393224 | tf_op jit(solution)/shard_map/ppermute | solution.py:346
  42.4 0.0 collective-permute-done.8
  42.4 3.7 %collective-permute-start.9 = (f32[64,256]{1,0:T(8,128)S(1)}, f32[64,256]{1,0:T(8,128)S(1)}, u32[]{:S(2)}, u32[]{:S(2)}) collective-permute-start(f32[64,256]{1,0:T(8,128)S(1)} %get-tuple-element.78), channel_id=1, source_target_pairs={{0,6},{1,7},{2,4},{3,5},{4,2},{5,3},{6,0},{7,1},{8,14},{9,15},{10,... | collective-permute-start | bytes 196616 | tf_op jit(solution)/shard_map/ppermute | solution.py:353
  46.1 0.0 collective-permute-start.11
  46.1 0.8 %collective-permute-start.10 = (f32[64,256]{1,0:T(8,128)S(1)}, f32[64,256]{1,0:T(8,128)S(1)}, u32[]{:S(2)}, u32[]{:S(2)}) collective-permute-start(f32[64,256]{1,0:T(8,128)S(1)} %get-tuple-element.80), channel_id=1, source_target_pairs={{0,2},{1,3},{2,0},{3,1},{4,6},{5,7},{6,4},{7,5},{8,10},{9,11},{10,... | collective-permute-start | bytes 196616 | tf_op jit(solution)/shard_map/ppermute | solution.py:353
  46.9 0.0 collective-permute-done.12
  46.9 2.2 %collective-permute-start.13 = (f32[64,256]{1,0:T(8,128)S(1)}, f32[64,256]{1,0:T(8,128)S(1)}, u32[]{:S(2)}, u32[]{:S(2)}) collective-permute-start(f32[64,256]{1,0:T(8,128)S(1)} %slice_bitcast_fusion.4), channel_id=1, source_target_pairs={{0,4},{1,5},{2,6},{3,7},{4,0},{5,1},{6,2},{7,3},{8,12},{9,13},{10,... | collective-permute-start | bytes 196616 | tf_op jit(solution)/shard_map/ppermute | solution.py:353
  49.1 0.0 collective-permute-done.9
  49.1 2.9 %collective-permute-done.11 = f32[64,256]{1,0:T(8,128)S(1)} collective-permute-done((f32[64,256]{1,0:T(8,128)S(1)}, f32[64,256]{1,0:T(8,128)S(1)}, u32[]{:S(2)}, u32[]{:S(2)}) %collective-permute-start.11) | collective-permute-done | bytes 65568 | tf_op jit(solution)/shard_map/ppermute | solution.py:353
  52.0 0.0 collective-permute-done.10
  52.0 0.6 %fusion.6 = f32[64,256]{1,0:T(8,128)} fusion(f32[64,256]{1,0:T(8,128)S(1)} %collective-permute-done.11, f32[64,256]{1,0:T(8,128)S(1)} %collective-permute-done.10, f32[64,256]{1,0:T(8,128)S(1)} %collective-permute-done.9, f32[4,64,256]{2,1,0:T(8,128)S(1)} %add.92), kind=kLoop, calls=%fused_computation.25 | loop fusion | flops 49152 | bytes 327680 | tf_op jit(solution)/shard_map/add | solution.py:398
  52.6 0.1 collective-permute-done.13
  52.7 0.6 %fusion.4 = f32[1,64,256]{2,1,0:T(8,128)} fusion(f32[64,256]{1,0:T(8,128)S(1)} %collective-permute-done.13, f32[2,64,256]{2,1,0:T(8,128)S(1)} %add.98), kind=kLoop, calls=%fused_computation.22 | loop fusion | flops 16384 | bytes 196608 | tf_op jit(solution)/shard_map/broadcast_in_dim | solution.py:401
  (9 shorter events, 0.3 us)
Async XLA Ops:
  0.6 2.6 %copy-start.1 = (f32[1,1,32,128,128]{4,3,2,1,0:T(8,128)S(1)}, f32[1,1,32,128,128]{4,3,2,1,0:T(8,128)}, u32[]{:S(2)}) copy-start(f32[1,1,32,128,128]{4,3,2,1,0:T(8,128)} %param.10) | copy-start | bytes 6291460
  0.6 2.6 %copy-start.4 = (s32[1,1,32]{2,1,0:T(1,128)S(1)}, s32[1,1,32]{2,1,0:T(1,128)}, u32[]{:S(2)}) copy-start(s32[1,1,32]{2,1,0:T(1,128)} %param.12) | copy-start | bytes 388
  0.7 2.6 %copy-start.3 = (s32[1,1,32]{2,1,0:T(1,128)S(1)}, s32[1,1,32]{2,1,0:T(1,128)}, u32[]{:S(2)}) copy-start(s32[1,1,32]{2,1,0:T(1,128)} %param.11) | copy-start | bytes 388
  3.2 2.2 %copy-start = (f32[1,1,32,128,128]{4,3,2,1,0:T(8,128)S(1)}, f32[1,1,32,128,128]{4,3,2,1,0:T(8,128)}, u32[]{:S(2)}) copy-start(f32[1,1,32,128,128]{4,3,2,1,0:T(8,128)} %param.9) | copy-start | bytes 6291460
  3.2 2.2 %copy-start.2 = (f32[800,16,6]{0,1,2:T(8,128)S(1)}, f32[800,16,6]{0,1,2:T(8,128)}, u32[]{:S(2)}) copy-start(f32[800,16,6]{0,1,2:T(8,128)} %param.15) | copy-start | bytes 921604
  3.2 2.2 %copy-start.5 = (s32[1,1,32]{2,1,0:T(1,128)S(1)}, s32[1,1,32]{2,1,0:T(1,128)}, u32[]{:S(2)}) copy-start(s32[1,1,32]{2,1,0:T(1,128)} %param.13) | copy-start | bytes 388
  4.9 11.4 %collective-permute-start.2 = (f32[2,2,2,2,64,256]{5,4,3,2,1,0:T(8,128)S(1)}, f32[2,2,2,2,64,256]{5,4,3,2,1,0:T(8,128)S(1)}, u32[]{:S(2)}, u32[]{:S(2)}) collective-permute-start(f32[2,2,2,2,64,256]{5,4,3,2,1,0:T(8,128)S(1)} %get-tuple-element.44), channel_id=1, source_target_pairs={{0,1},{1,0},{2,3},{3,2},{4,5},{5,4},{6,7},{7,6},{8,9},{9,8},{10,11... | collective-permute-start | bytes 3145736 | tf_op jit(solution)/shard_map/ppermute | solution.py:343
  14.3 1.6 %collective-permute-start = (f32[4,64,256]{2,1,0:T(8,128)S(1)}, f32[4,64,256]{2,1,0:T(8,128)S(1)}, u32[]{:S(2)}, u32[]{:S(2)}) collective-permute-start(f32[4,64,256]{2,1,0:T(8,128)S(1)} %get-tuple-element.76), channel_id=1, source_target_pairs={{0,1},{1,0},{2,3},{3,2},{4,5},{5,4},{6,7},{7,6},{8,9},{9,8},{10,11... | collective-permute-start | bytes 786440 | tf_op jit(solution)/shard_map/ppermute | solution.py:343
  14.4 1.8 %collective-permute-start.1 = (f32[4,64,256]{2,1,0:T(8,128)S(1)}, f32[4,64,256]{2,1,0:T(8,128)S(1)}, u32[]{:S(2)}, u32[]{:S(2)}) collective-permute-start(f32[4,64,256]{2,1,0:T(8,128)S(1)} %get-tuple-element.77), channel_id=1, source_target_pairs={{0,1},{1,0},{2,3},{3,2},{4,5},{5,4},{6,7},{7,6},{8,9},{9,8},{10,11... | collective-permute-start | bytes 786440 | tf_op jit(solution)/shard_map/ppermute | solution.py:343
  16.3 17.3 %collective-permute-start.4 = (f32[2,4,64,256]{3,2,1,0:T(8,128)S(1)}, f32[2,4,64,256]{3,2,1,0:T(8,128)S(1)}, u32[]{:S(2)}, u32[]{:S(2)}) collective-permute-start(f32[2,4,64,256]{3,2,1,0:T(8,128)S(1)} %maximum_add_fusion), channel_id=1, source_target_pairs={{0,8},{8,0},{16,24},{24,16},{1,9},{9,1},{17,25},{25,17},{2,10},{10... | collective-permute-start | bytes 1572872 | tf_op jit(solution)/shard_map/ppermute | solution.py:346
  19.2 14.0 %collective-permute-start.3 = (f32[2,2,2,64,256]{4,3,2,1,0:T(8,128)S(1)}, f32[2,2,2,64,256]{4,3,2,1,0:T(8,128)S(1)}, u32[]{:S(2)}, u32[]{:S(2)}) collective-permute-start(f32[2,2,2,64,256]{4,3,2,1,0:T(8,128)S(1)} %get-tuple-element.49), channel_id=1, source_target_pairs={{0,2},{1,3},{2,0},{3,1},{4,6},{5,7},{6,4},{7,5},{8,10},{9,11},{10,... | collective-permute-start | bytes 1572872 | tf_op jit(solution)/shard_map/ppermute | solution.py:353
  29.7 4.0 %collective-permute-start.6 = (f32[4,64,256]{2,1,0:T(8,128)S(1)}, f32[4,64,256]{2,1,0:T(8,128)S(1)}, u32[]{:S(2)}, u32[]{:S(2)}) collective-permute-start(f32[4,64,256]{2,1,0:T(8,128)S(1)} %get-tuple-element.74), channel_id=1, source_target_pairs={{0,1},{1,0},{2,3},{3,2},{4,5},{5,4},{6,7},{7,6},{8,9},{9,8},{10,11... | collective-permute-start | bytes 786440 | tf_op jit(solution)/shard_map/ppermute | solution.py:343
  29.8 4.0 %collective-permute-start.5 = (f32[4,64,256]{2,1,0:T(8,128)S(1)}, f32[4,64,256]{2,1,0:T(8,128)S(1)}, u32[]{:S(2)}, u32[]{:S(2)}) collective-permute-start(f32[4,64,256]{2,1,0:T(8,128)S(1)} %get-tuple-element.75), channel_id=1, source_target_pairs={{0,1},{1,0},{2,3},{3,2},{4,5},{5,4},{6,7},{7,6},{8,9},{9,8},{10,11... | collective-permute-start | bytes 786440 | tf_op jit(solution)/shard_map/ppermute | solution.py:343
  33.3 7.5 %collective-permute-start.7 = (f32[2,2,64,256]{3,2,1,0:T(8,128)S(1)}, f32[2,2,64,256]{3,2,1,0:T(8,128)S(1)}, u32[]{:S(2)}, u32[]{:S(2)}) collective-permute-start(f32[2,2,64,256]{3,2,1,0:T(8,128)S(1)} %get-tuple-element.68), channel_id=1, source_target_pairs={{0,8},{8,0},{16,24},{24,16},{1,9},{9,1},{17,25},{25,17},{2,10},{10... | collective-permute-start | bytes 786440 | tf_op jit(solution)/shard_map/ppermute | solution.py:346
  33.8 8.6 %collective-permute-start.8 = (f32[4,64,256]{2,1,0:T(8,128)S(1)}, f32[4,64,256]{2,1,0:T(8,128)S(1)}, u32[]{:S(2)}, u32[]{:S(2)}) collective-permute-start(f32[4,64,256]{2,1,0:T(8,128)S(1)} %add.91), channel_id=1, source_target_pairs={{0,16},{8,24},{16,0},{24,8},{1,17},{9,25},{17,1},{25,9},{2,18},{10... | collective-permute-start | bytes 786440 | tf_op jit(solution)/shard_map/ppermute | solution.py:346
  40.8 6.1 %collective-permute-start.12 = (f32[2,64,256]{2,1,0:T(8,128)S(1)}, f32[2,64,256]{2,1,0:T(8,128)S(1)}, u32[]{:S(2)}, u32[]{:S(2)}) collective-permute-start(f32[2,64,256]{2,1,0:T(8,128)S(1)} %get-tuple-element.72), channel_id=1, source_target_pairs={{0,16},{8,24},{16,0},{24,8},{1,17},{9,25},{17,1},{25,9},{2,18},{10... | collective-permute-start | bytes 393224 | tf_op jit(solution)/shard_map/ppermute | solution.py:346
  42.4 6.7 %collective-permute-start.9 = (f32[64,256]{1,0:T(8,128)S(1)}, f32[64,256]{1,0:T(8,128)S(1)}, u32[]{:S(2)}, u32[]{:S(2)}) collective-permute-start(f32[64,256]{1,0:T(8,128)S(1)} %get-tuple-element.78), channel_id=1, source_target_pairs={{0,6},{1,7},{2,4},{3,5},{4,2},{5,3},{6,0},{7,1},{8,14},{9,15},{10,... | collective-permute-start | bytes 196616 | tf_op jit(solution)/shard_map/ppermute | solution.py:353
  46.1 5.9 %collective-permute-start.11 = (f32[64,256]{1,0:T(8,128)S(1)}, f32[64,256]{1,0:T(8,128)S(1)}, u32[]{:S(2)}, u32[]{:S(2)}) collective-permute-start(f32[64,256]{1,0:T(8,128)S(1)} %get-tuple-element.79), channel_id=1, source_target_pairs={{0,4},{1,5},{2,6},{3,7},{4,0},{5,1},{6,2},{7,3},{8,12},{9,13},{10,... | collective-permute-start | bytes 196616 | tf_op jit(solution)/shard_map/ppermute | solution.py:353
  46.1 5.9 %collective-permute-start.10 = (f32[64,256]{1,0:T(8,128)S(1)}, f32[64,256]{1,0:T(8,128)S(1)}, u32[]{:S(2)}, u32[]{:S(2)}) collective-permute-start(f32[64,256]{1,0:T(8,128)S(1)} %get-tuple-element.80), channel_id=1, source_target_pairs={{0,2},{1,3},{2,0},{3,1},{4,6},{5,7},{6,4},{7,5},{8,10},{9,11},{10,... | collective-permute-start | bytes 196616 | tf_op jit(solution)/shard_map/ppermute | solution.py:353
  46.9 5.8 %collective-permute-start.13 = (f32[64,256]{1,0:T(8,128)S(1)}, f32[64,256]{1,0:T(8,128)S(1)}, u32[]{:S(2)}, u32[]{:S(2)}) collective-permute-start(f32[64,256]{1,0:T(8,128)S(1)} %slice_bitcast_fusion.4), channel_id=1, source_target_pairs={{0,4},{1,5},{2,6},{3,7},{4,0},{5,1},{6,2},{7,3},{8,12},{9,13},{10,... | collective-permute-start | bytes 196616 | tf_op jit(solution)/shard_map/ppermute | solution.py:353

commit v7 on v6

--- a/solution.py
+++ b/solution.py
@@ -55,29 +55,18 @@
 
 
 def weight_kernel(
-    targets_in, quarters_in, count_in, variance_in, keep_out, send_out,
-    targets, quarters, count, variance, canvas, scalar_done, block_done, out_done,
+    targets_in, quarters_in, count_in, variance, keep_out, send_out,
+    targets, quarters, count, canvas, scalar_done, out_done,
 ):
     blocks, side, _ = variance.shape
     half = side // 2
-    chunks = block_done.shape[0]
-    size = blocks // chunks
     scalars = [
         pltpu.make_async_copy(a, b, scalar_done.at[i])
         for i, (a, b) in enumerate(
             [(targets_in, targets), (quarters_in, quarters), (count_in, count)]
         )
     ]
-    arrays = [
-        pltpu.make_async_copy(
-            variance_in.at[pl.ds(i * size, size)],
-            variance.at[pl.ds(i * size, size)],
-            block_done.at[i],
-        )
-        for i in range(chunks)
-    ]
     start_all(scalars)
-    start_all(arrays)
     canvas[...] = jnp.zeros_like(canvas)
     where = my_place(2 * canvas.shape[4])
     wait_all(scalars)
@@ -95,9 +84,7 @@
             ]
         return carry
 
-    for i in range(chunks):
-        arrays[i].wait()
-        lax.fori_loop(i * size, (i + 1) * size, add_block, 0, unroll=2)
+    lax.fori_loop(0, blocks, add_block, 0, unroll=4)
     outs = [
         pltpu.make_async_copy(canvas.at[1], send_out, out_done.at[0]),
         pltpu.make_async_copy(canvas.at[0], keep_out, out_done.at[1]),
@@ -114,16 +101,14 @@
     return pl.pallas_call(
         weight_kernel,
         out_shape=(part, part),
-        in_specs=[anywhere] * 4,
+        in_specs=[anywhere] * 3 + [pl.BlockSpec(memory_space=pltpu.VMEM)],
         out_specs=[anywhere] * 2,
         scratch_shapes=[
             pltpu.SMEM(targets.shape, jnp.int32),
             pltpu.SMEM(quarters.shape, jnp.int32),
             pltpu.SMEM(count.shape, jnp.int32),
-            pltpu.VMEM(variance.shape, f32),
             pltpu.VMEM((2,) + part.shape, f32),
             pltpu.SemaphoreType.DMA((3,)),
-            pltpu.SemaphoreType.DMA((4,)),
             pltpu.SemaphoreType.DMA((2,)),
         ],
         compiler_params=pltpu.CompilerParams(vmem_limit_bytes=VMEM_BYTES),
@@ -132,7 +117,7 @@
 
 
 def band_kernel(
-    taps_in, col_out, row_out, row_padded, col_padded, col_band, row_band, done
+    taps_in, col_band, row_band, row_padded, col_padded
 ):
     nbasis, taps = row_padded.shape[0], taps_in.shape[1]
     side = row_padded.shape[1]
@@ -155,23 +140,17 @@
         first, second = split_left(band)
         col_band[k, :, :side] = first
         col_band[k, :, side:] = second
-    col_copy = pltpu.make_async_copy(col_band, col_out, done.at[0])
-    col_copy.start()
     for k in range(nbasis):
         base = jnp.broadcast_to(row_placed[k : k + 1], (side, side))
         band = jnp.where(near, pltpu.roll(base, 0, 1, stride=1, stride_axis=0), 0.0)
         first, second = split_right(band)
         row_band[k, :side, :] = first
         row_band[k, side:, :] = second
-    row_copy = pltpu.make_async_copy(row_band, row_out, done.at[1])
-    row_copy.start()
-    col_copy.wait()
-    row_copy.wait()
 
 
 def make_bands(row_taps, col_taps, side):
     nbasis, taps = row_taps.shape
-    anywhere = pl.BlockSpec(memory_space=pltpu.HBM)
+    vector = pl.BlockSpec(memory_space=pltpu.VMEM)
     col_shape, row_shape = (nbasis, side, 2 * side), (nbasis, 2 * side, side)
     tap_block = pl.BlockSpec((2 * nbasis, taps), lambda i: (0, 0))
     return pl.pallas_call(
@@ -182,13 +161,10 @@
             jax.ShapeDtypeStruct(row_shape, bf16),
         ),
         in_specs=[tap_block],
-        out_specs=[anywhere] * 2,
+        out_specs=[vector] * 2,
         scratch_shapes=[
             pltpu.VMEM((nbasis, side), f32),
             pltpu.VMEM((nbasis, side), f32),
-            pltpu.VMEM(col_shape, bf16),
-            pltpu.VMEM(row_shape, bf16),
-            pltpu.SemaphoreType.DMA((2,)),
         ],
         compiler_params=pltpu.CompilerParams(vmem_limit_bytes=VMEM_BYTES),
         cost_estimate=pl.CostEstimate(flops=10**9, bytes_accessed=0, transcendentals=0),

time: 53.6 us -> 53.3 us (level)
  no operation moved by 1% of the time
where the time goes in v7:
time: 53.3 us; the launch traced here: 53.1 us
  Pallas kernels  19.9 us (37%)
  starting transfers between devices  16.5 us (31%)
  waiting for transfers between devices  12.3 us (23%)
  other arithmetic  2.53 us (5%)
  between operations  1.63 us (3%)
    pallas_call x2, Pallas kernels, match(): pl.pallas_call(functools.partial(match_kernel, offset), out_shape=(part,...  17.6 us
    ppermute x5, starting transfers between devices, over_depth(): return lax.ppermute(value, 'patch', pairs)  8.37 us
    ppermute x4, starting transfers between devices, over_visit(): return lax.ppermute(value, 'visit', [(i, i ^ flip) for i in range(visits)])  6.52 us
    ppermute x5, waiting for transfers between devices, over_depth(): return lax.ppermute(value, 'patch', pairs)  5.74 us
    ppermute x4, waiting for transfers between devices, over_visit(): return lax.ppermute(value, 'visit', [(i, i ^ flip) for i in range(visits)])  5.13 us
    ppermute x5, starting transfers between devices, over_core(): return lax.ppermute(value, 'patch', [(i, i ^ 1) for i in range(owners)])  1.66 us
    pallas_call x1, Pallas kernels, sum_weights(): pl.pallas_call(weight_kernel, out_shape=(part, part), in_specs=[anywhere]...  1.59 us
    ppermute x5, waiting for transfers between devices, over_core(): return lax.ppermute(value, 'patch', [(i, i ^ 1) for i in range(owners)])  1.41 us
  transfers between devices with their start and end apart: 14, of which 6 were waited for; matrix products, arithmetic and copies ran while one was open for 2% of the time, Pallas kernels for 33%

profile of v7, /device:TPU:0, one launch (start us, length us, event | category | flops | bytes accessed | tf_op | source)
XLA Modules:
  0.0 53.1 jit_solution(10745906867434447708)
XLA Ops:
  0.6 0.0 copy-start.1
  0.6 0.0 copy-start.4
  0.7 0.0 copy-start.3
  1.5 0.7 %pad_maximum_fusion.taps_in = f32[32,41]{1,0:T(8,128)S(1)} fusion(f32[16,41]{1,0:T(8,128)} %param.17, f32[16,41]{1,0:T(8,128)} %param.16), kind=kLoop, calls=%fused_computation.26 | loop fusion | flops 1312 | bytes 10496 | tf_op jit(solution)/shard_map/concatenate | solution.py:171
  2.2 0.8 %shard_map.104 = (bf16[16,128,256]{2,1,0:T(8,128)(2,1)S(1)}, bf16[16,256,128]{2,1,0:T(8,128)(2,1)S(1)}) custom-call(f32[32,41]{1,0:T(8,128)S(1)} %pad_maximum_fusion.taps_in), custom_call_target="tpu_custom_call" | custom-call | flops 1000000000 | tf_op jit(solution)/shard_map/pallas_call | solution.py:156
  3.0 0.0 copy-start
  3.0 0.0 copy-start.2
  3.0 0.0 copy-start.5
  3.0 0.0 copy-done.1
  3.0 0.0 copy-done.4
  3.0 0.0 copy-done.3
  3.0 1.6 %shard_map.105 = (f32[2,2,2,2,64,256]{5,4,3,2,1,0:T(8,128)S(1)}, f32[2,2,2,2,64,256]{5,4,3,2,1,0:T(8,128)S(1)}) custom-call(s32[32]{0:T(128)S(1)} %bitcast.64, s32[32]{0:T(128)S(1)} %bitcast.67, s32[1]{0:T(128)} %bitcast.54.count_in, f32[32,128,128]{2,1,0:T(8,128)S(1)} %bitcast.59), custom_call_target="tpu_custom_call" | custom-call | flops 1000000000 | tf_op jit(solution)/shard_map/pallas_call | solution.py:101
  4.6 0.5 collective-permute-start.2
  5.2 0.0 copy-done
  5.2 0.0 copy-done.2
  5.2 0.0 copy-done.5
  5.2 8.8 %shard_map.106 = (f32[2,4,64,256]{3,2,1,0:T(8,128)S(1)}, f32[2,4,64,256]{3,2,1,0:T(8,128)S(1)}) custom-call(s32[32]{0:T(128)S(1)} %bitcast.65, s32[32]{0:T(128)S(1)} %bitcast.68, s32[32]{0:T(128)S(1)} %bitcast.70, s32[1]{0:T(128)} %bitcast.55.count_in, f32[32,128,128]{2,1,0:T(8,128)S(1)} %bitcast.57, f32[32,128,128]{2,1,0:T(8,128)S(1)} %bitcast.60, ...), custom_call_target="tpu_custom_call" | custom-call | flops 10737418240 | bytes 10000000 | tf_op jit(solution)/shard_map/pallas_call | solution.py:281
  14.0 0.1 collective-permute-start
  14.1 0.4 collective-permute-start.1
  14.6 1.0 %collective-permute-done = f32[4,64,256]{2,1,0:T(8,128)S(1)} collective-permute-done((f32[4,64,256]{2,1,0:T(8,128)S(1)}, f32[4,64,256]{2,1,0:T(8,128)S(1)}, u32[]{:S(2)}, u32[]{:S(2)}) %collective-permute-start) | collective-permute-done | bytes 262176 | tf_op jit(solution)/shard_map/ppermute | solution.py:319
  15.6 0.4 collective-permute-done.1
  16.0 0.1 maximum_add_fusion
  16.0 0.0 collective-permute-done.2
  16.1 2.7 %collective-permute-start.4 = (f32[2,4,64,256]{3,2,1,0:T(8,128)S(1)}, f32[2,4,64,256]{3,2,1,0:T(8,128)S(1)}, u32[]{:S(2)}, u32[]{:S(2)}) collective-permute-start(f32[2,4,64,256]{3,2,1,0:T(8,128)S(1)} %maximum_add_fusion), channel_id=1, source_target_pairs={{0,8},{8,0},{16,24},{24,16},{1,9},{9,1},{17,25},{25,17},{2,10},{10... | collective-permute-start | bytes 1572872 | tf_op jit(solution)/shard_map/ppermute | solution.py:322
  18.8 0.1 add_bitcast_fusion
  18.9 1.7 %collective-permute-start.3 = (f32[2,2,2,64,256]{4,3,2,1,0:T(8,128)S(1)}, f32[2,2,2,64,256]{4,3,2,1,0:T(8,128)S(1)}, u32[]{:S(2)}, u32[]{:S(2)}) collective-permute-start(f32[2,2,2,64,256]{4,3,2,1,0:T(8,128)S(1)} %get-tuple-element.49), channel_id=1, source_target_pairs={{0,2},{1,3},{2,0},{3,1},{4,6},{5,7},{6,4},{7,5},{8,10},{9,11},{10,... | collective-permute-start | bytes 1572872 | tf_op jit(solution)/shard_map/ppermute | solution.py:329
  20.6 8.8 %shard_map.107 = (f32[2,4,64,256]{3,2,1,0:T(8,128)S(1)}, f32[2,4,64,256]{3,2,1,0:T(8,128)S(1)}) custom-call(s32[32]{0:T(128)S(1)} %bitcast.66, s32[32]{0:T(128)S(1)} %bitcast.69, s32[32]{0:T(128)S(1)} %bitcast.71, s32[1]{0:T(128)} %bitcast.56.count_in, f32[32,128,128]{2,1,0:T(8,128)S(1)} %bitcast.58, f32[32,128,128]{2,1,0:T(8,128)S(1)} %bitcast.61, ...), custom_call_target="tpu_custom_call" | custom-call | flops 10737418240 | bytes 10000000 | tf_op jit(solution)/shard_map/pallas_call | solution.py:281
  29.4 0.1 collective-permute-start.6
  29.5 0.5 collective-permute-start.5
  30.0 2.9 %collective-permute-done.3 = f32[2,2,2,64,256]{4,3,2,1,0:T(8,128)S(1)} collective-permute-done((f32[2,2,2,64,256]{4,3,2,1,0:T(8,128)S(1)}, f32[2,2,2,64,256]{4,3,2,1,0:T(8,128)S(1)}, u32[]{:S(2)}, u32[]{:S(2)}) %collective-permute-start.3) | collective-permute-done | bytes 524320 | tf_op jit(solution)/shard_map/ppermute | solution.py:329
  32.9 0.1 fusion
  33.0 0.5 collective-permute-start.7
  33.4 0.0 collective-permute-done.4
  33.4 0.1 add_bitcast_fusion.2
  33.5 0.0 collective-permute-done.6
  33.5 0.0 collective-permute-done.5
  33.6 1.7 %collective-permute-start.8 = (f32[4,64,256]{2,1,0:T(8,128)S(1)}, f32[4,64,256]{2,1,0:T(8,128)S(1)}, u32[]{:S(2)}, u32[]{:S(2)}) collective-permute-start(f32[4,64,256]{2,1,0:T(8,128)S(1)} %add.91), channel_id=1, source_target_pairs={{0,16},{8,24},{16,0},{24,8},{1,17},{9,25},{17,1},{25,9},{2,18},{10... | collective-permute-start | bytes 786440 | tf_op jit(solution)/shard_map/ppermute | solution.py:322
  35.3 5.1 %collective-permute-done.7 = f32[2,2,64,256]{3,2,1,0:T(8,128)S(1)} collective-permute-done((f32[2,2,64,256]{3,2,1,0:T(8,128)S(1)}, f32[2,2,64,256]{3,2,1,0:T(8,128)S(1)}, u32[]{:S(2)}, u32[]{:S(2)}) %collective-permute-start.7) | collective-permute-done | bytes 262176 | tf_op jit(solution)/shard_map/ppermute | solution.py:322
  40.5 1.6 %collective-permute-start.12 = (f32[2,64,256]{2,1,0:T(8,128)S(1)}, f32[2,64,256]{2,1,0:T(8,128)S(1)}, u32[]{:S(2)}, u32[]{:S(2)}) collective-permute-start(f32[2,64,256]{2,1,0:T(8,128)S(1)} %get-tuple-element.72), channel_id=1, source_target_pairs={{0,16},{8,24},{16,0},{24,8},{1,17},{9,25},{17,1},{25,9},{2,18},{10... | collective-permute-start | bytes 393224 | tf_op jit(solution)/shard_map/ppermute | solution.py:322
  42.1 0.0 collective-permute-done.8
  42.2 3.7 %collective-permute-start.9 = (f32[64,256]{1,0:T(8,128)S(1)}, f32[64,256]{1,0:T(8,128)S(1)}, u32[]{:S(2)}, u32[]{:S(2)}) collective-permute-start(f32[64,256]{1,0:T(8,128)S(1)} %get-tuple-element.78), channel_id=1, source_target_pairs={{0,6},{1,7},{2,4},{3,5},{4,2},{5,3},{6,0},{7,1},{8,14},{9,15},{10,... | collective-permute-start | bytes 196616 | tf_op jit(solution)/shard_map/ppermute | solution.py:329
  45.9 0.0 collective-permute-start.11
  45.9 0.8 %collective-permute-start.10 = (f32[64,256]{1,0:T(8,128)S(1)}, f32[64,256]{1,0:T(8,128)S(1)}, u32[]{:S(2)}, u32[]{:S(2)}) collective-permute-start(f32[64,256]{1,0:T(8,128)S(1)} %get-tuple-element.80), channel_id=1, source_target_pairs={{0,2},{1,3},{2,0},{3,1},{4,6},{5,7},{6,4},{7,5},{8,10},{9,11},{10,... | collective-permute-start | bytes 196616 | tf_op jit(solution)/shard_map/ppermute | solution.py:329
  46.6 0.0 collective-permute-done.12
  46.7 2.2 %collective-permute-start.13 = (f32[64,256]{1,0:T(8,128)S(1)}, f32[64,256]{1,0:T(8,128)S(1)}, u32[]{:S(2)}, u32[]{:S(2)}) collective-permute-start(f32[64,256]{1,0:T(8,128)S(1)} %slice_bitcast_fusion.4), channel_id=1, source_target_pairs={{0,4},{1,5},{2,6},{3,7},{4,0},{5,1},{6,2},{7,3},{8,12},{9,13},{10,... | collective-permute-start | bytes 196616 | tf_op jit(solution)/shard_map/ppermute | solution.py:329
  48.9 0.0 collective-permute-done.9
  48.9 2.8 %collective-permute-done.11 = f32[64,256]{1,0:T(8,128)S(1)} collective-permute-done((f32[64,256]{1,0:T(8,128)S(1)}, f32[64,256]{1,0:T(8,128)S(1)}, u32[]{:S(2)}, u32[]{:S(2)}) %collective-permute-start.11) | collective-permute-done | bytes 65568 | tf_op jit(solution)/shard_map/ppermute | solution.py:329
  51.7 0.0 collective-permute-done.10
  51.7 0.6 %fusion.6 = f32[64,256]{1,0:T(8,128)} fusion(f32[64,256]{1,0:T(8,128)S(1)} %collective-permute-done.11, f32[64,256]{1,0:T(8,128)S(1)} %collective-permute-done.10, f32[64,256]{1,0:T(8,128)S(1)} %collective-permute-done.9, f32[4,64,256]{2,1,0:T(8,128)S(1)} %add.92), kind=kLoop, calls=%fused_computation.25 | loop fusion | flops 49152 | bytes 327680 | tf_op jit(solution)/shard_map/add | solution.py:374
  52.4 0.1 collective-permute-done.13
  52.4 0.6 %fusion.4 = f32[1,64,256]{2,1,0:T(8,128)} fusion(f32[64,256]{1,0:T(8,128)S(1)} %collective-permute-done.13, f32[2,64,256]{2,1,0:T(8,128)S(1)} %add.98), kind=kLoop, calls=%fused_computation.22 | loop fusion | flops 16384 | bytes 196608 | tf_op jit(solution)/shard_map/broadcast_in_dim | solution.py:377
  (9 shorter events, 0.3 us)
Async XLA Ops:
  0.6 2.4 %copy-start.1 = (f32[1,1,32,128,128]{4,3,2,1,0:T(8,128)S(1)}, f32[1,1,32,128,128]{4,3,2,1,0:T(8,128)}, u32[]{:S(2)}) copy-start(f32[1,1,32,128,128]{4,3,2,1,0:T(8,128)} %param.10) | copy-start | bytes 6291460
  0.6 2.4 %copy-start.4 = (s32[1,1,32]{2,1,0:T(1,128)S(1)}, s32[1,1,32]{2,1,0:T(1,128)}, u32[]{:S(2)}) copy-start(s32[1,1,32]{2,1,0:T(1,128)} %param.12) | copy-start | bytes 388
  0.7 2.4 %copy-start.3 = (s32[1,1,32]{2,1,0:T(1,128)S(1)}, s32[1,1,32]{2,1,0:T(1,128)}, u32[]{:S(2)}) copy-start(s32[1,1,32]{2,1,0:T(1,128)} %param.11) | copy-start | bytes 388
  3.0 2.2 %copy-start = (f32[1,1,32,128,128]{4,3,2,1,0:T(8,128)S(1)}, f32[1,1,32,128,128]{4,3,2,1,0:T(8,128)}, u32[]{:S(2)}) copy-start(f32[1,1,32,128,128]{4,3,2,1,0:T(8,128)} %param.9) | copy-start | bytes 6291460
  3.0 2.2 %copy-start.2 = (f32[800,16,6]{0,1,2:T(8,128)S(1)}, f32[800,16,6]{0,1,2:T(8,128)}, u32[]{:S(2)}) copy-start(f32[800,16,6]{0,1,2:T(8,128)} %param.15) | copy-start | bytes 921604
  3.0 2.2 %copy-start.5 = (s32[1,1,32]{2,1,0:T(1,128)S(1)}, s32[1,1,32]{2,1,0:T(1,128)}, u32[]{:S(2)}) copy-start(s32[1,1,32]{2,1,0:T(1,128)} %param.13) | copy-start | bytes 388
  4.6 11.4 %collective-permute-start.2 = (f32[2,2,2,2,64,256]{5,4,3,2,1,0:T(8,128)S(1)}, f32[2,2,2,2,64,256]{5,4,3,2,1,0:T(8,128)S(1)}, u32[]{:S(2)}, u32[]{:S(2)}) collective-permute-start(f32[2,2,2,2,64,256]{5,4,3,2,1,0:T(8,128)S(1)} %get-tuple-element.44), channel_id=1, source_target_pairs={{0,1},{1,0},{2,3},{3,2},{4,5},{5,4},{6,7},{7,6},{8,9},{9,8},{10,11... | collective-permute-start | bytes 3145736 | tf_op jit(solution)/shard_map/ppermute | solution.py:319
  14.0 1.6 %collective-permute-start = (f32[4,64,256]{2,1,0:T(8,128)S(1)}, f32[4,64,256]{2,1,0:T(8,128)S(1)}, u32[]{:S(2)}, u32[]{:S(2)}) collective-permute-start(f32[4,64,256]{2,1,0:T(8,128)S(1)} %get-tuple-element.76), channel_id=1, source_target_pairs={{0,1},{1,0},{2,3},{3,2},{4,5},{5,4},{6,7},{7,6},{8,9},{9,8},{10,11... | collective-permute-start | bytes 786440 | tf_op jit(solution)/shard_map/ppermute | solution.py:319
  14.1 1.8 %collective-permute-start.1 = (f32[4,64,256]{2,1,0:T(8,128)S(1)}, f32[4,64,256]{2,1,0:T(8,128)S(1)}, u32[]{:S(2)}, u32[]{:S(2)}) collective-permute-start(f32[4,64,256]{2,1,0:T(8,128)S(1)} %get-tuple-element.77), channel_id=1, source_target_pairs={{0,1},{1,0},{2,3},{3,2},{4,5},{5,4},{6,7},{7,6},{8,9},{9,8},{10,11... | collective-permute-start | bytes 786440 | tf_op jit(solution)/shard_map/ppermute | solution.py:319
  16.1 17.4 %collective-permute-start.4 = (f32[2,4,64,256]{3,2,1,0:T(8,128)S(1)}, f32[2,4,64,256]{3,2,1,0:T(8,128)S(1)}, u32[]{:S(2)}, u32[]{:S(2)}) collective-permute-start(f32[2,4,64,256]{3,2,1,0:T(8,128)S(1)} %maximum_add_fusion), channel_id=1, source_target_pairs={{0,8},{8,0},{16,24},{24,16},{1,9},{9,1},{17,25},{25,17},{2,10},{10... | collective-permute-start | bytes 1572872 | tf_op jit(solution)/shard_map/ppermute | solution.py:322
  18.9 14.0 %collective-permute-start.3 = (f32[2,2,2,64,256]{4,3,2,1,0:T(8,128)S(1)}, f32[2,2,2,64,256]{4,3,2,1,0:T(8,128)S(1)}, u32[]{:S(2)}, u32[]{:S(2)}) collective-permute-start(f32[2,2,2,64,256]{4,3,2,1,0:T(8,128)S(1)} %get-tuple-element.49), channel_id=1, source_target_pairs={{0,2},{1,3},{2,0},{3,1},{4,6},{5,7},{6,4},{7,5},{8,10},{9,11},{10,... | collective-permute-start | bytes 1572872 | tf_op jit(solution)/shard_map/ppermute | solution.py:329
  29.4 4.1 %collective-permute-start.6 = (f32[4,64,256]{2,1,0:T(8,128)S(1)}, f32[4,64,256]{2,1,0:T(8,128)S(1)}, u32[]{:S(2)}, u32[]{:S(2)}) collective-permute-start(f32[4,64,256]{2,1,0:T(8,128)S(1)} %get-tuple-element.74), channel_id=1, source_target_pairs={{0,1},{1,0},{2,3},{3,2},{4,5},{5,4},{6,7},{7,6},{8,9},{9,8},{10,11... | collective-permute-start | bytes 786440 | tf_op jit(solution)/shard_map/ppermute | solution.py:319
  29.5 4.0 %collective-permute-start.5 = (f32[4,64,256]{2,1,0:T(8,128)S(1)}, f32[4,64,256]{2,1,0:T(8,128)S(1)}, u32[]{:S(2)}, u32[]{:S(2)}) collective-permute-start(f32[4,64,256]{2,1,0:T(8,128)S(1)} %get-tuple-element.75), channel_id=1, source_target_pairs={{0,1},{1,0},{2,3},{3,2},{4,5},{5,4},{6,7},{7,6},{8,9},{9,8},{10,11... | collective-permute-start | bytes 786440 | tf_op jit(solution)/shard_map/ppermute | solution.py:319
  33.0 7.5 %collective-permute-start.7 = (f32[2,2,64,256]{3,2,1,0:T(8,128)S(1)}, f32[2,2,64,256]{3,2,1,0:T(8,128)S(1)}, u32[]{:S(2)}, u32[]{:S(2)}) collective-permute-start(f32[2,2,64,256]{3,2,1,0:T(8,128)S(1)} %get-tuple-element.68), channel_id=1, source_target_pairs={{0,8},{8,0},{16,24},{24,16},{1,9},{9,1},{17,25},{25,17},{2,10},{10... | collective-permute-start | bytes 786440 | tf_op jit(solution)/shard_map/ppermute | solution.py:322
  33.6 8.5 %collective-permute-start.8 = (f32[4,64,256]{2,1,0:T(8,128)S(1)}, f32[4,64,256]{2,1,0:T(8,128)S(1)}, u32[]{:S(2)}, u32[]{:S(2)}) collective-permute-start(f32[4,64,256]{2,1,0:T(8,128)S(1)} %add.91), channel_id=1, source_target_pairs={{0,16},{8,24},{16,0},{24,8},{1,17},{9,25},{17,1},{25,9},{2,18},{10... | collective-permute-start | bytes 786440 | tf_op jit(solution)/shard_map/ppermute | solution.py:322
  40.5 6.1 %collective-permute-start.12 = (f32[2,64,256]{2,1,0:T(8,128)S(1)}, f32[2,64,256]{2,1,0:T(8,128)S(1)}, u32[]{:S(2)}, u32[]{:S(2)}) collective-permute-start(f32[2,64,256]{2,1,0:T(8,128)S(1)} %get-tuple-element.72), channel_id=1, source_target_pairs={{0,16},{8,24},{16,0},{24,8},{1,17},{9,25},{17,1},{25,9},{2,18},{10... | collective-permute-start | bytes 393224 | tf_op jit(solution)/shard_map/ppermute | solution.py:322
  42.2 6.7 %collective-permute-start.9 = (f32[64,256]{1,0:T(8,128)S(1)}, f32[64,256]{1,0:T(8,128)S(1)}, u32[]{:S(2)}, u32[]{:S(2)}) collective-permute-start(f32[64,256]{1,0:T(8,128)S(1)} %get-tuple-element.78), channel_id=1, source_target_pairs={{0,6},{1,7},{2,4},{3,5},{4,2},{5,3},{6,0},{7,1},{8,14},{9,15},{10,... | collective-permute-start | bytes 196616 | tf_op jit(solution)/shard_map/ppermute | solution.py:329
  45.9 5.9 %collective-permute-start.11 = (f32[64,256]{1,0:T(8,128)S(1)}, f32[64,256]{1,0:T(8,128)S(1)}, u32[]{:S(2)}, u32[]{:S(2)}) collective-permute-start(f32[64,256]{1,0:T(8,128)S(1)} %get-tuple-element.79), channel_id=1, source_target_pairs={{0,4},{1,5},{2,6},{3,7},{4,0},{5,1},{6,2},{7,3},{8,12},{9,13},{10,... | collective-permute-start | bytes 196616 | tf_op jit(solution)/shard_map/ppermute | solution.py:329
  45.9 5.9 %collective-permute-start.10 = (f32[64,256]{1,0:T(8,128)S(1)}, f32[64,256]{1,0:T(8,128)S(1)}, u32[]{:S(2)}, u32[]{:S(2)}) collective-permute-start(f32[64,256]{1,0:T(8,128)S(1)} %get-tuple-element.80), channel_id=1, source_target_pairs={{0,2},{1,3},{2,0},{3,1},{4,6},{5,7},{6,4},{7,5},{8,10},{9,11},{10,... | collective-permute-start | bytes 196616 | tf_op jit(solution)/shard_map/ppermute | solution.py:329
  46.7 5.8 %collective-permute-start.13 = (f32[64,256]{1,0:T(8,128)S(1)}, f32[64,256]{1,0:T(8,128)S(1)}, u32[]{:S(2)}, u32[]{:S(2)}) collective-permute-start(f32[64,256]{1,0:T(8,128)S(1)} %slice_bitcast_fusion.4), channel_id=1, source_target_pairs={{0,4},{1,5},{2,6},{3,7},{4,0},{5,1},{6,2},{7,3},{8,12},{9,13},{10,... | collective-permute-start | bytes 196616 | tf_op jit(solution)/shard_map/ppermute | solution.py:329

commit v8 on v7

--- a/solution.py
+++ b/solution.py
@@ -56,7 +56,7 @@
 
 def weight_kernel(
     targets_in, quarters_in, count_in, variance, keep_out, send_out,
-    targets, quarters, count, canvas, scalar_done, out_done,
+    targets, quarters, count, canvas, scalar_done,
 ):
     blocks, side, _ = variance.shape
     half = side // 2
@@ -85,12 +85,8 @@
         return carry
 
     lax.fori_loop(0, blocks, add_block, 0, unroll=4)
-    outs = [
-        pltpu.make_async_copy(canvas.at[1], send_out, out_done.at[0]),
-        pltpu.make_async_copy(canvas.at[0], keep_out, out_done.at[1]),
-    ]
-    start_all(outs)
-    wait_all(outs)
+    send_out[...] = canvas[1]
+    keep_out[...] = canvas[0]
 
 
 def sum_weights(targets, quarters, count, variance, depths):
@@ -102,14 +98,13 @@
         weight_kernel,
         out_shape=(part, part),
         in_specs=[anywhere] * 3 + [pl.BlockSpec(memory_space=pltpu.VMEM)],
-        out_specs=[anywhere] * 2,
+        out_specs=[pl.BlockSpec(memory_space=pltpu.VMEM)] * 2,
         scratch_shapes=[
             pltpu.SMEM(targets.shape, jnp.int32),
             pltpu.SMEM(quarters.shape, jnp.int32),
             pltpu.SMEM(count.shape, jnp.int32),
             pltpu.VMEM((2,) + part.shape, f32),
             pltpu.SemaphoreType.DMA((3,)),
-            pltpu.SemaphoreType.DMA((2,)),
         ],
         compiler_params=pltpu.CompilerParams(vmem_limit_bytes=VMEM_BYTES),
         cost_estimate=pl.CostEstimate(flops=10**9, bytes_accessed=0, transcendentals=0),
@@ -174,7 +169,7 @@
 def match_kernel(
     offset, targets_in, quarters_in, rows_in, count_in, pixels, variance, table,
     col_band, row_band, keep_out, send_out,
-    targets, quarters, table_rows, count, canvas, total, coefficients, scalar_done, out_done,
+    targets, quarters, table_rows, count, canvas, total, coefficients, scalar_done,
 ):
     side = pixels.shape[1]
     nbasis = col_band.shape[0]
@@ -258,12 +253,8 @@
         return carry
 
     lax.fori_loop(0, blocks // group, add_group, 0)
-    outs = [
-        pltpu.make_async_copy(canvas.at[1], send_out, out_done.at[0]),
-        pltpu.make_async_copy(canvas.at[0], keep_out, out_done.at[1]),
-    ]
-    start_all(outs)
-    wait_all(outs)
+    send_out[...] = canvas[1]
+    keep_out[...] = canvas[0]
 
 
 def match(
@@ -282,14 +273,13 @@
         functools.partial(match_kernel, offset),
         out_shape=(part, part),
         in_specs=[anywhere] * 4 + [vector] * 5,
-        out_specs=[anywhere] * 2,
+        out_specs=[vector] * 2,
         scratch_shapes=[pltpu.SMEM(a.shape, jnp.int32) for a in scalars]
         + [
             pltpu.VMEM((2, 2, depths, rows, 2 * side), f32),
             pltpu.VMEM((group, rows, side), f32),
             pltpu.VMEM(table.shape[:2] + (entries,), f32),
             pltpu.SemaphoreType.DMA((4,)),
-            pltpu.SemaphoreType.DMA((2,)),
         ],
         compiler_params=pltpu.CompilerParams(vmem_limit_bytes=VMEM_BYTES),
         cost_estimate=pl.CostEstimate(

time: 53.3 us -> 53.3 us (level)
  no operation moved by 1% of the time
where the time goes in v8:
time: 53.3 us; the launch traced here: 53 us
  Pallas kernels  19.9 us (37%)
  starting transfers between devices  16.4 us (31%)
  waiting for transfers between devices  12.4 us (23%)
  other arithmetic  2.53 us (5%)
  between operations  1.63 us (3%)
    pallas_call x2, Pallas kernels, match(): pl.pallas_call(functools.partial(match_kernel, offset), out_shape=(part,...  17.6 us
    ppermute x5, starting transfers between devices, over_depth(): return lax.ppermute(value, 'patch', pairs)  8.29 us
    ppermute x4, starting transfers between devices, over_visit(): return lax.ppermute(value, 'visit', [(i, i ^ flip) for i in range(visits)])  6.46 us
    ppermute x5, waiting for transfers between devices, over_depth(): return lax.ppermute(value, 'patch', pairs)  5.86 us
    ppermute x4, waiting for transfers between devices, over_visit(): return lax.ppermute(value, 'visit', [(i, i ^ flip) for i in range(visits)])  5.18 us
    ppermute x5, starting transfers between devices, over_core(): return lax.ppermute(value, 'patch', [(i, i ^ 1) for i in range(owners)])  1.66 us
    pallas_call x1, Pallas kernels, sum_weights(): pl.pallas_call(weight_kernel, out_shape=(part, part), in_specs=[anywhere]...  1.55 us
    ppermute x5, waiting for transfers between devices, over_core(): return lax.ppermute(value, 'patch', [(i, i ^ 1) for i in range(owners)])  1.41 us
  transfers between devices with their start and end apart: 14, of which 6 were waited for; matrix products, arithmetic and copies ran while one was open for 2% of the time, Pallas kernels for 33%

profile of v8, /device:TPU:0, one launch (start us, length us, event | category | flops | bytes accessed | tf_op | source)
XLA Modules:
  0.0 53.0 jit_solution(11913049729715266210)
XLA Ops:
  0.6 0.0 copy-start.1
  0.6 0.0 copy-start.4
  0.7 0.0 copy-start.3
  1.5 0.7 %pad_maximum_fusion.taps_in = f32[32,41]{1,0:T(8,128)S(1)} fusion(f32[16,41]{1,0:T(8,128)} %param.17, f32[16,41]{1,0:T(8,128)} %param.16), kind=kLoop, calls=%fused_computation.26 | loop fusion | flops 1312 | bytes 10496 | tf_op jit(solution)/shard_map/concatenate | solution.py:166
  2.2 0.8 %shard_map.104 = (bf16[16,128,256]{2,1,0:T(8,128)(2,1)S(1)}, bf16[16,256,128]{2,1,0:T(8,128)(2,1)S(1)}) custom-call(f32[32,41]{1,0:T(8,128)S(1)} %pad_maximum_fusion.taps_in), custom_call_target="tpu_custom_call" | custom-call | flops 1000000000 | tf_op jit(solution)/shard_map/pallas_call | solution.py:151
  3.0 0.0 copy-start
  3.0 0.0 copy-start.2
  3.0 0.0 copy-start.5
  3.0 0.0 copy-done.1
  3.0 0.0 copy-done.4
  3.0 0.0 copy-done.3
  3.0 1.6 %shard_map.105 = (f32[2,2,2,2,64,256]{5,4,3,2,1,0:T(8,128)S(1)}, f32[2,2,2,2,64,256]{5,4,3,2,1,0:T(8,128)S(1)}) custom-call(s32[32]{0:T(128)S(1)} %bitcast.64, s32[32]{0:T(128)S(1)} %bitcast.67, s32[1]{0:T(128)} %bitcast.54.count_in, f32[32,128,128]{2,1,0:T(8,128)S(1)} %bitcast.59), custom_call_target="tpu_custom_call" | custom-call | flops 1000000000 | tf_op jit(solution)/shard_map/pallas_call | solution.py:97
  4.6 0.5 collective-permute-start.2
  5.1 0.0 copy-done
  5.1 0.0 copy-done.2
  5.1 0.0 copy-done.5
  5.1 8.8 %shard_map.106 = (f32[2,4,64,256]{3,2,1,0:T(8,128)S(1)}, f32[2,4,64,256]{3,2,1,0:T(8,128)S(1)}) custom-call(s32[32]{0:T(128)S(1)} %bitcast.65, s32[32]{0:T(128)S(1)} %bitcast.68, s32[32]{0:T(128)S(1)} %bitcast.70, s32[1]{0:T(128)} %bitcast.55.count_in, f32[32,128,128]{2,1,0:T(8,128)S(1)} %bitcast.57, f32[32,128,128]{2,1,0:T(8,128)S(1)} %bitcast.60, ...), custom_call_target="tpu_custom_call" | custom-call | flops 10737418240 | bytes 10000000 | tf_op jit(solution)/shard_map/pallas_call | solution.py:272
  13.9 0.1 collective-permute-start
  14.1 0.4 collective-permute-start.1
  14.5 1.0 %collective-permute-done = f32[4,64,256]{2,1,0:T(8,128)S(1)} collective-permute-done((f32[4,64,256]{2,1,0:T(8,128)S(1)}, f32[4,64,256]{2,1,0:T(8,128)S(1)}, u32[]{:S(2)}, u32[]{:S(2)}) %collective-permute-start) | collective-permute-done | bytes 262176 | tf_op jit(solution)/shard_map/ppermute | solution.py:309
  15.5 0.4 collective-permute-done.1
  15.9 0.1 maximum_add_fusion
  16.0 0.0 collective-permute-done.2
  16.0 2.7 %collective-permute-start.4 = (f32[2,4,64,256]{3,2,1,0:T(8,128)S(1)}, f32[2,4,64,256]{3,2,1,0:T(8,128)S(1)}, u32[]{:S(2)}, u32[]{:S(2)}) collective-permute-start(f32[2,4,64,256]{3,2,1,0:T(8,128)S(1)} %maximum_add_fusion), channel_id=1, source_target_pairs={{0,8},{8,0},{16,24},{24,16},{1,9},{9,1},{17,25},{25,17},{2,10},{10... | collective-permute-start | bytes 1572872 | tf_op jit(solution)/shard_map/ppermute | solution.py:312
  18.7 0.1 add_bitcast_fusion
  18.9 1.6 %collective-permute-start.3 = (f32[2,2,2,64,256]{4,3,2,1,0:T(8,128)S(1)}, f32[2,2,2,64,256]{4,3,2,1,0:T(8,128)S(1)}, u32[]{:S(2)}, u32[]{:S(2)}) collective-permute-start(f32[2,2,2,64,256]{4,3,2,1,0:T(8,128)S(1)} %get-tuple-element.49), channel_id=1, source_target_pairs={{0,2},{1,3},{2,0},{3,1},{4,6},{5,7},{6,4},{7,5},{8,10},{9,11},{10,... | collective-permute-start | bytes 1572872 | tf_op jit(solution)/shard_map/ppermute | solution.py:319
  20.5 8.8 %shard_map.107 = (f32[2,4,64,256]{3,2,1,0:T(8,128)S(1)}, f32[2,4,64,256]{3,2,1,0:T(8,128)S(1)}) custom-call(s32[32]{0:T(128)S(1)} %bitcast.66, s32[32]{0:T(128)S(1)} %bitcast.69, s32[32]{0:T(128)S(1)} %bitcast.71, s32[1]{0:T(128)} %bitcast.56.count_in, f32[32,128,128]{2,1,0:T(8,128)S(1)} %bitcast.58, f32[32,128,128]{2,1,0:T(8,128)S(1)} %bitcast.61, ...), custom_call_target="tpu_custom_call" | custom-call | flops 10737418240 | bytes 10000000 | tf_op jit(solution)/shard_map/pallas_call | solution.py:272
  29.4 0.1 collective-permute-start.6
  29.4 0.5 collective-permute-start.5
  29.9 2.9 %collective-permute-done.3 = f32[2,2,2,64,256]{4,3,2,1,0:T(8,128)S(1)} collective-permute-done((f32[2,2,2,64,256]{4,3,2,1,0:T(8,128)S(1)}, f32[2,2,2,64,256]{4,3,2,1,0:T(8,128)S(1)}, u32[]{:S(2)}, u32[]{:S(2)}) %collective-permute-start.3) | collective-permute-done | bytes 524320 | tf_op jit(solution)/shard_map/ppermute | solution.py:319
  32.8 0.1 fusion
  32.9 0.4 collective-permute-start.7
  33.3 0.0 collective-permute-done.4
  33.3 0.1 add_bitcast_fusion.2
  33.4 0.0 collective-permute-done.6
  33.4 0.0 collective-permute-done.5
  33.5 1.7 %collective-permute-start.8 = (f32[4,64,256]{2,1,0:T(8,128)S(1)}, f32[4,64,256]{2,1,0:T(8,128)S(1)}, u32[]{:S(2)}, u32[]{:S(2)}) collective-permute-start(f32[4,64,256]{2,1,0:T(8,128)S(1)} %add.91), channel_id=1, source_target_pairs={{0,16},{8,24},{16,0},{24,8},{1,17},{9,25},{17,1},{25,9},{2,18},{10... | collective-permute-start | bytes 786440 | tf_op jit(solution)/shard_map/ppermute | solution.py:312
  35.3 5.2 %collective-permute-done.7 = f32[2,2,64,256]{3,2,1,0:T(8,128)S(1)} collective-permute-done((f32[2,2,64,256]{3,2,1,0:T(8,128)S(1)}, f32[2,2,64,256]{3,2,1,0:T(8,128)S(1)}, u32[]{:S(2)}, u32[]{:S(2)}) %collective-permute-start.7) | collective-permute-done | bytes 262176 | tf_op jit(solution)/shard_map/ppermute | solution.py:312
  40.5 1.6 %collective-permute-start.12 = (f32[2,64,256]{2,1,0:T(8,128)S(1)}, f32[2,64,256]{2,1,0:T(8,128)S(1)}, u32[]{:S(2)}, u32[]{:S(2)}) collective-permute-start(f32[2,64,256]{2,1,0:T(8,128)S(1)} %get-tuple-element.72), channel_id=1, source_target_pairs={{0,16},{8,24},{16,0},{24,8},{1,17},{9,25},{17,1},{25,9},{2,18},{10... | collective-permute-start | bytes 393224 | tf_op jit(solution)/shard_map/ppermute | solution.py:312
  42.1 0.0 collective-permute-done.8
  42.1 3.7 %collective-permute-start.9 = (f32[64,256]{1,0:T(8,128)S(1)}, f32[64,256]{1,0:T(8,128)S(1)}, u32[]{:S(2)}, u32[]{:S(2)}) collective-permute-start(f32[64,256]{1,0:T(8,128)S(1)} %get-tuple-element.78), channel_id=1, source_target_pairs={{0,6},{1,7},{2,4},{3,5},{4,2},{5,3},{6,0},{7,1},{8,14},{9,15},{10,... | collective-permute-start | bytes 196616 | tf_op jit(solution)/shard_map/ppermute | solution.py:319
  45.8 0.0 collective-permute-start.11
  45.8 0.8 %collective-permute-start.10 = (f32[64,256]{1,0:T(8,128)S(1)}, f32[64,256]{1,0:T(8,128)S(1)}, u32[]{:S(2)}, u32[]{:S(2)}) collective-permute-start(f32[64,256]{1,0:T(8,128)S(1)} %get-tuple-element.80), channel_id=1, source_target_pairs={{0,2},{1,3},{2,0},{3,1},{4,6},{5,7},{6,4},{7,5},{8,10},{9,11},{10,... | collective-permute-start | bytes 196616 | tf_op jit(solution)/shard_map/ppermute | solution.py:319
  46.6 0.0 collective-permute-done.12
  46.6 2.2 %collective-permute-start.13 = (f32[64,256]{1,0:T(8,128)S(1)}, f32[64,256]{1,0:T(8,128)S(1)}, u32[]{:S(2)}, u32[]{:S(2)}) collective-permute-start(f32[64,256]{1,0:T(8,128)S(1)} %slice_bitcast_fusion.4), channel_id=1, source_target_pairs={{0,4},{1,5},{2,6},{3,7},{4,0},{5,1},{6,2},{7,3},{8,12},{9,13},{10,... | collective-permute-start | bytes 196616 | tf_op jit(solution)/shard_map/ppermute | solution.py:319
  48.8 0.0 collective-permute-done.9
  48.8 2.9 %collective-permute-done.11 = f32[64,256]{1,0:T(8,128)S(1)} collective-permute-done((f32[64,256]{1,0:T(8,128)S(1)}, f32[64,256]{1,0:T(8,128)S(1)}, u32[]{:S(2)}, u32[]{:S(2)}) %collective-permute-start.11) | collective-permute-done | bytes 65568 | tf_op jit(solution)/shard_map/ppermute | solution.py:319
  51.7 0.0 collective-permute-done.10
  51.7 0.6 %fusion.6 = f32[64,256]{1,0:T(8,128)} fusion(f32[64,256]{1,0:T(8,128)S(1)} %collective-permute-done.11, f32[64,256]{1,0:T(8,128)S(1)} %collective-permute-done.10, f32[64,256]{1,0:T(8,128)S(1)} %collective-permute-done.9, f32[4,64,256]{2,1,0:T(8,128)S(1)} %add.92), kind=kLoop, calls=%fused_computation.25 | loop fusion | flops 49152 | bytes 327680 | tf_op jit(solution)/shard_map/add | solution.py:364
  52.3 0.1 collective-permute-done.13
  52.4 0.6 %fusion.4 = f32[1,64,256]{2,1,0:T(8,128)} fusion(f32[64,256]{1,0:T(8,128)S(1)} %collective-permute-done.13, f32[2,64,256]{2,1,0:T(8,128)S(1)} %add.98), kind=kLoop, calls=%fused_computation.22 | loop fusion | flops 16384 | bytes 196608 | tf_op jit(solution)/shard_map/broadcast_in_dim | solution.py:367
  (9 shorter events, 0.3 us)
Async XLA Ops:
  0.6 2.4 %copy-start.1 = (f32[1,1,32,128,128]{4,3,2,1,0:T(8,128)S(1)}, f32[1,1,32,128,128]{4,3,2,1,0:T(8,128)}, u32[]{:S(2)}) copy-start(f32[1,1,32,128,128]{4,3,2,1,0:T(8,128)} %param.10) | copy-start | bytes 6291460
  0.6 2.4 %copy-start.4 = (s32[1,1,32]{2,1,0:T(1,128)S(1)}, s32[1,1,32]{2,1,0:T(1,128)}, u32[]{:S(2)}) copy-start(s32[1,1,32]{2,1,0:T(1,128)} %param.12) | copy-start | bytes 388
  0.7 2.4 %copy-start.3 = (s32[1,1,32]{2,1,0:T(1,128)S(1)}, s32[1,1,32]{2,1,0:T(1,128)}, u32[]{:S(2)}) copy-start(s32[1,1,32]{2,1,0:T(1,128)} %param.11) | copy-start | bytes 388
  3.0 2.1 %copy-start = (f32[1,1,32,128,128]{4,3,2,1,0:T(8,128)S(1)}, f32[1,1,32,128,128]{4,3,2,1,0:T(8,128)}, u32[]{:S(2)}) copy-start(f32[1,1,32,128,128]{4,3,2,1,0:T(8,128)} %param.9) | copy-start | bytes 6291460
  3.0 2.1 %copy-start.2 = (f32[800,16,6]{0,1,2:T(8,128)S(1)}, f32[800,16,6]{0,1,2:T(8,128)}, u32[]{:S(2)}) copy-start(f32[800,16,6]{0,1,2:T(8,128)} %param.15) | copy-start | bytes 921604
  3.0 2.1 %copy-start.5 = (s32[1,1,32]{2,1,0:T(1,128)S(1)}, s32[1,1,32]{2,1,0:T(1,128)}, u32[]{:S(2)}) copy-start(s32[1,1,32]{2,1,0:T(1,128)} %param.13) | copy-start | bytes 388
  4.6 11.4 %collective-permute-start.2 = (f32[2,2,2,2,64,256]{5,4,3,2,1,0:T(8,128)S(1)}, f32[2,2,2,2,64,256]{5,4,3,2,1,0:T(8,128)S(1)}, u32[]{:S(2)}, u32[]{:S(2)}) collective-permute-start(f32[2,2,2,2,64,256]{5,4,3,2,1,0:T(8,128)S(1)} %get-tuple-element.44), channel_id=1, source_target_pairs={{0,1},{1,0},{2,3},{3,2},{4,5},{5,4},{6,7},{7,6},{8,9},{9,8},{10,11... | collective-permute-start | bytes 3145736 | tf_op jit(solution)/shard_map/ppermute | solution.py:309
  13.9 1.6 %collective-permute-start = (f32[4,64,256]{2,1,0:T(8,128)S(1)}, f32[4,64,256]{2,1,0:T(8,128)S(1)}, u32[]{:S(2)}, u32[]{:S(2)}) collective-permute-start(f32[4,64,256]{2,1,0:T(8,128)S(1)} %get-tuple-element.76), channel_id=1, source_target_pairs={{0,1},{1,0},{2,3},{3,2},{4,5},{5,4},{6,7},{7,6},{8,9},{9,8},{10,11... | collective-permute-start | bytes 786440 | tf_op jit(solution)/shard_map/ppermute | solution.py:309
  14.1 1.8 %collective-permute-start.1 = (f32[4,64,256]{2,1,0:T(8,128)S(1)}, f32[4,64,256]{2,1,0:T(8,128)S(1)}, u32[]{:S(2)}, u32[]{:S(2)}) collective-permute-start(f32[4,64,256]{2,1,0:T(8,128)S(1)} %get-tuple-element.77), channel_id=1, source_target_pairs={{0,1},{1,0},{2,3},{3,2},{4,5},{5,4},{6,7},{7,6},{8,9},{9,8},{10,11... | collective-permute-start | bytes 786440 | tf_op jit(solution)/shard_map/ppermute | solution.py:309
  16.0 17.3 %collective-permute-start.4 = (f32[2,4,64,256]{3,2,1,0:T(8,128)S(1)}, f32[2,4,64,256]{3,2,1,0:T(8,128)S(1)}, u32[]{:S(2)}, u32[]{:S(2)}) collective-permute-start(f32[2,4,64,256]{3,2,1,0:T(8,128)S(1)} %maximum_add_fusion), channel_id=1, source_target_pairs={{0,8},{8,0},{16,24},{24,16},{1,9},{9,1},{17,25},{25,17},{2,10},{10... | collective-permute-start | bytes 1572872 | tf_op jit(solution)/shard_map/ppermute | solution.py:312
  18.9 14.0 %collective-permute-start.3 = (f32[2,2,2,64,256]{4,3,2,1,0:T(8,128)S(1)}, f32[2,2,2,64,256]{4,3,2,1,0:T(8,128)S(1)}, u32[]{:S(2)}, u32[]{:S(2)}) collective-permute-start(f32[2,2,2,64,256]{4,3,2,1,0:T(8,128)S(1)} %get-tuple-element.49), channel_id=1, source_target_pairs={{0,2},{1,3},{2,0},{3,1},{4,6},{5,7},{6,4},{7,5},{8,10},{9,11},{10,... | collective-permute-start | bytes 1572872 | tf_op jit(solution)/shard_map/ppermute | solution.py:319
  29.4 4.1 %collective-permute-start.6 = (f32[4,64,256]{2,1,0:T(8,128)S(1)}, f32[4,64,256]{2,1,0:T(8,128)S(1)}, u32[]{:S(2)}, u32[]{:S(2)}) collective-permute-start(f32[4,64,256]{2,1,0:T(8,128)S(1)} %get-tuple-element.74), channel_id=1, source_target_pairs={{0,1},{1,0},{2,3},{3,2},{4,5},{5,4},{6,7},{7,6},{8,9},{9,8},{10,11... | collective-permute-start | bytes 786440 | tf_op jit(solution)/shard_map/ppermute | solution.py:309
  29.4 4.0 %collective-permute-start.5 = (f32[4,64,256]{2,1,0:T(8,128)S(1)}, f32[4,64,256]{2,1,0:T(8,128)S(1)}, u32[]{:S(2)}, u32[]{:S(2)}) collective-permute-start(f32[4,64,256]{2,1,0:T(8,128)S(1)} %get-tuple-element.75), channel_id=1, source_target_pairs={{0,1},{1,0},{2,3},{3,2},{4,5},{5,4},{6,7},{7,6},{8,9},{9,8},{10,11... | collective-permute-start | bytes 786440 | tf_op jit(solution)/shard_map/ppermute | solution.py:309
  32.9 7.5 %collective-permute-start.7 = (f32[2,2,64,256]{3,2,1,0:T(8,128)S(1)}, f32[2,2,64,256]{3,2,1,0:T(8,128)S(1)}, u32[]{:S(2)}, u32[]{:S(2)}) collective-permute-start(f32[2,2,64,256]{3,2,1,0:T(8,128)S(1)} %get-tuple-element.68), channel_id=1, source_target_pairs={{0,8},{8,0},{16,24},{24,16},{1,9},{9,1},{17,25},{25,17},{2,10},{10... | collective-permute-start | bytes 786440 | tf_op jit(solution)/shard_map/ppermute | solution.py:312
  33.5 8.6 %collective-permute-start.8 = (f32[4,64,256]{2,1,0:T(8,128)S(1)}, f32[4,64,256]{2,1,0:T(8,128)S(1)}, u32[]{:S(2)}, u32[]{:S(2)}) collective-permute-start(f32[4,64,256]{2,1,0:T(8,128)S(1)} %add.91), channel_id=1, source_target_pairs={{0,16},{8,24},{16,0},{24,8},{1,17},{9,25},{17,1},{25,9},{2,18},{10... | collective-permute-start | bytes 786440 | tf_op jit(solution)/shard_map/ppermute | solution.py:312
  40.5 6.1 %collective-permute-start.12 = (f32[2,64,256]{2,1,0:T(8,128)S(1)}, f32[2,64,256]{2,1,0:T(8,128)S(1)}, u32[]{:S(2)}, u32[]{:S(2)}) collective-permute-start(f32[2,64,256]{2,1,0:T(8,128)S(1)} %get-tuple-element.72), channel_id=1, source_target_pairs={{0,16},{8,24},{16,0},{24,8},{1,17},{9,25},{17,1},{25,9},{2,18},{10... | collective-permute-start | bytes 393224 | tf_op jit(solution)/shard_map/ppermute | solution.py:312
  42.1 6.7 %collective-permute-start.9 = (f32[64,256]{1,0:T(8,128)S(1)}, f32[64,256]{1,0:T(8,128)S(1)}, u32[]{:S(2)}, u32[]{:S(2)}) collective-permute-start(f32[64,256]{1,0:T(8,128)S(1)} %get-tuple-element.78), channel_id=1, source_target_pairs={{0,6},{1,7},{2,4},{3,5},{4,2},{5,3},{6,0},{7,1},{8,14},{9,15},{10,... | collective-permute-start | bytes 196616 | tf_op jit(solution)/shard_map/ppermute | solution.py:319
  45.8 5.9 %collective-permute-start.11 = (f32[64,256]{1,0:T(8,128)S(1)}, f32[64,256]{1,0:T(8,128)S(1)}, u32[]{:S(2)}, u32[]{:S(2)}) collective-permute-start(f32[64,256]{1,0:T(8,128)S(1)} %get-tuple-element.79), channel_id=1, source_target_pairs={{0,4},{1,5},{2,6},{3,7},{4,0},{5,1},{6,2},{7,3},{8,12},{9,13},{10,... | collective-permute-start | bytes 196616 | tf_op jit(solution)/shard_map/ppermute | solution.py:319
  45.8 5.9 %collective-permute-start.10 = (f32[64,256]{1,0:T(8,128)S(1)}, f32[64,256]{1,0:T(8,128)S(1)}, u32[]{:S(2)}, u32[]{:S(2)}) collective-permute-start(f32[64,256]{1,0:T(8,128)S(1)} %get-tuple-element.80), channel_id=1, source_target_pairs={{0,2},{1,3},{2,0},{3,1},{4,6},{5,7},{6,4},{7,5},{8,10},{9,11},{10,... | collective-permute-start | bytes 196616 | tf_op jit(solution)/shard_map/ppermute | solution.py:319
  46.6 5.8 %collective-permute-start.13 = (f32[64,256]{1,0:T(8,128)S(1)}, f32[64,256]{1,0:T(8,128)S(1)}, u32[]{:S(2)}, u32[]{:S(2)}) collective-permute-start(f32[64,256]{1,0:T(8,128)S(1)} %slice_bitcast_fusion.4), channel_id=1, source_target_pairs={{0,4},{1,5},{2,6},{3,7},{4,0},{5,1},{6,2},{7,3},{8,12},{9,13},{10,... | collective-permute-start | bytes 196616 | tf_op jit(solution)/shard_map/ppermute | solution.py:319
